TPU v7x, 32 devices: a whole 2x2x4 slice. The times are simulated.
32 devices in a mesh: section: 16 (over z, y, x), tp: 2 (over core).
Axes of the slice: x: 2, y: 2, z: 4, core: 2. Of those that a mesh axis runs over, the one named last changes fastest.
Arguments:
- preview: bfloat16 [256, 8192], P('section', 'tp'), may hold values from -6 to 6
- row_owner: int32 [256], P('section'), may hold values from 0 to 31, never falling along the last dimension, each value on 1 to 32 neighbouring positions
- norm_gain: float32 [8192], P('tp'), may hold values from 0.25 to 1.75
- w_gate: bfloat16 [28672, 8192], P('section', 'tp'), may hold values from -0.0625 to 0.0625
- w_up: bfloat16 [28672, 8192], P('section', 'tp'), may hold values from -0.0625 to 0.0625
- w_down: bfloat16 [28672, 8192], P('section', 'tp'), may hold values from -0.03125 to 0.03125
- score_vec: float32 [8192], P('tp'), may hold values from -0.75 to 0.75
Outputs:
- verified: bfloat16 [256, 8192], P('section', 'tp')
- scores: float32 [32], replicated
Inputs may be any that keep to these rules, and one draw needn't show every extreme that they name: row_owner never falls along the rows; every candidate owns 1 to 32 consecutive rows, some candidate exactly 32.
All inputs are finite; a program needn't handle non-finite values.
Results may differ from a plain program's by a relative error of at most 0.017.
Values may be sent and summed in bfloat16 or wider, within the bound.
No kernel may reach another device: no remote copies, remote signals or barrier semaphores. Data moves between devices by JAX's collectives and lax.ppermute only.
A program may use at most 128 MiB of HBM per device.

v0:
```python
import jax
import jax.numpy as jnp
from jax import lax
from jax.sharding import PartitionSpec as P

D = 8192
CAND = 32


def shards(preview, row_owner, norm_gain, w_gate, w_up, w_down, score_vec):
    resid = preview.astype(jnp.float32)
    sq_sum = lax.psum(jnp.sum(resid * resid, axis=1), "tp")
    normed = (resid * lax.rsqrt(sq_sum[:, None] / D + 1e-05) * norm_gain[None, :]).astype(
        jnp.bfloat16
    )
    dims = (((1,), (1,)), ((), ()))
    hidden_cols = w_gate.shape[0]
    piece = lax.all_gather(normed, "section", axis=0, tiled=True)
    gate_part = lax.dot_general(piece, w_gate, dims, preferred_element_type=jnp.float32)
    up_part = lax.dot_general(piece, w_up, dims, preferred_element_type=jnp.float32)
    partial_gu = jnp.concatenate([gate_part, up_part], axis=1)
    summed = lax.psum(partial_gu.astype(jnp.bfloat16), "tp").astype(jnp.float32)
    hidden = (jax.nn.silu(summed[:, :hidden_cols]) * summed[:, hidden_cols:]).astype(jnp.bfloat16)
    own_rows = resid.shape[0]
    full_down = jnp.dot(hidden, w_down, preferred_element_type=jnp.float32)
    total_down = lax.psum(full_down, "section")
    mine = lax.dynamic_slice_in_dim(total_down, lax.axis_index("section") * own_rows, own_rows, 0)
    verified = (resid + mine).astype(jnp.bfloat16)
    row_score = jnp.dot(verified.astype(jnp.float32), score_vec, precision=lax.Precision.HIGHEST)
    member = (row_owner[None, :] == jnp.arange(CAND, dtype=jnp.int32)[:, None]).astype(jnp.float32)
    totals = jnp.dot(member, row_score, precision=lax.Precision.HIGHEST)
    counts = jnp.sum(member, axis=1) / lax.axis_size("tp")
    totals, counts = lax.psum((totals, counts), ("section", "tp"))
    return (verified, totals / counts)


def solution(mesh):
    placed = (
        P("section", "tp"),
        P("section"),
        P("tp"),
        P("section", "tp"),
        P("section", "tp"),
        P("section", "tp"),
        P("tp"),
    )
    return jax.shard_map(
        shards, mesh=mesh, in_specs=placed, out_specs=(P("section", "tp"), P()), check_vma=False
    )
```

profile of v0, /device:TPU:0, one launch (start us, length us, event | category | flops | bytes accessed | tf_op | source)
XLA Modules:
  0.0 344.3 jit_solution(18096223151269934554)
XLA Ops:
  7.2 0.0 copy-start
  7.2 0.0 all-gather.2.cloned.1.call-start
  7.2 1.1 fusion.4
  8.3 2.6 psum.35
  10.9 1.7 fusion.6
  12.5 0.0 all-gather.2.cloned.1.call-update
  12.6 0.0 all-reduce.4.cloned.1.call-start
  12.6 63.4 %all-gather.2.cloned.1.call-done = bf16[256,4096]{1,0:T(8,128)(2,1)} async-done(((bf16[16,4096]{1,0:T(8,128)(2,1)}), bf16[256,4096]{1,0:T(8,128)(2,1)}) %all-gather.2.cloned.1.call-update) | async-done | bytes 2097168 | tf_op jit(solution)/shard_map/all_gather | solution.py:18
  76.0 0.0 copy-start.3
  76.0 9.9 %convolution_convert_fusion = bf16[256,1792]{1,0:T(8,128)(2,1)S(1)} fusion(bf16[256,4096]{1,0:T(8,128)(2,1)} %all-gather.2.cloned.1.call-done, bf16[1792,4096]{1,0:T(8,128)(2,1)} %param.11), kind=kOutput, calls=%fused_computation | convolution fusion | flops 3758555136 | bytes 17694720 | tf_op jit(solution)/shard_map/dot_general | solution.py:20
  85.9 0.0 copy-done.3
  85.9 7.4 %convolution_convert_fusion.1 = bf16[256,1792]{1,0:T(8,128)(2,1)S(1)} fusion(bf16[256,4096]{1,0:T(8,128)(2,1)S(1)} %copy-done.3, bf16[1792,4096]{1,0:T(8,128)(2,1)} %param.10), kind=kOutput, calls=%fused_computation.1 | convolution fusion | flops 3758555136 | bytes 17694720 | tf_op jit(solution)/shard_map/dot_general | solution.py:19
  93.4 1.4 pad_maximum_fusion
  94.7 0.0 all-reduce.4.cloned.1.call-update
  94.7 0.0 all-reduce.6.cloned.1.call-start
  94.8 19.6 %all-reduce.4.cloned.1.call-done = bf16[256,3584]{1,0:T(8,128)(2,1)} async-done(((bf16[256,3584]{1,0:T(8,128)(2,1)}), bf16[256,3584]{1,0:T(8,128)(2,1)}) %all-reduce.4.cloned.1.call-update) | async-done | bytes 1835024 | tf_op jit(solution)/shard_map/psum | solution.py:22
  114.4 1.9 convert_element_type.22
  116.3 10.9 %fusion.1 = f32[256,4096]{1,0:T(8,128)} fusion(bf16[1792,4096]{1,0:T(8,128)(2,1)} %param.12, f32[256,3584]{1,0:T(8,128)S(1)} %convert_element_type.22), kind=kOutput, calls=%fused_computation.7 | convolution fusion | flops 3760848896 | bytes 22544384 | tf_op jit(solution)/shard_map/dot_general | solution.py:25
  127.2 0.0 copy-start.4
  127.2 0.0 copy-start.1
  127.2 0.0 all-reduce.6.cloned.1.call-update
  127.3 0.6 copy-done.4
  127.9 0.1 convert_reduce_fusion
  128.0 168.8 %all-reduce.6.cloned.1.call-done = f32[256,4096]{1,0:T(8,128)} async-done(((f32[256,4096]{1,0:T(8,128)}), f32[256,4096]{1,0:T(8,128)}) %all-reduce.6.cloned.1.call-update) | async-done | bytes 4194320 | tf_op jit(solution)/shard_map/psum | solution.py:26
  296.8 0.0 copy-done.1
  296.8 1.0 fusion.7
  297.7 0.0 copy-done
  297.8 0.0 copy-start.2
  297.8 0.2 convolution_bitcast_fusion.1
  298.0 0.2 convolution_bitcast_fusion
  298.2 39.0 %all-reduce = (f32[32]{0:T(128)S(1)}, f32[32]{0:T(128)S(1)}) all-reduce(f32[32]{0:T(128)S(1)} %convolution_bitcast_fusion, f32[32]{0:T(128)S(1)} %broadcast_multiply_fusion), channel_id=1, replica_groups=mesh['section'=16,'tp'=2] {'section','tp'}, use_global_device_ids=true, to_apply=%region_4.5 | all-reduce | flops 64 | bytes 512 | tf_op jit(solution)/shard_map/psum | solution.py:33
  337.3 0.5 div.20
  337.8 0.0 copy-done.2
  (2 shorter events, 0.0 us)
Async XLA Ops:
  7.2 290.6 %copy-start = (f32[4096]{0:T(1024)S(1)}, f32[4096]{0:T(1024)}, u32[]{:S(2)}) copy-start(f32[4096]{0:T(1024)} %param.13) | copy-start | bytes 49156
  7.2 68.8 %all-gather.2.cloned.1.call-start = ((), (), s32[]{:S(2)}) async-start(), calls=%async_computation | async-start | bytes 2228224 | tf_op jit(solution)/shard_map/all_gather | solution.py:18
  12.6 101.8 %all-reduce.4.cloned.1.call-start = ((), (), s32[]{:S(2)}) async-start(), calls=%async_computation.1 | async-start | bytes 3670016 | tf_op jit(solution)/shard_map/psum | solution.py:22
  76.0 9.9 %copy-start.3 = (bf16[256,4096]{1,0:T(8,128)(2,1)S(1)}, bf16[256,4096]{1,0:T(8,128)(2,1)}, u32[]{:S(2)}) copy-start(bf16[256,4096]{1,0:T(8,128)(2,1)} %all-gather.2.cloned.1.call-done) | copy-start | bytes 6291460
  94.7 202.0 %all-reduce.6.cloned.1.call-start = ((), (), s32[]{:S(2)}) async-start(), calls=%async_computation.2 | async-start | bytes 8388608 | tf_op jit(solution)/shard_map/psum | solution.py:26
  127.2 0.7 copy-start.4
  127.2 169.5 %copy-start.1 = (bf16[16,4096]{1,0:T(8,128)(2,1)S(1)}, bf16[16,4096]{1,0:T(8,128)(2,1)}, u32[]{:S(2)}) copy-start(bf16[16,4096]{1,0:T(8,128)(2,1)} %param.7) | copy-start | bytes 393220
  297.8 40.0 %copy-start.2 = (bf16[16,4096]{1,0:T(8,128)(2,1)}, bf16[16,4096]{1,0:T(8,128)(2,1)S(1)}, u32[]{:S(2)}) copy-start(bf16[16,4096]{1,0:T(8,128)(2,1)S(1)} %fusion.7) | copy-start | bytes 393220
Sparse Core Ops, SparseCore 0:
  12.7 63.2 all-gather.1
  94.9 19.4 all-reduce.3
  127.4 169.3 all-reduce.5
where the time goes:
time: 345 us; the launch traced here: 344 us
  waiting for transfers between devices  252 us (73%)
  blocking collectives  41.6 us (12%)
  matrix products  28.7 us (8%)
  between operations  13.8 us (4%)
  other arithmetic  7.58 us (2%)
    psum x1, waiting for transfers between devices, shards(): total_down = lax.psum(full_down, 'section')  169 us
    all_gather x1, waiting for transfers between devices, shards(): piece = lax.all_gather(normed, 'section', axis=0, tiled=True)  63.4 us
    psum x1, blocking collectives, shards(): totals, counts = lax.psum((totals, counts), ('section', 'tp'))  39 us
    psum x1, waiting for transfers between devices, shards(): summed = lax.psum(partial_gu.astype(jnp.bfloat16), 'tp').astype(jnp.float32)  19.6 us
    dot_general x1, matrix products, shards(): full_down = jnp.dot(hidden, w_down, preferred_element_type=jnp.float32)  10.9 us
    dot_general x1, matrix products, shards(): lax.dot_general(piece, w_up, dims, preferred_element_type=jnp.float32)  9.93 us
    dot_general x1, matrix products, shards(): lax.dot_general(piece, w_gate, dims, preferred_element_type=jnp.float32)  7.4 us
  transfers between devices with their start and end apart: 3, of which 3 were waited for; matrix products, arithmetic and copies ran while one was open for 0% of the time, Pallas kernels for 0%

commit v1 on v0

v1 whole, which is shorter than its diff:
```python
import jax
import jax.numpy as jnp
from jax import lax
from jax.sharding import PartitionSpec as P

CAND = 32
LANES = 128
BOTH = ("section", "tp")
F32 = jnp.float32
BF16 = jnp.bfloat16


def cat(*parts):
    return jnp.concatenate(parts, axis=0)


def add(a, b):
    return (a.astype(F32) + b.astype(F32)).astype(BF16)


def build(n, tp):
    def swap(v, even, odd=None):
        odd = even if odd is None else odd
        pairs = [(s * tp + t, (s ^ (odd if t % 2 else even)) * tp + t) for s in range(n) for t in range(tp)]
        return lax.ppermute(v, BOTH, pairs)

    long_bits = [8 << i for i in range((n // 8).bit_length() - 1)]

    def gather_quad(g):
        a = swap(g, 1, 2)
        g = cat(g, a)
        return cat(g, swap(g, 2, 1))

    def gather(own):
        rows = own.shape[0]
        far = own
        for bit in long_bits:
            far = cat(far, swap(far, bit))
        far = far[rows:]
        near = cat(own, swap(own, 4))
        far = cat(far, swap(far, 4))
        return cat(gather_quad(near), gather_quad(far))

    def swap_middle(v):
        rows = v.shape[0] // n
        out, at = [], 0
        for length in (8 * rows, v.shape[0] - 8 * rows):
            q = length // 4
            out += [v[at + i * q : at + (i + 1) * q] for i in (0, 2, 1, 3)]
            at += length
        return cat(*out)

    def scatter_quad(v):
        h = v.shape[0] // 2
        v = add(v[:h], swap(v[h:], 2, 1))
        h //= 2
        return add(v[:h], swap(v[h:], 1, 2))

    def scatter(v):
        rows = v.shape[0] // n
        far = scatter_quad(v[8 * rows :])
        near = scatter_quad(v[: 8 * rows])
        h = far.shape[0] // 2
        far = add(far[:h], swap(far[h:], 4))
        near = add(near[:rows], swap(near[rows:], 4))
        v = cat(near, far)
        for bit in reversed(long_bits):
            h = v.shape[0] // 2
            got = swap(v[h:], bit)
            v = add(v[:h], got) if h > rows else v[:h].astype(F32) + got.astype(F32)
        return v

    def sum_sections(v):
        for bit in [1 << i for i in range(n.bit_length() - 1)]:
            v = v + swap(v, bit)
        return v

    def tp_swap(v):
        return lax.ppermute(v, "tp", [(t, t ^ 1) for t in range(tp)])

    def tp_sum(v):
        if tp == 2:
            return v.astype(F32) + swap_middle(tp_swap(v)).astype(F32)
        t = lax.axis_index("tp") % 2
        both = lax.psum(jnp.stack([jnp.where(t == 0, v, 0), jnp.where(t == 1, v, 0)]), "tp").astype(F32)
        mine = jnp.where(t == 0, both[0], both[1])
        return mine + swap_middle(jnp.where(t == 0, both[1], both[0]))

    def shards(preview, row_owner, norm_gain, w_gate, w_up, w_down, score_vec):
        width = preview.shape[1]
        dims = (((1,), (1,)), ((), ()))
        owner_lanes = jnp.broadcast_to(row_owner.astype(BF16)[:, None], (row_owner.shape[0], LANES))
        both = gather(jnp.concatenate([preview, owner_lanes], axis=1))
        rows_all = both[:, :width].astype(F32)
        owner = both[:, width].astype(jnp.int32)
        member = (owner[:, None] == jnp.arange(CAND, dtype=jnp.int32)[None, :]).astype(F32)
        x = (rows_all * norm_gain[None, :]).astype(BF16)
        sq = tp_sum(jnp.sum(rows_all * rows_all, axis=1)[:, None])
        scale = lax.rsqrt(sq / (width * tp) + 1e-05)
        units = w_gate.shape[0]
        gate = lax.dot_general(x, w_gate, dims, preferred_element_type=F32).astype(BF16)
        up = lax.dot_general(x, w_up, dims, preferred_element_type=F32).astype(BF16)
        gate_up = tp_sum(jnp.concatenate([gate, up], axis=1)) * scale
        hidden = (jax.nn.silu(gate_up[:, :units]) * gate_up[:, units:]).astype(BF16)
        unit_score = jnp.sum(w_down.astype(F32) * score_vec[None, :], axis=1)
        rows = preview.shape[0]
        row_part = jnp.sum(hidden.astype(F32) * unit_score[None, :], axis=1)
        own_part = jnp.sum(preview.astype(F32) * score_vec[None, :], axis=1)
        totals = jnp.sum(member * row_part[:, None], axis=0) + jnp.sum(member[:rows] * own_part[:, None], axis=0)
        totals = tp_swap(totals) + totals if tp == 2 else lax.psum(totals, "tp")
        totals = sum_sections(totals)
        scores = totals / jnp.sum(member, axis=0)
        down = jnp.dot(hidden, w_down, preferred_element_type=F32).astype(BF16)
        verified = (preview.astype(F32) + scatter(down)).astype(BF16)
        return verified, scores

    return shards


def solution(mesh):
    placed = (
        P("section", "tp"),
        P("section"),
        P("tp"),
        P("section", "tp"),
        P("section", "tp"),
        P("section", "tp"),
        P("tp"),
    )
    return jax.shard_map(
        build(mesh.shape["section"], mesh.shape["tp"]),
        mesh=mesh,
        in_specs=placed,
        out_specs=(P("section", "tp"), P()),
        check_vma=False,
    )
```

time: 345 us -> 139 us (0.40)
  waiting for transfers between devices: 252 us -> 60.7 us
  blocking collectives: 41.6 us -> 0 us
  starting transfers between devices: 0.12 us -> 22.3 us
  between operations: 13.8 us -> 0.89 us
  other arithmetic: 7.58 us -> 17.8 us
  local copies, waits for them, and re-layouts: 0.65 us -> 9.69 us
    psum x2 -> x0, waiting for transfers between devices: 188 us -> none  [the longest x1 169 us: shards(): total_down = lax.psum(full_down, 'section')]
    all_gather x1 -> x0, waiting for transfers between devices: 63.4 us -> none  [shards(): piece = lax.all_gather(normed, 'section', axis=0, tiled=True)]
    ppermute x0 -> x21, waiting for transfers between devices: none -> 60.7 us  [the longest x18 59.6 us: swap(): return lax.ppermute(v, BOTH, pairs)]
    psum x2 -> x0, blocking collectives: 41.6 us -> none  [the longest x1 39 us: shards(): totals, counts = lax.psum((totals, counts), ('section', 'tp'))]
    ppermute x0 -> x21, starting transfers between devices: none -> 22.3 us  [the longest x18 22.2 us: swap(): return lax.ppermute(v, BOTH, pairs)]
    reduce_sum x2 -> x6, other arithmetic: 1.14 us -> 10.3 us  [the longest x1 8.07 us: shards(): unit_score = jnp.sum(w_down.astype(F32) * score_vec[None, :], axis=1)]
    unnamed x10 -> x22, local copies, waits for them, and re-layouts: 0.65 us -> 8.25 us
    dot_general x5 -> x3, matrix products: 28.7 us -> 27.3 us  [the longest x1 10 us: shards(): down = jnp.dot(hidden, w_down, preferred_element_type=F32).astype(BF16)]
  transfers between devices with their start and end apart: 3 -> 21, of which waited for: 3 -> 18; matrix products, arithmetic and copies ran while one was open for 0% -> 9% of each run, Pallas kernels for 0% -> 0%
where the time goes in v1:
time: 139 us
  waiting for transfers between devices  60.7 us (44%)
  matrix products  27.3 us (20%)
  starting transfers between devices  22.3 us (16%)
  other arithmetic  17.8 us (13%)
  local copies, waits for them, and re-layouts  9.69 us (7%)
    ppermute x18, waiting for transfers between devices, swap(): return lax.ppermute(v, BOTH, pairs)  59.6 us
    ppermute x18, starting transfers between devices, swap(): return lax.ppermute(v, BOTH, pairs)  22.2 us
    dot_general x1, matrix products, shards(): down = jnp.dot(hidden, w_down, preferred_element_type=F32).astype(BF16)  10 us
    dot_general x1, matrix products, shards(): lax.dot_general(x, w_gate, dims, preferred_element_type=F32).astype(BF16)  9.8 us
    unnamed x22, local copies, waits for them, and re-layouts  8.25 us
    reduce_sum x1, other arithmetic, shards(): unit_score = jnp.sum(w_down.astype(F32) * score_vec[None, :], axis=1)  8.07 us
    dot_general x1, matrix products, shards(): up = lax.dot_general(x, w_up, dims, preferred_element_type=F32).astype(BF16)  7.44 us
  transfers between devices with their start and end apart: 21, of which 18 were waited for; matrix products, arithmetic and copies ran while one was open for 9% of the time, Pallas kernels for 0%

profile of v1, /device:TPU:0, one launch (start us, length us, event | category | flops | bytes accessed | tf_op | source)
XLA Modules:
  0.0 138.7 jit_solution(14400770992474434507)
XLA Ops:
  0.6 0.7 convert_element_type.106
  1.4 0.9 pad_maximum_fusion.5
  2.3 3.1 %collective-permute-start = (bf16[16,4224]{1,0:T(8,128)(2,1)S(1)}, bf16[16,4224]{1,0:T(8,128)(2,1)S(1)}, u32[]{:S(2)}, u32[]{:S(2)}) collective-permute-start(bf16[16,4224]{1,0:T(8,128)(2,1)S(1)} %get-tuple-element.10), channel_id=1, source_target_pairs={{0,8},{1,9},{2,10},{3,11},{4,12},{5,13},{6,14},{7,15},{8,0},{9,1},... | collective-permute-start | bytes 405512 | tf_op jit(solution)/shard_map/ppermute | solution.py:25
  5.4 2.6 %collective-permute-start.3 = (bf16[16,4224]{1,0:T(8,128)(2,1)S(1)}, bf16[16,4224]{1,0:T(8,128)(2,1)S(1)}, u32[]{:S(2)}, u32[]{:S(2)}) collective-permute-start(bf16[16,4224]{1,0:T(8,128)(2,1)S(1)} %get-tuple-element.10), channel_id=1, source_target_pairs={{0,16},{1,17},{2,18},{3,19},{4,20},{5,21},{6,22},{7,23},{8,24},{9,... | collective-permute-start | bytes 405512 | tf_op jit(solution)/shard_map/ppermute | solution.py:25
  8.0 3.0 %collective-permute-done = bf16[16,4224]{1,0:T(8,128)(2,1)S(1)} collective-permute-done((bf16[16,4224]{1,0:T(8,128)(2,1)S(1)}, bf16[16,4224]{1,0:T(8,128)(2,1)S(1)}, u32[]{:S(2)}, u32[]{:S(2)}) %collective-permute-start) | collective-permute-done | bytes 135200 | tf_op jit(solution)/shard_map/ppermute | solution.py:25
  11.0 0.9 pad_maximum_fusion.3
  11.9 1.9 %collective-permute-start.1 = (bf16[32,4224]{1,0:T(8,128)(2,1)S(1)}, bf16[32,4224]{1,0:T(8,128)(2,1)S(1)}, u32[]{:S(2)}, u32[]{:S(2)}) collective-permute-start(bf16[32,4224]{1,0:T(8,128)(2,1)S(1)} %pad_maximum_fusion.3), channel_id=1, source_target_pairs={{0,2},{1,5},{2,0},{3,7},{4,6},{5,1},{6,4},{7,3},{8,10},{9,13},{10,... | collective-permute-start | bytes 811016 | tf_op jit(solution)/shard_map/ppermute | solution.py:25
  13.8 0.5 collective-permute-done.3
  14.3 0.4 collective-permute-start.4
  14.7 4.5 %collective-permute-done.4 = bf16[16,4224]{1,0:T(8,128)(2,1)S(1)} collective-permute-done((bf16[16,4224]{1,0:T(8,128)(2,1)S(1)}, bf16[16,4224]{1,0:T(8,128)(2,1)S(1)}, u32[]{:S(2)}, u32[]{:S(2)}) %collective-permute-start.4) | collective-permute-done | bytes 135200 | tf_op jit(solution)/shard_map/ppermute | solution.py:25
  19.3 1.6 %collective-permute-start.5 = (bf16[32,4224]{1,0:T(8,128)(2,1)S(1)}, bf16[32,4224]{1,0:T(8,128)(2,1)S(1)}, u32[]{:S(2)}, u32[]{:S(2)}) collective-permute-start(bf16[32,4224]{1,0:T(8,128)(2,1)S(1)} %pad_maximum_fusion.4), channel_id=1, source_target_pairs={{0,2},{1,5},{2,0},{3,7},{4,6},{5,1},{6,4},{7,3},{8,10},{9,13},{10,... | collective-permute-start | bytes 811016 | tf_op jit(solution)/shard_map/ppermute | solution.py:25
  20.9 0.9 pad_maximum_fusion.1
  21.8 1.6 %collective-permute-start.2 = (bf16[64,4224]{1,0:T(8,128)(2,1)S(1)}, bf16[64,4224]{1,0:T(8,128)(2,1)S(1)}, u32[]{:S(2)}, u32[]{:S(2)}) collective-permute-start(bf16[64,4224]{1,0:T(8,128)(2,1)S(1)} %pad_maximum_fusion.1), channel_id=1, source_target_pairs={{0,4},{1,3},{2,6},{3,1},{4,0},{5,7},{6,2},{7,5},{8,12},{9,11},{10,... | collective-permute-start | bytes 1622024 | tf_op jit(solution)/shard_map/ppermute | solution.py:25
  23.4 5.4 %collective-permute-done.5 = bf16[32,4224]{1,0:T(8,128)(2,1)S(1)} collective-permute-done((bf16[32,4224]{1,0:T(8,128)(2,1)S(1)}, bf16[32,4224]{1,0:T(8,128)(2,1)S(1)}, u32[]{:S(2)}, u32[]{:S(2)}) %collective-permute-start.5) | collective-permute-done | bytes 270368 | tf_op jit(solution)/shard_map/ppermute | solution.py:25
  28.8 1.6 %collective-permute-start.6 = (bf16[64,4224]{1,0:T(8,128)(2,1)S(1)}, bf16[64,4224]{1,0:T(8,128)(2,1)S(1)}, u32[]{:S(2)}, u32[]{:S(2)}) collective-permute-start(bf16[64,4224]{1,0:T(8,128)(2,1)S(1)} %pad_maximum_fusion.2), channel_id=1, source_target_pairs={{0,4},{1,3},{2,6},{3,1},{4,0},{5,7},{6,2},{7,5},{8,12},{9,11},{10,... | collective-permute-start | bytes 1622024 | tf_op jit(solution)/shard_map/ppermute | solution.py:25
  30.4 0.8 collective-permute-done.2
  31.4 6.9 %collective-permute-done.6 = bf16[64,4224]{1,0:T(8,128)(2,1)S(1)} collective-permute-done((bf16[64,4224]{1,0:T(8,128)(2,1)S(1)}, bf16[64,4224]{1,0:T(8,128)(2,1)S(1)}, u32[]{:S(2)}, u32[]{:S(2)}) %collective-permute-start.6) | collective-permute-done | bytes 540704 | tf_op jit(solution)/shard_map/ppermute | solution.py:25
  38.3 1.3 copy-done
  39.7 7.4 %convolution_convert_fusion.1 = bf16[256,1792]{1,0:T(8,128)(2,1)S(1)} fusion(bf16[1792,4096]{1,0:T(8,128)(2,1)} %param.11, f32[4096]{0:T(1024)S(1)} %copy-done.4, bf16[256,4224]{1,0:T(8,128)(2,1)S(1)} %constant_dynamic-update-slice_fusion), kind=kOutput, calls=%fused_computation.7 | convolution fusion | flops 3761700864 | bytes 17711104 | tf_op jit(solution)/shard_map/dot_general | solution.py:102
  47.1 9.8 %convolution_convert_fusion.2 = bf16[256,1792]{1,0:T(8,128)(2,1)S(1)} fusion(bf16[1792,4096]{1,0:T(8,128)(2,1)} %param.10, f32[4096]{0:T(1024)S(1)} %copy-done.4, bf16[256,4224]{1,0:T(8,128)(2,1)} %copy-done), kind=kOutput, calls=%fused_computation.8 | convolution fusion | flops 3761700864 | bytes 17711104 | tf_op jit(solution)/shard_map/dot_general | solution.py:101
  56.9 1.3 pad_maximum_fusion
  58.3 0.9 copy-done.1
  59.2 0.5 fusion.1
  59.8 8.1 %multiply_reduce_fusion = f32[1792]{0:T(1024)S(1)} fusion(bf16[1792,4096]{1,0:T(8,128)(2,1)} %param.12, f32[4096]{0:T(1024)S(1)} %copy-done.3), kind=kLoop, calls=%fused_computation | loop fusion | flops 22018304 | bytes 14703616 | tf_op jit(solution)/shard_map/reduce_sum | solution.py:105
  68.0 0.1 concatenate.66
  68.1 1.0 slice_dynamic-update-slice_fusion.6
  69.1 1.0 slice_dynamic-update-slice_fusion.5
  70.0 1.0 slice_dynamic-update-slice_fusion.4
  71.0 1.1 slice_dynamic-update-slice_fusion
  72.0 1.0 slice_dynamic-update-slice_fusion.3
  73.0 1.0 slice_dynamic-update-slice_fusion.2
  73.9 1.0 slice_dynamic-update-slice_fusion.1
  74.9 0.6 add_multiply_fusion
  75.6 0.7 multiply_reduce_fusion.1
  76.2 10.0 %convolution_convert_fusion = bf16[256,4096]{1,0:T(8,128)(2,1)S(1)} fusion(bf16[256,1792]{1,0:T(8,128)(2,1)S(1)} %get-tuple-element.5, bf16[1792,4096]{1,0:T(8,128)(2,1)} %param.12), kind=kOutput, calls=%fused_computation.3 | convolution fusion | flops 3759144960 | bytes 17694720 | tf_op jit(solution)/shard_map/dot_general | solution.py:113
  86.3 1.5 %collective-permute-start.9 = (bf16[64,4096]{1,0:T(8,128)(2,1)S(1)}, bf16[64,4096]{1,0:T(8,128)(2,1)S(1)}, u32[]{:S(2)}, u32[]{:S(2)}) collective-permute-start(bf16[64,4096]{1,0:T(8,128)(2,1)S(1)} %get-tuple-element.8), channel_id=1, source_target_pairs={{0,4},{1,3},{2,6},{3,1},{4,0},{5,7},{6,2},{7,5},{8,12},{9,11},{10,... | collective-permute-start | bytes 1572872 | tf_op jit(solution)/shard_map/ppermute | solution.py:25
  87.9 0.5 collective-permute-start.12
  88.4 7.2 %collective-permute-done.9 = bf16[64,4096]{1,0:T(8,128)(2,1)S(1)} collective-permute-done((bf16[64,4096]{1,0:T(8,128)(2,1)S(1)}, bf16[64,4096]{1,0:T(8,128)(2,1)S(1)}, u32[]{:S(2)}, u32[]{:S(2)}) %collective-permute-start.9) | collective-permute-done | bytes 524320 | tf_op jit(solution)/shard_map/ppermute | solution.py:25
  95.6 5.6 %collective-permute-done.12 = bf16[64,4096]{1,0:T(8,128)(2,1)S(1)} collective-permute-done((bf16[64,4096]{1,0:T(8,128)(2,1)S(1)}, bf16[64,4096]{1,0:T(8,128)(2,1)S(1)}, u32[]{:S(2)}, u32[]{:S(2)}) %collective-permute-start.12) | collective-permute-done | bytes 524320 | tf_op jit(solution)/shard_map/ppermute | solution.py:25
  101.2 0.3 add_convert_fusion.1
  101.5 1.5 %collective-permute-start.13 = (bf16[32,4096]{1,0:T(8,128)(2,1)S(1)}, bf16[32,4096]{1,0:T(8,128)(2,1)S(1)}, u32[]{:S(2)}, u32[]{:S(2)}) collective-permute-start(bf16[32,4096]{1,0:T(8,128)(2,1)S(1)} %slice.160), channel_id=1, source_target_pairs={{0,2},{1,5},{2,0},{3,7},{4,6},{5,1},{6,4},{7,3},{8,10},{9,13},{10,... | collective-permute-start | bytes 786440 | tf_op jit(solution)/shard_map/ppermute | solution.py:25
  103.0 1.0 convert_reduce_fusion
  104.0 0.6 collective-permute-start.10
  104.6 3.3 %collective-permute-done.13 = bf16[32,4096]{1,0:T(8,128)(2,1)S(1)} collective-permute-done((bf16[32,4096]{1,0:T(8,128)(2,1)S(1)}, bf16[32,4096]{1,0:T(8,128)(2,1)S(1)}, u32[]{:S(2)}, u32[]{:S(2)}) %collective-permute-start.13) | collective-permute-done | bytes 262176 | tf_op jit(solution)/shard_map/ppermute | solution.py:25
  108.0 0.4 collective-permute-start.14
  108.4 2.4 %collective-permute-done.10 = bf16[32,4096]{1,0:T(8,128)(2,1)S(1)} collective-permute-done((bf16[32,4096]{1,0:T(8,128)(2,1)S(1)}, bf16[32,4096]{1,0:T(8,128)(2,1)S(1)}, u32[]{:S(2)}, u32[]{:S(2)}) %collective-permute-start.10) | collective-permute-done | bytes 262176 | tf_op jit(solution)/shard_map/ppermute | solution.py:25
  110.8 0.4 collective-permute-start.11
  111.2 2.7 %collective-permute-done.14 = bf16[16,4096]{1,0:T(8,128)(2,1)S(1)} collective-permute-done((bf16[16,4096]{1,0:T(8,128)(2,1)S(1)}, bf16[16,4096]{1,0:T(8,128)(2,1)S(1)}, u32[]{:S(2)}, u32[]{:S(2)}) %collective-permute-start.14) | collective-permute-done | bytes 131104 | tf_op jit(solution)/shard_map/ppermute | solution.py:25
  114.0 0.8 collective-permute-start.15
  114.7 0.1 fusion.7
  114.9 0.1 select_reduce_fusion
  115.0 2.3 %collective-permute-done.11 = bf16[16,4096]{1,0:T(8,128)(2,1)S(1)} collective-permute-done((bf16[16,4096]{1,0:T(8,128)(2,1)S(1)}, bf16[16,4096]{1,0:T(8,128)(2,1)S(1)}, u32[]{:S(2)}, u32[]{:S(2)}) %collective-permute-start.11) | collective-permute-done | bytes 131104 | tf_op jit(solution)/shard_map/ppermute | solution.py:25
  117.3 3.7 %collective-permute-done.15 = bf16[16,4096]{1,0:T(8,128)(2,1)S(1)} collective-permute-done((bf16[16,4096]{1,0:T(8,128)(2,1)S(1)}, bf16[16,4096]{1,0:T(8,128)(2,1)S(1)}, u32[]{:S(2)}, u32[]{:S(2)}) %collective-permute-start.15) | collective-permute-done | bytes 131104 | tf_op jit(solution)/shard_map/ppermute | solution.py:25
  121.0 0.9 fusion.6
  121.9 0.1 fusion.9
  122.0 1.1 collective-permute-done.16
  123.1 1.6 %collective-permute-start.17 = (f32[32]{0:T(128)S(1)}, f32[32]{0:T(128)S(1)}, u32[]{:S(2)}, u32[]{:S(2)}) collective-permute-start(f32[32]{0:T(128)S(1)} %add.82), channel_id=1, source_target_pairs={{0,2},{1,3},{2,0},{3,1},{4,6},{5,7},{6,4},{7,5},{8,10},{9,11},{10,... | collective-permute-start | bytes 392 | tf_op jit(solution)/shard_map/ppermute | solution.py:25
  124.7 2.0 %collective-permute-done.17 = f32[32]{0:T(128)S(1)} collective-permute-done((f32[32]{0:T(128)S(1)}, f32[32]{0:T(128)S(1)}, u32[]{:S(2)}, u32[]{:S(2)}) %collective-permute-start.17) | collective-permute-done | bytes 160 | tf_op jit(solution)/shard_map/ppermute | solution.py:25
  126.7 1.7 %collective-permute-start.18 = (f32[32]{0:T(128)S(1)}, f32[32]{0:T(128)S(1)}, u32[]{:S(2)}, u32[]{:S(2)}) collective-permute-start(f32[32]{0:T(128)S(1)} %add.83), channel_id=1, source_target_pairs={{0,4},{1,5},{2,6},{3,7},{4,0},{5,1},{6,2},{7,3},{8,12},{9,13},{10,... | collective-permute-start | bytes 392 | tf_op jit(solution)/shard_map/ppermute | solution.py:25
  128.3 1.9 %collective-permute-done.18 = f32[32]{0:T(128)S(1)} collective-permute-done((f32[32]{0:T(128)S(1)}, f32[32]{0:T(128)S(1)}, u32[]{:S(2)}, u32[]{:S(2)}) %collective-permute-start.18) | collective-permute-done | bytes 160 | tf_op jit(solution)/shard_map/ppermute | solution.py:25
  130.2 3.5 %collective-permute-done.19 = f32[32]{0:T(128)S(1)} collective-permute-done((f32[32]{0:T(128)S(1)}, f32[32]{0:T(128)S(1)}, u32[]{:S(2)}, u32[]{:S(2)}) %collective-permute-start.19) | collective-permute-done | bytes 160 | tf_op jit(solution)/shard_map/ppermute | solution.py:25
  133.8 0.5 collective-permute-start.20
  134.2 4.0 %collective-permute-done.20 = f32[32]{0:T(128)S(1)} collective-permute-done((f32[32]{0:T(128)S(1)}, f32[32]{0:T(128)S(1)}, u32[]{:S(2)}, u32[]{:S(2)}) %collective-permute-start.20) | collective-permute-done | bytes 160 | tf_op jit(solution)/shard_map/ppermute | solution.py:25
  138.2 0.5 add_divide_fusion
  (41 shorter events, 1.0 us)
Async XLA Ops:
  2.3 8.7 %collective-permute-start = (bf16[16,4224]{1,0:T(8,128)(2,1)S(1)}, bf16[16,4224]{1,0:T(8,128)(2,1)S(1)}, u32[]{:S(2)}, u32[]{:S(2)}) collective-permute-start(bf16[16,4224]{1,0:T(8,128)(2,1)S(1)} %get-tuple-element.10), channel_id=1, source_target_pairs={{0,8},{1,9},{2,10},{3,11},{4,12},{5,13},{6,14},{7,15},{8,0},{9,1},... | collective-permute-start | bytes 405512 | tf_op jit(solution)/shard_map/ppermute | solution.py:25
  5.4 8.9 %collective-permute-start.3 = (bf16[16,4224]{1,0:T(8,128)(2,1)S(1)}, bf16[16,4224]{1,0:T(8,128)(2,1)S(1)}, u32[]{:S(2)}, u32[]{:S(2)}) collective-permute-start(bf16[16,4224]{1,0:T(8,128)(2,1)S(1)} %get-tuple-element.10), channel_id=1, source_target_pairs={{0,16},{1,17},{2,18},{3,19},{4,20},{5,21},{6,22},{7,23},{8,24},{9,... | collective-permute-start | bytes 405512 | tf_op jit(solution)/shard_map/ppermute | solution.py:25
  11.9 9.0 %collective-permute-start.1 = (bf16[32,4224]{1,0:T(8,128)(2,1)S(1)}, bf16[32,4224]{1,0:T(8,128)(2,1)S(1)}, u32[]{:S(2)}, u32[]{:S(2)}) collective-permute-start(bf16[32,4224]{1,0:T(8,128)(2,1)S(1)} %pad_maximum_fusion.3), channel_id=1, source_target_pairs={{0,2},{1,5},{2,0},{3,7},{4,6},{5,1},{6,4},{7,3},{8,10},{9,13},{10,... | collective-permute-start | bytes 811016 | tf_op jit(solution)/shard_map/ppermute | solution.py:25
  14.3 5.0 %collective-permute-start.4 = (bf16[16,4224]{1,0:T(8,128)(2,1)S(1)}, bf16[16,4224]{1,0:T(8,128)(2,1)S(1)}, u32[]{:S(2)}, u32[]{:S(2)}) collective-permute-start(bf16[16,4224]{1,0:T(8,128)(2,1)S(1)} %collective-permute-done.3), channel_id=1, source_target_pairs={{0,8},{1,9},{2,10},{3,11},{4,12},{5,13},{6,14},{7,15},{8,0},{9,1},... | collective-permute-start | bytes 405512 | tf_op jit(solution)/shard_map/ppermute | solution.py:25
  19.3 9.5 %collective-permute-start.5 = (bf16[32,4224]{1,0:T(8,128)(2,1)S(1)}, bf16[32,4224]{1,0:T(8,128)(2,1)S(1)}, u32[]{:S(2)}, u32[]{:S(2)}) collective-permute-start(bf16[32,4224]{1,0:T(8,128)(2,1)S(1)} %pad_maximum_fusion.4), channel_id=1, source_target_pairs={{0,2},{1,5},{2,0},{3,7},{4,6},{5,1},{6,4},{7,3},{8,10},{9,13},{10,... | collective-permute-start | bytes 811016 | tf_op jit(solution)/shard_map/ppermute | solution.py:25
  21.8 9.4 %collective-permute-start.2 = (bf16[64,4224]{1,0:T(8,128)(2,1)S(1)}, bf16[64,4224]{1,0:T(8,128)(2,1)S(1)}, u32[]{:S(2)}, u32[]{:S(2)}) collective-permute-start(bf16[64,4224]{1,0:T(8,128)(2,1)S(1)} %pad_maximum_fusion.1), channel_id=1, source_target_pairs={{0,4},{1,3},{2,6},{3,1},{4,0},{5,7},{6,2},{7,5},{8,12},{9,11},{10,... | collective-permute-start | bytes 1622024 | tf_op jit(solution)/shard_map/ppermute | solution.py:25
  23.4 16.2 %copy-start.4 = (f32[4096]{0:T(1024)S(1)}, f32[4096]{0:T(1024)}, u32[]{:S(2)}) copy-start(f32[4096]{0:T(1024)} %param.9) | copy-start | bytes 49156
  28.8 9.4 %collective-permute-start.6 = (bf16[64,4224]{1,0:T(8,128)(2,1)S(1)}, bf16[64,4224]{1,0:T(8,128)(2,1)S(1)}, u32[]{:S(2)}, u32[]{:S(2)}) collective-permute-start(bf16[64,4224]{1,0:T(8,128)(2,1)S(1)} %pad_maximum_fusion.2), channel_id=1, source_target_pairs={{0,4},{1,3},{2,6},{3,1},{4,0},{5,7},{6,2},{7,5},{8,12},{9,11},{10,... | collective-permute-start | bytes 1622024 | tf_op jit(solution)/shard_map/ppermute | solution.py:25
  38.3 1.3 copy-start
  56.9 2.3 %copy-start.1 = (bf16[256,4224]{1,0:T(8,128)(2,1)S(1)}, bf16[256,4224]{1,0:T(8,128)(2,1)}, u32[]{:S(2)}) copy-start(bf16[256,4224]{1,0:T(8,128)(2,1)} %copy-done) | copy-start | bytes 6488068
  56.9 2.8 %copy-start.3 = (f32[4096]{0:T(1024)S(1)}, f32[4096]{0:T(1024)}, u32[]{:S(2)}) copy-start(f32[4096]{0:T(1024)} %param.13) | copy-start | bytes 49156
  58.3 9.8 %collective-permute-start.7 = (bf16[256,3584]{1,0:T(8,128)(2,1)}, bf16[256,3584]{1,0:T(8,128)(2,1)}, u32[]{:S(2)}, u32[]{:S(2)}) collective-permute-start(bf16[256,3584]{1,0:T(8,128)(2,1)} %pad_maximum_fusion), channel_id=1, source_target_pairs={{0,1},{1,0},{2,3},{3,2},{4,5},{5,4},{6,7},{7,6},{8,9},{9,8},{10,11... | collective-permute-start | bytes 5505032 | tf_op jit(solution)/shard_map/ppermute | solution.py:79
  59.7 8.2 %collective-permute-start.8 = (f32[256,1]{0,1:T(1,128)S(1)}, f32[256,1]{0,1:T(1,128)S(1)}, u32[]{:S(2)}, u32[]{:S(2)}) collective-permute-start(f32[256,1]{0,1:T(1,128)S(1)} %bitcast.19), channel_id=1, source_target_pairs={{0,1},{1,0},{2,3},{3,2},{4,5},{5,4},{6,7},{7,6},{8,9},{9,8},{10,11... | collective-permute-start | bytes 3080 | tf_op jit(solution)/shard_map/ppermute | solution.py:79
  86.3 9.2 %collective-permute-start.9 = (bf16[64,4096]{1,0:T(8,128)(2,1)S(1)}, bf16[64,4096]{1,0:T(8,128)(2,1)S(1)}, u32[]{:S(2)}, u32[]{:S(2)}) collective-permute-start(bf16[64,4096]{1,0:T(8,128)(2,1)S(1)} %get-tuple-element.8), channel_id=1, source_target_pairs={{0,4},{1,3},{2,6},{3,1},{4,0},{5,7},{6,2},{7,5},{8,12},{9,11},{10,... | collective-permute-start | bytes 1572872 | tf_op jit(solution)/shard_map/ppermute | solution.py:25
  87.9 13.3 %collective-permute-start.12 = (bf16[64,4096]{1,0:T(8,128)(2,1)S(1)}, bf16[64,4096]{1,0:T(8,128)(2,1)S(1)}, u32[]{:S(2)}, u32[]{:S(2)}) collective-permute-start(bf16[64,4096]{1,0:T(8,128)(2,1)S(1)} %get-tuple-element.9), channel_id=1, source_target_pairs={{0,4},{1,3},{2,6},{3,1},{4,0},{5,7},{6,2},{7,5},{8,12},{9,11},{10,... | collective-permute-start | bytes 1572872 | tf_op jit(solution)/shard_map/ppermute | solution.py:25
  101.5 19.5 %copy-start.2 = (bf16[16,4096]{1,0:T(8,128)(2,1)S(1)}, bf16[16,4096]{1,0:T(8,128)(2,1)}, u32[]{:S(2)}) copy-start(bf16[16,4096]{1,0:T(8,128)(2,1)} %param.7) | copy-start | bytes 393220
  101.5 6.4 %collective-permute-start.13 = (bf16[32,4096]{1,0:T(8,128)(2,1)S(1)}, bf16[32,4096]{1,0:T(8,128)(2,1)S(1)}, u32[]{:S(2)}, u32[]{:S(2)}) collective-permute-start(bf16[32,4096]{1,0:T(8,128)(2,1)S(1)} %slice.160), channel_id=1, source_target_pairs={{0,2},{1,5},{2,0},{3,7},{4,6},{5,1},{6,4},{7,3},{8,10},{9,13},{10,... | collective-permute-start | bytes 786440 | tf_op jit(solution)/shard_map/ppermute | solution.py:25
  104.0 6.7 %collective-permute-start.10 = (bf16[32,4096]{1,0:T(8,128)(2,1)S(1)}, bf16[32,4096]{1,0:T(8,128)(2,1)S(1)}, u32[]{:S(2)}, u32[]{:S(2)}) collective-permute-start(bf16[32,4096]{1,0:T(8,128)(2,1)S(1)} %slice.154), channel_id=1, source_target_pairs={{0,2},{1,5},{2,0},{3,7},{4,6},{5,1},{6,4},{7,3},{8,10},{9,13},{10,... | collective-permute-start | bytes 786440 | tf_op jit(solution)/shard_map/ppermute | solution.py:25
  108.0 5.9 %collective-permute-start.14 = (bf16[16,4096]{1,0:T(8,128)(2,1)S(1)}, bf16[16,4096]{1,0:T(8,128)(2,1)S(1)}, u32[]{:S(2)}, u32[]{:S(2)}) collective-permute-start(bf16[16,4096]{1,0:T(8,128)(2,1)S(1)} %slice.162), channel_id=1, source_target_pairs={{0,8},{1,9},{2,10},{3,11},{4,12},{5,13},{6,14},{7,15},{8,0},{9,1},... | collective-permute-start | bytes 393224 | tf_op jit(solution)/shard_map/ppermute | solution.py:25
  110.8 6.4 %collective-permute-start.11 = (bf16[16,4096]{1,0:T(8,128)(2,1)S(1)}, bf16[16,4096]{1,0:T(8,128)(2,1)S(1)}, u32[]{:S(2)}, u32[]{:S(2)}) collective-permute-start(bf16[16,4096]{1,0:T(8,128)(2,1)S(1)} %slice.156), channel_id=1, source_target_pairs={{0,8},{1,9},{2,10},{3,11},{4,12},{5,13},{6,14},{7,15},{8,0},{9,1},... | collective-permute-start | bytes 393224 | tf_op jit(solution)/shard_map/ppermute | solution.py:25
  114.0 7.0 %collective-permute-start.15 = (bf16[16,4096]{1,0:T(8,128)(2,1)S(1)}, bf16[16,4096]{1,0:T(8,128)(2,1)S(1)}, u32[]{:S(2)}, u32[]{:S(2)}) collective-permute-start(bf16[16,4096]{1,0:T(8,128)(2,1)S(1)} %add_convert_fusion.4), channel_id=1, source_target_pairs={{0,16},{1,17},{2,18},{3,19},{4,20},{5,21},{6,22},{7,23},{8,24},{9,... | collective-permute-start | bytes 393224 | tf_op jit(solution)/shard_map/ppermute | solution.py:25
  122.0 1.2 collective-permute-start.16
  123.1 3.5 %collective-permute-start.17 = (f32[32]{0:T(128)S(1)}, f32[32]{0:T(128)S(1)}, u32[]{:S(2)}, u32[]{:S(2)}) collective-permute-start(f32[32]{0:T(128)S(1)} %add.82), channel_id=1, source_target_pairs={{0,2},{1,3},{2,0},{3,1},{4,6},{5,7},{6,4},{7,5},{8,10},{9,11},{10,... | collective-permute-start | bytes 392 | tf_op jit(solution)/shard_map/ppermute | solution.py:25
  126.7 3.5 %collective-permute-start.18 = (f32[32]{0:T(128)S(1)}, f32[32]{0:T(128)S(1)}, u32[]{:S(2)}, u32[]{:S(2)}) collective-permute-start(f32[32]{0:T(128)S(1)} %add.83), channel_id=1, source_target_pairs={{0,4},{1,5},{2,6},{3,7},{4,0},{5,1},{6,2},{7,3},{8,12},{9,13},{10,... | collective-permute-start | bytes 392 | tf_op jit(solution)/shard_map/ppermute | solution.py:25
  130.2 3.5 %collective-permute-start.19 = (f32[32]{0:T(128)S(1)}, f32[32]{0:T(128)S(1)}, u32[]{:S(2)}, u32[]{:S(2)}) collective-permute-start(f32[32]{0:T(128)S(1)} %add.84), channel_id=1, source_target_pairs={{0,8},{1,9},{2,10},{3,11},{4,12},{5,13},{6,14},{7,15},{8,0},{9,1},... | collective-permute-start | bytes 392 | tf_op jit(solution)/shard_map/ppermute | solution.py:25
  133.8 4.4 %collective-permute-start.20 = (f32[32]{0:T(128)S(1)}, f32[32]{0:T(128)S(1)}, u32[]{:S(2)}, u32[]{:S(2)}) collective-permute-start(f32[32]{0:T(128)S(1)} %add.85), channel_id=1, source_target_pairs={{0,16},{1,17},{2,18},{3,19},{4,20},{5,21},{6,22},{7,23},{8,24},{9,... | collective-permute-start | bytes 392 | tf_op jit(solution)/shard_map/ppermute | solution.py:25

commit v2 on v1

--- a/solution.py
+++ b/solution.py
@@ -1,6 +1,8 @@
 import jax
 import jax.numpy as jnp
 from jax import lax
+from jax.experimental import pallas as pl
+from jax.experimental.pallas import tpu as pltpu
 from jax.sharding import PartitionSpec as P
 
 CAND = 32
@@ -18,7 +20,7 @@
     return (a.astype(F32) + b.astype(F32)).astype(BF16)
 
 
-def build(n, tp):
+def general(n, tp):
     def swap(v, even, odd=None):
         odd = even if odd is None else odd
         pairs = [(s * tp + t, (s ^ (odd if t % 2 else even)) * tp + t) for s in range(n) for t in range(tp)]
@@ -117,7 +119,190 @@
     return shards
 
 
+NT = (((1,), (1,)), ((), ()))
+VMEM = pl.BlockSpec(memory_space=pltpu.VMEM)
+TILE = 256
+
+
+def call(body, out_shape, args, scratch, megabytes, flops):
+    size = sum(a.size * a.dtype.itemsize for a in args)
+    return pl.pallas_call(
+        body,
+        out_shape=out_shape,
+        in_specs=[VMEM] * len(args),
+        out_specs=jax.tree.map(lambda _: VMEM, out_shape),
+        scratch_shapes=scratch,
+        compiler_params=pltpu.CompilerParams(vmem_limit_bytes=megabytes << 20),
+        cost_estimate=pl.CostEstimate(flops=flops, bytes_accessed=size, transcendentals=0),
+    )(*args)
+
+
+def payload(preview, row_owner, flops):
+    rows, width = preview.shape
+
+    def body(rows_ref, owner_ref, out):
+        out[:, :width] = rows_ref[...]
+        at = lax.broadcasted_iota(jnp.int32, (rows, LANES), 0)
+        owner = jnp.zeros((rows, LANES), F32)
+        for i in range(rows):
+            owner = jnp.where(at == i, owner_ref[i].astype(F32), owner)
+        out[:, width:] = owner.astype(BF16)
+
+    return pl.pallas_call(
+        body,
+        out_shape=jax.ShapeDtypeStruct((rows, width + LANES), BF16),
+        in_specs=[VMEM, pl.BlockSpec(memory_space=pltpu.SMEM)],
+        out_specs=VMEM,
+        cost_estimate=pl.CostEstimate(flops=flops, bytes_accessed=4 * rows * width, transcendentals=0),
+    )(preview, row_owner)
+
+
+def join(a, b, flops):
+    def body(a_ref, b_ref, out):
+        out[: a.shape[0], :] = a_ref[...]
+        out[a.shape[0] :, :] = b_ref[...]
+
+    return call(body, jax.ShapeDtypeStruct((a.shape[0] + b.shape[0], a.shape[1]), a.dtype), (a, b), [], 4, flops)
+
+
+def gate_up(pieces, places, gain, w_gate, w_up):
+    rows, width = sum(p.shape[0] for p in pieces), gain.shape[1]
+    units = w_gate.shape[0]
+    half = rows // 2
+
+    def body(*refs):
+        given = refs[: len(pieces)]
+        gain_ref, gate_ref, up_ref, near, far, squares, owner, x = refs[len(pieces) :]
+        for ref, blocks in zip(given, places):
+            size = ref.shape[0] // len(blocks)
+            for i, to in enumerate(blocks):
+                v = ref[i * size : (i + 1) * size, :width].astype(F32)
+                here = slice(to, to + size)
+                owner[here, :] = ref[i * size : (i + 1) * size, width:].astype(F32)
+                squares[here, :] = jnp.broadcast_to(jnp.sum(v * v, axis=1, keepdims=True), (size, LANES))
+                x[here, :] = (v * gain_ref[...]).astype(BF16)
+
+        @pl.loop(0, units // TILE)
+        def _(i):
+            tile = pl.ds(pl.multiple_of(i * TILE, TILE), TILE)
+            for k, w in enumerate((gate_ref, up_ref)):
+                product = lax.dot_general(x[...], w[tile, :], NT, preferred_element_type=F32).astype(BF16)
+                near[k, :, tile] = product[:half]
+                far[k, :, tile] = product[half:]
+
+    part = jax.ShapeDtypeStruct((2, half, units), BF16)
+    lanes = jax.ShapeDtypeStruct((rows, LANES), F32)
+    out_shape = (part, part, lanes, lanes)
+    scratch = [pltpu.VMEM((rows, width), BF16)]
+    return call(body, out_shape, (*pieces, gain, w_gate, w_up), scratch, 12, 4 * rows * width * units)
+
+
+def down_rows(first, mine, theirs, squares, other_squares, owner, w_down, score, own, devices, flops):
+    units, width = w_down.shape
+    rows = squares.shape[0] // 2
+    q = rows // 4
+    wide = 2048
+
+    def body(a, b, sq, other_sq, owner_ref, w, score_ref, own_ref, down, totals, hidden):
+        for block, other in enumerate((0, 2, 1, 3)):
+            here = slice(block * q, (block + 1) * q)
+            there = slice(other * q, (other + 1) * q)
+            both = sq[first + block * q : first + (block + 1) * q, :1]
+            both += other_sq[first + other * q : first + (other + 1) * q, :1]
+            scale = lax.rsqrt(both / (2 * width) + 1e-05)
+            for lo in range(0, units, TILE):
+                cols = slice(lo, lo + TILE)
+                g = (a[0, here, cols].astype(F32) + b[0, there, cols].astype(F32)) * scale
+                u = (a[1, here, cols].astype(F32) + b[1, there, cols].astype(F32)) * scale
+                hidden[here, cols] = (jax.nn.silu(g) * u).astype(BF16)
+        row_part = jnp.zeros((rows, 1), F32)
+        for lo in range(0, width, wide):
+            cols = slice(lo, lo + wide)
+            product = jnp.dot(hidden[...], w[:, cols], preferred_element_type=F32)
+            down[:, cols] = product.astype(BF16)
+            row_part += jnp.sum(product * score_ref[:, cols], axis=1, keepdims=True)
+        group = owner_ref[first : first + rows, :]
+        member = group == lax.broadcasted_iota(jnp.int32, group.shape, 1).astype(F32)
+        total = jnp.sum(jnp.where(member, row_part, 0.0), axis=0, keepdims=True)
+        if first == 0:
+            h = own_ref.shape[0]
+            own_part = jnp.sum(own_ref[:, :width].astype(F32) * score_ref[...], axis=1, keepdims=True)
+            total += jnp.sum(jnp.where(member[:h], own_part, 0.0), axis=0, keepdims=True)
+        totals[...] = jnp.zeros_like(totals)
+        totals[0:1, :] = total
+        totals[1:2, :] = jnp.sum(member.astype(F32), axis=0, keepdims=True) / devices
+
+    out_shape = (jax.ShapeDtypeStruct((rows, width), BF16), jax.ShapeDtypeStruct((8, LANES), F32))
+    args = (mine, theirs, squares, other_squares, owner, w_down, score, own)
+    return call(body, out_shape, args, [pltpu.VMEM((rows, units), BF16)], 12, flops)
+
+
+def paired(n, tp):
+    def swap(v, even, odd=None):
+        odd = even if odd is None else odd
+        pairs = [(s * tp + t, (s ^ (odd if t else even)) * tp + t) for s in range(n) for t in range(tp)]
+        return lax.ppermute(v, BOTH, pairs)
+
+    def tp_swap(v):
+        return lax.ppermute(v, "tp", [(0, 1), (1, 0)])
+
+    after = lax.optimization_barrier
+
+    def shards(preview, row_owner, norm_gain, w_gate, w_up, w_down, score_vec):
+        rows = preview.shape[0]
+        own = payload(preview, row_owner, 10**10)
+        z2, z1 = swap(own, 8), swap(own, 4)
+        z3 = swap(z2, 4)
+        near = join(own, z1, 10**10)
+        near_a, near_b = swap(near, 1, 2), swap(near, 2, 1)
+        far = join(z2, z3, 10**10)
+        far_a, far_b = swap(far, 1, 2), swap(far, 2, 1)
+        near_a, near_b = after((near_a, near_b))
+        near_c = swap(near_a, 2, 1)
+        far_a, far_b = after((far_a, far_b))
+        far_c = swap(far_a, 2, 1)
+        pieces = [near, near_a, near_b, near_c, far, far_a, far_b, far_c]
+        q = near.shape[0]
+        places = [(i * q,) for i in range(len(pieces))]
+        half = 4 * q
+        gain, score = norm_gain[None, :], score_vec[None, :]
+        part_near, part_far, squares, owner = gate_up(pieces, places, gain, w_gate, w_up)
+        other_squares, other_far, other_near = tp_swap(squares), tp_swap(part_far), tp_swap(part_near)
+
+        def down(first, mine, other, flops):
+            return down_rows(first, mine, other, squares, other_squares, owner, w_down, score, own, n * tp, flops)
+
+        f, totals_far = down(half, part_far, other_far, 10**9)
+        f, part_near = after((f, part_near))
+        g, totals_near = down(0, part_near, other_near, 10**10)
+        f3, f2 = swap(f[3 * q :], 2, 1), swap(f[2 * q : 3 * q], 2, 1)
+        totals = totals_far + totals_near
+        f3, g, t = after((f3, g, tp_swap(totals)))
+        totals = totals + t
+        f1 = swap(add(f[q : 2 * q], f3), 1, 2)
+        g3, g2 = swap(g[3 * q :], 2, 1), swap(g[2 * q : 3 * q], 2, 1)
+        f1, f2, t = after((f1, f2, swap(totals, 1)))
+        totals = totals + t
+        f = (f[:q].astype(F32) + f2.astype(F32) + f1.astype(F32)).astype(BF16)
+        z3 = swap(f[rows:], 4)
+        g3, t = after((g3, swap(totals, 2)))
+        totals = totals + t
+        g1 = swap(add(g[q : 2 * q], g3), 1, 2)
+        z3, totals = after((z3, totals))
+        z2 = swap(add(f[:rows], z3), 8)
+        g1, g2, t = after((g1, g2, swap(totals, 4)))
+        totals = totals + t
+        g = g[:q].astype(F32) + g2.astype(F32) + g1.astype(F32)
+        z1 = swap(g[rows:].astype(BF16), 4)
+        totals = totals + swap(totals, 8)
+        verified = (own[:, : preview.shape[1]].astype(F32) + g[:rows] + z1.astype(F32) + z2.astype(F32)).astype(BF16)
+        return verified, totals[0, :CAND] / totals[1, :CAND]
+
+    return shards
+
+
 def solution(mesh):
+    n, tp = mesh.shape["section"], mesh.shape["tp"]
     placed = (
         P("section", "tp"),
         P("section"),
@@ -128,7 +313,7 @@
         P("tp"),
     )
     return jax.shard_map(
-        build(mesh.shape["section"], mesh.shape["tp"]),
+        (paired if (n, tp) == (16, 2) else general)(n, tp),
         mesh=mesh,
         in_specs=placed,
         out_specs=(P("section", "tp"), P()),

time: 139 us -> 87.7 us (0.63)
  waiting for transfers between devices: 60.7 us -> 30.1 us
  matrix products: 27.3 us -> 0 us
  Pallas kernels: 0 us -> 16.4 us
  other arithmetic: 17.8 us -> 1.62 us
  starting transfers between devices: 22.3 us -> 37.4 us
  local copies, waits for them, and re-layouts: 9.69 us -> 1.08 us
    ppermute x18 -> x22, waiting for transfers between devices: 59.6 us -> 28 us  [swap(): return lax.ppermute(v, BOTH, pairs)]
    dot_general x3 -> x0, matrix products: 27.3 us -> none  [the longest x1 10 us: shards(): down = jnp.dot(hidden, w_down, preferred_element_type=F32).astype(BF16)]
    pallas_call x0 -> x6, Pallas kernels: none -> 16.4 us  [the longest x5 14.8 us: call(): pl.pallas_call(body, out_shape=out_shape, in_specs=[VMEM] * len(args), ou...]
    ppermute x18 -> x22, starting transfers between devices: 22.2 us -> 36.6 us  [swap(): return lax.ppermute(v, BOTH, pairs)]
    reduce_sum x6 -> x0, other arithmetic: 10.3 us -> none  [the longest x1 8.07 us: shards(): unit_score = jnp.sum(w_down.astype(F32) * score_vec[None, :], axis=1)]
    unnamed x22 -> x32, local copies, waits for them, and re-layouts: 8.25 us -> 0.98 us
    concatenate x6 -> x0, other arithmetic: 4.21 us -> none  [the longest x4 1.95 us: cat(): return jnp.concatenate(parts, axis=0)]
  transfers between devices with their start and end apart: 21 -> 26, of which waited for: 18 -> 15; matrix products, arithmetic and copies ran while one was open for 9% -> 1% of each run, Pallas kernels for 0% -> 6%
where the time goes in v2:
time: 87.7 us; the launch traced here: 87.6 us
  starting transfers between devices  37.4 us (43%)
  waiting for transfers between devices  30.1 us (34%)
  Pallas kernels  16.4 us (19%)
  other arithmetic  1.62 us (2%)
  local copies, waits for them, and re-layouts  1.08 us (1%)
  between operations  0.95 us (1%)
    ppermute x22, starting transfers between devices, swap(): return lax.ppermute(v, BOTH, pairs)  36.6 us
    ppermute x22, waiting for transfers between devices, swap(): return lax.ppermute(v, BOTH, pairs)  28 us
    pallas_call x5, Pallas kernels, call(): pl.pallas_call(body, out_shape=out_shape, in_specs=[VMEM] * len(args), ou...  14.8 us
    ppermute x4, waiting for transfers between devices, tp_swap(): return lax.ppermute(v, 'tp', [(0, 1), (1, 0)])  2.08 us
  transfers between devices with their start and end apart: 26, of which 15 were waited for; matrix products, arithmetic and copies ran while one was open for 1% of the time, Pallas kernels for 6%

profile of v2, /device:TPU:0, one launch (start us, length us, event | category | flops | bytes accessed | tf_op | source)
XLA Modules:
  0.0 87.6 jit_solution(11878282768464125129)
XLA Ops:
  0.6 1.6 %shard_map.86.a_ref.own_ref = bf16[16,4224]{1,0:T(8,128)(2,1)} custom-call(bf16[16,4096]{1,0:T(8,128)(2,1)} %rows_ref.1, s32[16]{0:T(128)} %owner_ref.1), custom_call_target="tpu_custom_call" | custom-call | flops 10000000000 | bytes 262144 | tf_op jit(solution)/shard_map/pallas_call | solution.py:151
  2.2 4.0 %collective-permute-start.4 = (bf16[16,4224]{1,0:T(8,128)(2,1)}, bf16[16,4224]{1,0:T(8,128)(2,1)S(1)}, u32[]{:S(2)}, u32[]{:S(2)}) collective-permute-start(bf16[16,4224]{1,0:T(8,128)(2,1)} %shard_map.86.a_ref.own_ref), channel_id=1, source_target_pairs={{0,16},{1,17},{2,18},{3,19},{4,20},{5,21},{6,22},{7,23},{8,24},{9,... | collective-permute-start | bytes 405512 | tf_op jit(solution)/shard_map/ppermute | solution.py:244
  6.3 1.6 %collective-permute-start = (bf16[16,4224]{1,0:T(8,128)(2,1)}, bf16[16,4224]{1,0:T(8,128)(2,1)S(1)}, u32[]{:S(2)}, u32[]{:S(2)}) collective-permute-start(bf16[16,4224]{1,0:T(8,128)(2,1)} %shard_map.86.a_ref.own_ref), channel_id=1, source_target_pairs={{0,8},{1,9},{2,10},{3,11},{4,12},{5,13},{6,14},{7,15},{8,0},{9,1},... | collective-permute-start | bytes 405512 | tf_op jit(solution)/shard_map/ppermute | solution.py:244
  7.8 5.2 %collective-permute-done.4.a_ref = bf16[16,4224]{1,0:T(8,128)(2,1)S(1)} collective-permute-done((bf16[16,4224]{1,0:T(8,128)(2,1)}, bf16[16,4224]{1,0:T(8,128)(2,1)S(1)}, u32[]{:S(2)}, u32[]{:S(2)}) %collective-permute-start.4) | collective-permute-done | bytes 135200 | tf_op jit(solution)/shard_map/ppermute | solution.py:244
  13.1 0.7 collective-permute-start.5
  13.8 0.0 collective-permute-done.b_ref
  13.8 0.9 %copy-done = bf16[16,4224]{1,0:T(8,128)(2,1)S(1)} copy-done((bf16[16,4224]{1,0:T(8,128)(2,1)S(1)}, bf16[16,4224]{1,0:T(8,128)(2,1)}, u32[]{:S(2)}) %copy-start) | copy-done | bytes 135192
  14.7 0.0 slice-start.2
  14.7 0.0 slice-start.3
  14.8 0.0 slice-start.6
  14.8 0.0 copy-start.2
  14.8 1.6 %collective-permute-start.1 = (bf16[32,4224]{1,0:T(8,128)(2,1)S(1)}, bf16[32,4224]{1,0:T(8,128)(2,1)S(1)}, u32[]{:S(2)}, u32[]{:S(2)}) collective-permute-start(bf16[32,4224]{1,0:T(8,128)(2,1)S(1)} %shard_map.87.refs_0_), channel_id=1, source_target_pairs={{0,2},{1,5},{2,0},{3,7},{4,6},{5,1},{6,4},{7,3},{8,10},{9,13},{10,... | collective-permute-start | bytes 811016 | tf_op jit(solution)/shard_map/ppermute | solution.py:244
  16.3 1.5 %collective-permute-start.2 = (bf16[32,4224]{1,0:T(8,128)(2,1)S(1)}, bf16[32,4224]{1,0:T(8,128)(2,1)S(1)}, u32[]{:S(2)}, u32[]{:S(2)}) collective-permute-start(bf16[32,4224]{1,0:T(8,128)(2,1)S(1)} %shard_map.87.refs_0_), channel_id=1, source_target_pairs={{0,4},{1,3},{2,6},{3,1},{4,0},{5,7},{6,2},{7,5},{8,12},{9,11},{10,... | collective-permute-start | bytes 811016 | tf_op jit(solution)/shard_map/ppermute | solution.py:244
  17.9 0.2 collective-permute-done.5.b_ref
  18.1 1.6 %collective-permute-start.6 = (bf16[32,4224]{1,0:T(8,128)(2,1)S(1)}, bf16[32,4224]{1,0:T(8,128)(2,1)S(1)}, u32[]{:S(2)}, u32[]{:S(2)}) collective-permute-start(bf16[32,4224]{1,0:T(8,128)(2,1)S(1)} %shard_map.88.refs_4_), channel_id=1, source_target_pairs={{0,2},{1,5},{2,0},{3,7},{4,6},{5,1},{6,4},{7,3},{8,10},{9,13},{10,... | collective-permute-start | bytes 811016 | tf_op jit(solution)/shard_map/ppermute | solution.py:244
  19.7 1.5 %collective-permute-start.7 = (bf16[32,4224]{1,0:T(8,128)(2,1)S(1)}, bf16[32,4224]{1,0:T(8,128)(2,1)S(1)}, u32[]{:S(2)}, u32[]{:S(2)}) collective-permute-start(bf16[32,4224]{1,0:T(8,128)(2,1)S(1)} %shard_map.88.refs_4_), channel_id=1, source_target_pairs={{0,4},{1,3},{2,6},{3,1},{4,0},{5,7},{6,2},{7,5},{8,12},{9,11},{10,... | collective-permute-start | bytes 811016 | tf_op jit(solution)/shard_map/ppermute | solution.py:244
  21.2 3.0 %collective-permute-done.1.refs_1_ = bf16[32,4224]{1,0:T(8,128)(2,1)S(1)} collective-permute-done((bf16[32,4224]{1,0:T(8,128)(2,1)S(1)}, bf16[32,4224]{1,0:T(8,128)(2,1)S(1)}, u32[]{:S(2)}, u32[]{:S(2)}) %collective-permute-start.1) | collective-permute-done | bytes 270368 | tf_op jit(solution)/shard_map/ppermute | solution.py:244
  24.2 1.6 %collective-permute-done.2.refs_2_ = bf16[32,4224]{1,0:T(8,128)(2,1)S(1)} collective-permute-done((bf16[32,4224]{1,0:T(8,128)(2,1)S(1)}, bf16[32,4224]{1,0:T(8,128)(2,1)S(1)}, u32[]{:S(2)}, u32[]{:S(2)}) %collective-permute-start.2) | collective-permute-done | bytes 270368 | tf_op jit(solution)/shard_map/ppermute | solution.py:244
  25.8 1.5 %collective-permute-start.3 = (bf16[32,4224]{1,0:T(8,128)(2,1)S(1)}, bf16[32,4224]{1,0:T(8,128)(2,1)S(1)}, u32[]{:S(2)}, u32[]{:S(2)}) collective-permute-start(bf16[32,4224]{1,0:T(8,128)(2,1)S(1)} %collective-permute-done.1.refs_1_), channel_id=1, source_target_pairs={{0,4},{1,3},{2,6},{3,1},{4,0},{5,7},{6,2},{7,5},{8,12},{9,11},{10,... | collective-permute-start | bytes 811016 | tf_op jit(solution)/shard_map/ppermute | solution.py:244
  27.3 2.7 %collective-permute-done.6.refs_5_ = bf16[32,4224]{1,0:T(8,128)(2,1)S(1)} collective-permute-done((bf16[32,4224]{1,0:T(8,128)(2,1)S(1)}, bf16[32,4224]{1,0:T(8,128)(2,1)S(1)}, u32[]{:S(2)}, u32[]{:S(2)}) %collective-permute-start.6) | collective-permute-done | bytes 270368 | tf_op jit(solution)/shard_map/ppermute | solution.py:244
  30.0 0.0 collective-permute-done.7.refs_6_
  30.0 1.5 %collective-permute-start.8 = (bf16[32,4224]{1,0:T(8,128)(2,1)S(1)}, bf16[32,4224]{1,0:T(8,128)(2,1)S(1)}, u32[]{:S(2)}, u32[]{:S(2)}) collective-permute-start(bf16[32,4224]{1,0:T(8,128)(2,1)S(1)} %collective-permute-done.6.refs_5_), channel_id=1, source_target_pairs={{0,4},{1,3},{2,6},{3,1},{4,0},{5,7},{6,2},{7,5},{8,12},{9,11},{10,... | collective-permute-start | bytes 811016 | tf_op jit(solution)/shard_map/ppermute | solution.py:244
  31.5 0.7 collective-permute-done.3.refs_3_
  32.2 4.2 %collective-permute-done.8.refs_7_ = bf16[32,4224]{1,0:T(8,128)(2,1)S(1)} collective-permute-done((bf16[32,4224]{1,0:T(8,128)(2,1)S(1)}, bf16[32,4224]{1,0:T(8,128)(2,1)S(1)}, u32[]{:S(2)}, u32[]{:S(2)}) %collective-permute-start.8) | collective-permute-done | bytes 270368 | tf_op jit(solution)/shard_map/ppermute | solution.py:244
  36.5 0.0 slice-start.11
  36.6 0.0 copy-start.3
  36.6 9.8 %shard_map.89 = (bf16[2,128,1792]{2,1,0:T(8,128)(2,1)S(1)}, bf16[2,128,1792]{2,1,0:T(8,128)(2,1)S(1)}, f32[256,128]{1,0:T(8,128)S(1)}, f32[256,128]{1,0:T(8,128)S(1)}) custom-call(bf16[32,4224]{1,0:T(8,128)(2,1)S(1)} %shard_map.87.refs_0_, bf16[32,4224]{1,0:T(8,128)(2,1)S(1)} %collective-permute-done.1.refs_1_, ...), custom_call_target="tpu_custom_call" | custom-call | flops 7516192768 | bytes 31539200 | tf_op jit(solution)/shard_map/pallas_call | solution.py:129
  46.4 0.1 collective-permute-start.9
  46.5 0.5 collective-permute-start.10
  47.0 0.1 collective-permute-start.12
  47.1 2.1 %collective-permute-done.10.other_sq = f32[256,128]{1,0:T(8,128)S(1)} collective-permute-done((f32[256,128]{1,0:T(8,128)S(1)}, f32[256,128]{1,0:T(8,128)S(1)}, u32[]{:S(2)}, u32[]{:S(2)}) %collective-permute-start.10) | collective-permute-done | bytes 131104 | tf_op jit(solution)/shard_map/ppermute | solution.py:247
  49.1 0.0 collective-permute-done.9.b
  49.2 2.5 %shard_map.90 = (bf16[128,4096]{1,0:T(8,128)(2,1)S(1)}, f32[8,128]{1,0:T(8,128)S(1)}) custom-call(bf16[2,128,1792]{2,1,0:T(8,128)(2,1)S(1)} %get-tuple-element.33.a, bf16[2,128,1792]{2,1,0:T(8,128)(2,1)S(1)} %collective-permute-done.9.b, f32[256,128]{1,0:T(8,128)S(1)} %get-tuple-element.34.sq, f32[256,128]{1,0:T(8,128)S(1)} %collective-permute-done.10.other_sq, ...), custom_call_target="tpu_custom_call" | custom-call | flops 1000000000 | bytes 17059840 | tf_op jit(solution)/shard_map/pallas_call | solution.py:129
  51.7 1.6 %collective-permute-start.11 = (bf16[32,4096]{1,0:T(8,128)(2,1)S(1)}, bf16[32,4096]{1,0:T(8,128)(2,1)S(1)}, u32[]{:S(2)}, u32[]{:S(2)}) collective-permute-start(bf16[32,4096]{1,0:T(8,128)(2,1)S(1)} %get-tuple-element.59), channel_id=1, source_target_pairs={{0,4},{1,3},{2,6},{3,1},{4,0},{5,7},{6,2},{7,5},{8,12},{9,11},{10,... | collective-permute-start | bytes 786440 | tf_op jit(solution)/shard_map/ppermute | solution.py:244
  53.3 2.5 %shard_map.91 = (bf16[128,4096]{1,0:T(8,128)(2,1)S(1)}, f32[8,128]{1,0:T(8,128)S(1)}) custom-call(bf16[2,128,1792]{2,1,0:T(8,128)(2,1)S(1)} %get-tuple-element.39.a, bf16[2,128,1792]{2,1,0:T(8,128)(2,1)S(1)} %collective-permute-done.12.b, f32[256,128]{1,0:T(8,128)S(1)} %get-tuple-element.34.sq, f32[256,128]{1,0:T(8,128)S(1)} %collective-permute-done.10.other_sq, ...), custom_call_target="tpu_custom_call" | custom-call | flops 10000000000 | bytes 17059840 | tf_op jit(solution)/shard_map/pallas_call | solution.py:129
  55.8 0.1 collective-permute-start.13
  55.9 1.3 %collective-permute-start.16 = (bf16[32,4096]{1,0:T(8,128)(2,1)S(1)}, bf16[32,4096]{1,0:T(8,128)(2,1)S(1)}, u32[]{:S(2)}, u32[]{:S(2)}) collective-permute-start(bf16[32,4096]{1,0:T(8,128)(2,1)S(1)} %get-tuple-element.58), channel_id=1, source_target_pairs={{0,4},{1,3},{2,6},{3,1},{4,0},{5,7},{6,2},{7,5},{8,12},{9,11},{10,... | collective-permute-start | bytes 786440 | tf_op jit(solution)/shard_map/ppermute | solution.py:244
  57.2 0.0 collective-permute-done.13
  57.3 0.9 %collective-permute-done.11 = bf16[32,4096]{1,0:T(8,128)(2,1)S(1)} collective-permute-done((bf16[32,4096]{1,0:T(8,128)(2,1)S(1)}, bf16[32,4096]{1,0:T(8,128)(2,1)S(1)}, u32[]{:S(2)}, u32[]{:S(2)}) %collective-permute-start.11) | collective-permute-done | bytes 262176 | tf_op jit(solution)/shard_map/ppermute | solution.py:244
  58.2 0.1 add_convert_fusion.2
  58.2 1.6 %collective-permute-start.15 = (bf16[32,4096]{1,0:T(8,128)(2,1)S(1)}, bf16[32,4096]{1,0:T(8,128)(2,1)S(1)}, u32[]{:S(2)}, u32[]{:S(2)}) collective-permute-start(bf16[32,4096]{1,0:T(8,128)(2,1)S(1)} %add_convert_fusion.2), channel_id=1, source_target_pairs={{0,2},{1,5},{2,0},{3,7},{4,6},{5,1},{6,4},{7,3},{8,10},{9,13},{10,... | collective-permute-start | bytes 786440 | tf_op jit(solution)/shard_map/ppermute | solution.py:244
  59.8 0.5 collective-permute-start.17
  60.4 1.6 %collective-permute-start.14 = (bf16[32,4096]{1,0:T(8,128)(2,1)S(1)}, bf16[32,4096]{1,0:T(8,128)(2,1)S(1)}, u32[]{:S(2)}, u32[]{:S(2)}) collective-permute-start(bf16[32,4096]{1,0:T(8,128)(2,1)S(1)} %get-tuple-element.57), channel_id=1, source_target_pairs={{0,4},{1,3},{2,6},{3,1},{4,0},{5,7},{6,2},{7,5},{8,12},{9,11},{10,... | collective-permute-start | bytes 786440 | tf_op jit(solution)/shard_map/ppermute | solution.py:244
  62.0 0.5 collective-permute-start.20
  62.5 1.9 %collective-permute-done.16 = bf16[32,4096]{1,0:T(8,128)(2,1)S(1)} collective-permute-done((bf16[32,4096]{1,0:T(8,128)(2,1)S(1)}, bf16[32,4096]{1,0:T(8,128)(2,1)S(1)}, u32[]{:S(2)}, u32[]{:S(2)}) %collective-permute-start.16) | collective-permute-done | bytes 262176 | tf_op jit(solution)/shard_map/ppermute | solution.py:244
  64.4 2.4 %collective-permute-done.17 = f32[8,128]{1,0:T(8,128)S(1)} collective-permute-done((f32[8,128]{1,0:T(8,128)S(1)}, f32[8,128]{1,0:T(8,128)S(1)}, u32[]{:S(2)}, u32[]{:S(2)}) %collective-permute-start.17) | collective-permute-done | bytes 4128 | tf_op jit(solution)/shard_map/ppermute | solution.py:244
  66.7 2.4 %collective-permute-start.18 = (f32[8,128]{1,0:T(8,128)S(1)}, f32[8,128]{1,0:T(8,128)S(1)}, u32[]{:S(2)}, u32[]{:S(2)}) collective-permute-start(f32[8,128]{1,0:T(8,128)S(1)} %add.51), channel_id=1, source_target_pairs={{0,4},{1,5},{2,6},{3,7},{4,0},{5,1},{6,2},{7,3},{8,12},{9,13},{10,... | collective-permute-start | bytes 12296 | tf_op jit(solution)/shard_map/ppermute | solution.py:244
  69.1 0.1 add_convert_fusion
  69.2 1.5 %collective-permute-start.21 = (bf16[16,4096]{1,0:T(8,128)(2,1)S(1)}, bf16[16,4096]{1,0:T(8,128)(2,1)S(1)}, u32[]{:S(2)}, u32[]{:S(2)}) collective-permute-start(bf16[16,4096]{1,0:T(8,128)(2,1)S(1)} %slice.62), channel_id=1, source_target_pairs={{0,8},{1,9},{2,10},{3,11},{4,12},{5,13},{6,14},{7,15},{8,0},{9,1},... | collective-permute-start | bytes 393224 | tf_op jit(solution)/shard_map/ppermute | solution.py:244
  70.7 0.1 collective-permute-done.18
  70.9 0.1 add_convert_fusion.1
  70.9 1.9 %collective-permute-start.19 = (bf16[32,4096]{1,0:T(8,128)(2,1)S(1)}, bf16[32,4096]{1,0:T(8,128)(2,1)S(1)}, u32[]{:S(2)}, u32[]{:S(2)}) collective-permute-start(bf16[32,4096]{1,0:T(8,128)(2,1)S(1)} %add_convert_fusion.1), channel_id=1, source_target_pairs={{0,2},{1,5},{2,0},{3,7},{4,6},{5,1},{6,4},{7,3},{8,10},{9,13},{10,... | collective-permute-start | bytes 786440 | tf_op jit(solution)/shard_map/ppermute | solution.py:244
  72.9 1.4 %collective-permute-done.21 = bf16[16,4096]{1,0:T(8,128)(2,1)S(1)} collective-permute-done((bf16[16,4096]{1,0:T(8,128)(2,1)S(1)}, bf16[16,4096]{1,0:T(8,128)(2,1)S(1)}, u32[]{:S(2)}, u32[]{:S(2)}) %collective-permute-start.21) | collective-permute-done | bytes 131104 | tf_op jit(solution)/shard_map/ppermute | solution.py:244
  74.3 1.4 %collective-permute-start.22 = (f32[8,128]{1,0:T(8,128)S(1)}, f32[8,128]{1,0:T(8,128)S(1)}, u32[]{:S(2)}, u32[]{:S(2)}) collective-permute-start(f32[8,128]{1,0:T(8,128)S(1)} %add.55), channel_id=1, source_target_pairs={{0,8},{1,9},{2,10},{3,11},{4,12},{5,13},{6,14},{7,15},{8,0},{9,1},... | collective-permute-start | bytes 12296 | tf_op jit(solution)/shard_map/ppermute | solution.py:244
  75.8 2.4 %collective-permute-start.24 = (bf16[16,4096]{1,0:T(8,128)(2,1)S(1)}, bf16[16,4096]{1,0:T(8,128)(2,1)S(1)}, u32[]{:S(2)}, u32[]{:S(2)}) collective-permute-start(bf16[16,4096]{1,0:T(8,128)(2,1)S(1)} %add_convert_fusion.3), channel_id=1, source_target_pairs={{0,16},{1,17},{2,18},{3,19},{4,20},{5,21},{6,22},{7,23},{8,24},{9,... | collective-permute-start | bytes 393224 | tf_op jit(solution)/shard_map/ppermute | solution.py:244
  78.2 0.0 collective-permute-done.20
  78.2 0.0 collective-permute-done.22
  78.2 3.5 %collective-permute-start.25 = (f32[8,128]{1,0:T(8,128)S(1)}, f32[8,128]{1,0:T(8,128)S(1)}, u32[]{:S(2)}, u32[]{:S(2)}) collective-permute-start(f32[8,128]{1,0:T(8,128)S(1)} %add.62), channel_id=1, source_target_pairs={{0,16},{1,17},{2,18},{3,19},{4,20},{5,21},{6,22},{7,23},{8,24},{9,... | collective-permute-start | bytes 12296 | tf_op jit(solution)/shard_map/ppermute | solution.py:244
  81.7 0.1 convert_add_fusion
  81.8 0.8 collective-permute-start.23
  82.6 0.7 collective-permute-done.25
  83.3 0.5 fusion.3
  83.8 3.0 %collective-permute-done.23 = bf16[16,4096]{1,0:T(8,128)(2,1)S(1)} collective-permute-done((bf16[16,4096]{1,0:T(8,128)(2,1)S(1)}, bf16[16,4096]{1,0:T(8,128)(2,1)S(1)}, u32[]{:S(2)}, u32[]{:S(2)}) %collective-permute-start.23) | collective-permute-done | bytes 131104 | tf_op jit(solution)/shard_map/ppermute | solution.py:244
  86.9 0.7 fusion.2
  (46 shorter events, 0.3 us)
Async XLA Ops:
  2.2 10.8 %collective-permute-start.4 = (bf16[16,4224]{1,0:T(8,128)(2,1)}, bf16[16,4224]{1,0:T(8,128)(2,1)S(1)}, u32[]{:S(2)}, u32[]{:S(2)}) collective-permute-start(bf16[16,4224]{1,0:T(8,128)(2,1)} %shard_map.86.a_ref.own_ref), channel_id=1, source_target_pairs={{0,16},{1,17},{2,18},{3,19},{4,20},{5,21},{6,22},{7,23},{8,24},{9,... | collective-permute-start | bytes 405512 | tf_op jit(solution)/shard_map/ppermute | solution.py:244
  6.3 7.5 %collective-permute-start = (bf16[16,4224]{1,0:T(8,128)(2,1)}, bf16[16,4224]{1,0:T(8,128)(2,1)S(1)}, u32[]{:S(2)}, u32[]{:S(2)}) collective-permute-start(bf16[16,4224]{1,0:T(8,128)(2,1)} %shard_map.86.a_ref.own_ref), channel_id=1, source_target_pairs={{0,8},{1,9},{2,10},{3,11},{4,12},{5,13},{6,14},{7,15},{8,0},{9,1},... | collective-permute-start | bytes 405512 | tf_op jit(solution)/shard_map/ppermute | solution.py:244
  13.1 5.0 %collective-permute-start.5 = (bf16[16,4224]{1,0:T(8,128)(2,1)S(1)}, bf16[16,4224]{1,0:T(8,128)(2,1)S(1)}, u32[]{:S(2)}, u32[]{:S(2)}) collective-permute-start(bf16[16,4224]{1,0:T(8,128)(2,1)S(1)} %collective-permute-done.4.a_ref), channel_id=1, source_target_pairs={{0,8},{1,9},{2,10},{3,11},{4,12},{5,13},{6,14},{7,15},{8,0},{9,1},... | collective-permute-start | bytes 405512 | tf_op jit(solution)/shard_map/ppermute | solution.py:244
  13.8 0.9 %copy-start = (bf16[16,4224]{1,0:T(8,128)(2,1)S(1)}, bf16[16,4224]{1,0:T(8,128)(2,1)}, u32[]{:S(2)}) copy-start(bf16[16,4224]{1,0:T(8,128)(2,1)} %shard_map.86.a_ref.own_ref) | copy-start | bytes 405508
  14.7 21.8 %slice-start = ((s8[14680064]{0:T(1024)(128)(4,1)}), s8[4194304]{0:T(1024)(128)(4,1)S(1)}, s32[]{:S(2)}) async-start(s8[14680064]{0:T(1024)(128)(4,1)} %bitcast.4), calls=%async_computation | async-start | bytes 8388608
  14.7 21.8 %slice-start.1 = ((s8[14680064]{0:T(1024)(128)(4,1)}), s8[4194304]{0:T(1024)(128)(4,1)S(1)}, s32[]{:S(2)}) async-start(s8[14680064]{0:T(1024)(128)(4,1)} %bitcast.4), calls=%async_computation.1 | async-start | bytes 8388608
  14.7 21.8 %slice-start.4 = ((s8[14680064]{0:T(1024)(128)(4,1)}), s8[4194304]{0:T(1024)(128)(4,1)S(1)}, s32[]{:S(2)}) async-start(s8[14680064]{0:T(1024)(128)(4,1)} %bitcast.6), calls=%async_computation.4 | async-start | bytes 8388608
  14.7 21.8 %slice-start.5 = ((s8[14680064]{0:T(1024)(128)(4,1)}), s8[4194304]{0:T(1024)(128)(4,1)S(1)}, s32[]{:S(2)}) async-start(s8[14680064]{0:T(1024)(128)(4,1)} %bitcast.6), calls=%async_computation.5 | async-start | bytes 8388608
  14.7 21.8 %slice-start.2 = ((s8[14680064]{0:T(1024)(128)(4,1)}), s8[4194304]{0:T(1024)(128)(4,1)S(1)}, s32[]{:S(2)}) async-start(s8[14680064]{0:T(1024)(128)(4,1)} %bitcast.4), calls=%async_computation.2 | async-start | bytes 8388608
  14.7 21.7 %slice-start.3 = ((s8[14680064]{0:T(1024)(128)(4,1)}), s8[2097152]{0:T(1024)(128)(4,1)S(1)}, s32[]{:S(2)}) async-start(s8[14680064]{0:T(1024)(128)(4,1)} %bitcast.4), calls=%async_computation.3 | async-start | bytes 4194304
  14.8 21.7 %slice-start.6 = ((s8[14680064]{0:T(1024)(128)(4,1)}), s8[4194304]{0:T(1024)(128)(4,1)S(1)}, s32[]{:S(2)}) async-start(s8[14680064]{0:T(1024)(128)(4,1)} %bitcast.6), calls=%async_computation.6 | async-start | bytes 8388608
  14.8 21.7 %slice-start.7 = ((s8[14680064]{0:T(1024)(128)(4,1)}), s8[2097152]{0:T(1024)(128)(4,1)S(1)}, s32[]{:S(2)}) async-start(s8[14680064]{0:T(1024)(128)(4,1)} %bitcast.6), calls=%async_computation.7 | async-start | bytes 4194304
  14.8 21.7 %copy-start.2 = (f32[4096]{0:T(1024)S(1)}, f32[4096]{0:T(1024)}, u32[]{:S(2)}) copy-start(f32[4096]{0:T(1024)} %param.9) | copy-start | bytes 49156
  14.8 9.4 %collective-permute-start.1 = (bf16[32,4224]{1,0:T(8,128)(2,1)S(1)}, bf16[32,4224]{1,0:T(8,128)(2,1)S(1)}, u32[]{:S(2)}, u32[]{:S(2)}) collective-permute-start(bf16[32,4224]{1,0:T(8,128)(2,1)S(1)} %shard_map.87.refs_0_), channel_id=1, source_target_pairs={{0,2},{1,5},{2,0},{3,7},{4,6},{5,1},{6,4},{7,3},{8,10},{9,13},{10,... | collective-permute-start | bytes 811016 | tf_op jit(solution)/shard_map/ppermute | solution.py:244
  16.3 9.4 %collective-permute-start.2 = (bf16[32,4224]{1,0:T(8,128)(2,1)S(1)}, bf16[32,4224]{1,0:T(8,128)(2,1)S(1)}, u32[]{:S(2)}, u32[]{:S(2)}) collective-permute-start(bf16[32,4224]{1,0:T(8,128)(2,1)S(1)} %shard_map.87.refs_0_), channel_id=1, source_target_pairs={{0,4},{1,3},{2,6},{3,1},{4,0},{5,7},{6,2},{7,5},{8,12},{9,11},{10,... | collective-permute-start | bytes 811016 | tf_op jit(solution)/shard_map/ppermute | solution.py:244
  18.1 31.1 %slice-start.8 = ((s8[14680064]{0:T(1024)(128)(4,1)}), s8[4194304]{0:T(1024)(128)(4,1)S(1)}, s32[]{:S(2)}) async-start(s8[14680064]{0:T(1024)(128)(4,1)} %bitcast.8), calls=%async_computation.8 | async-start | bytes 8388608
  18.1 31.1 %slice-start.9 = ((s8[14680064]{0:T(1024)(128)(4,1)}), s8[4194304]{0:T(1024)(128)(4,1)S(1)}, s32[]{:S(2)}) async-start(s8[14680064]{0:T(1024)(128)(4,1)} %bitcast.8), calls=%async_computation.9 | async-start | bytes 8388608
  18.1 31.1 %slice-start.10 = ((s8[14680064]{0:T(1024)(128)(4,1)}), s8[4194304]{0:T(1024)(128)(4,1)S(1)}, s32[]{:S(2)}) async-start(s8[14680064]{0:T(1024)(128)(4,1)} %bitcast.8), calls=%async_computation.10 | async-start | bytes 8388608
  18.1 11.9 %collective-permute-start.6 = (bf16[32,4224]{1,0:T(8,128)(2,1)S(1)}, bf16[32,4224]{1,0:T(8,128)(2,1)S(1)}, u32[]{:S(2)}, u32[]{:S(2)}) collective-permute-start(bf16[32,4224]{1,0:T(8,128)(2,1)S(1)} %shard_map.88.refs_4_), channel_id=1, source_target_pairs={{0,2},{1,5},{2,0},{3,7},{4,6},{5,1},{6,4},{7,3},{8,10},{9,13},{10,... | collective-permute-start | bytes 811016 | tf_op jit(solution)/shard_map/ppermute | solution.py:244
  19.7 10.3 %collective-permute-start.7 = (bf16[32,4224]{1,0:T(8,128)(2,1)S(1)}, bf16[32,4224]{1,0:T(8,128)(2,1)S(1)}, u32[]{:S(2)}, u32[]{:S(2)}) collective-permute-start(bf16[32,4224]{1,0:T(8,128)(2,1)S(1)} %shard_map.88.refs_4_), channel_id=1, source_target_pairs={{0,4},{1,3},{2,6},{3,1},{4,0},{5,7},{6,2},{7,5},{8,12},{9,11},{10,... | collective-permute-start | bytes 811016 | tf_op jit(solution)/shard_map/ppermute | solution.py:244
  25.8 6.5 %collective-permute-start.3 = (bf16[32,4224]{1,0:T(8,128)(2,1)S(1)}, bf16[32,4224]{1,0:T(8,128)(2,1)S(1)}, u32[]{:S(2)}, u32[]{:S(2)}) collective-permute-start(bf16[32,4224]{1,0:T(8,128)(2,1)S(1)} %collective-permute-done.1.refs_1_), channel_id=1, source_target_pairs={{0,4},{1,3},{2,6},{3,1},{4,0},{5,7},{6,2},{7,5},{8,12},{9,11},{10,... | collective-permute-start | bytes 811016 | tf_op jit(solution)/shard_map/ppermute | solution.py:244
  30.0 6.5 %collective-permute-start.8 = (bf16[32,4224]{1,0:T(8,128)(2,1)S(1)}, bf16[32,4224]{1,0:T(8,128)(2,1)S(1)}, u32[]{:S(2)}, u32[]{:S(2)}) collective-permute-start(bf16[32,4224]{1,0:T(8,128)(2,1)S(1)} %collective-permute-done.6.refs_5_), channel_id=1, source_target_pairs={{0,4},{1,3},{2,6},{3,1},{4,0},{5,7},{6,2},{7,5},{8,12},{9,11},{10,... | collective-permute-start | bytes 811016 | tf_op jit(solution)/shard_map/ppermute | solution.py:244
  36.5 12.6 %slice-start.11 = ((s8[14680064]{0:T(1024)(128)(4,1)}), s8[2097152]{0:T(1024)(128)(4,1)S(1)}, s32[]{:S(2)}) async-start(s8[14680064]{0:T(1024)(128)(4,1)} %bitcast.8), calls=%async_computation.11 | async-start | bytes 4194304
  36.6 12.6 %copy-start.1 = (bf16[16,4224]{1,0:T(8,128)(2,1)S(1)}, bf16[16,4224]{1,0:T(8,128)(2,1)}, u32[]{:S(2)}) copy-start(bf16[16,4224]{1,0:T(8,128)(2,1)} %shard_map.86.a_ref.own_ref) | copy-start | bytes 405508
  36.6 12.6 %copy-start.3 = (f32[4096]{0:T(1024)S(1)}, f32[4096]{0:T(1024)}, u32[]{:S(2)}) copy-start(f32[4096]{0:T(1024)} %param.13) | copy-start | bytes 49156
  46.4 2.7 %collective-permute-start.9 = (bf16[2,128,1792]{2,1,0:T(8,128)(2,1)S(1)}, bf16[2,128,1792]{2,1,0:T(8,128)(2,1)S(1)}, u32[]{:S(2)}, u32[]{:S(2)}) collective-permute-start(bf16[2,128,1792]{2,1,0:T(8,128)(2,1)S(1)} %get-tuple-element.33.a), channel_id=1, source_target_pairs={{0,1},{1,0},{2,3},{3,2},{4,5},{5,4},{6,7},{7,6},{8,9},{9,8},{10,11... | collective-permute-start | bytes 2752520 | tf_op jit(solution)/shard_map/ppermute | solution.py:247
  46.5 2.6 %collective-permute-start.10 = (f32[256,128]{1,0:T(8,128)S(1)}, f32[256,128]{1,0:T(8,128)S(1)}, u32[]{:S(2)}, u32[]{:S(2)}) collective-permute-start(f32[256,128]{1,0:T(8,128)S(1)} %get-tuple-element.34.sq), channel_id=1, source_target_pairs={{0,1},{1,0},{2,3},{3,2},{4,5},{5,4},{6,7},{7,6},{8,9},{9,8},{10,11... | collective-permute-start | bytes 393224 | tf_op jit(solution)/shard_map/ppermute | solution.py:247
  47.0 6.3 %collective-permute-start.12 = (bf16[2,128,1792]{2,1,0:T(8,128)(2,1)S(1)}, bf16[2,128,1792]{2,1,0:T(8,128)(2,1)S(1)}, u32[]{:S(2)}, u32[]{:S(2)}) collective-permute-start(bf16[2,128,1792]{2,1,0:T(8,128)(2,1)S(1)} %get-tuple-element.39.a), channel_id=1, source_target_pairs={{0,1},{1,0},{2,3},{3,2},{4,5},{5,4},{6,7},{7,6},{8,9},{9,8},{10,11... | collective-permute-start | bytes 2752520 | tf_op jit(solution)/shard_map/ppermute | solution.py:247
  51.7 6.4 %collective-permute-start.11 = (bf16[32,4096]{1,0:T(8,128)(2,1)S(1)}, bf16[32,4096]{1,0:T(8,128)(2,1)S(1)}, u32[]{:S(2)}, u32[]{:S(2)}) collective-permute-start(bf16[32,4096]{1,0:T(8,128)(2,1)S(1)} %get-tuple-element.59), channel_id=1, source_target_pairs={{0,4},{1,3},{2,6},{3,1},{4,0},{5,7},{6,2},{7,5},{8,12},{9,11},{10,... | collective-permute-start | bytes 786440 | tf_op jit(solution)/shard_map/ppermute | solution.py:244
  55.8 1.4 %collective-permute-start.13 = (f32[8,128]{1,0:T(8,128)S(1)}, f32[8,128]{1,0:T(8,128)S(1)}, u32[]{:S(2)}, u32[]{:S(2)}) collective-permute-start(f32[8,128]{1,0:T(8,128)S(1)} %add.48), channel_id=1, source_target_pairs={{0,1},{1,0},{2,3},{3,2},{4,5},{5,4},{6,7},{7,6},{8,9},{9,8},{10,11... | collective-permute-start | bytes 12296 | tf_op jit(solution)/shard_map/ppermute | solution.py:247
  55.9 8.4 %collective-permute-start.16 = (bf16[32,4096]{1,0:T(8,128)(2,1)S(1)}, bf16[32,4096]{1,0:T(8,128)(2,1)S(1)}, u32[]{:S(2)}, u32[]{:S(2)}) collective-permute-start(bf16[32,4096]{1,0:T(8,128)(2,1)S(1)} %get-tuple-element.58), channel_id=1, source_target_pairs={{0,4},{1,3},{2,6},{3,1},{4,0},{5,7},{6,2},{7,5},{8,12},{9,11},{10,... | collective-permute-start | bytes 786440 | tf_op jit(solution)/shard_map/ppermute | solution.py:244
  58.2 8.5 %collective-permute-start.15 = (bf16[32,4096]{1,0:T(8,128)(2,1)S(1)}, bf16[32,4096]{1,0:T(8,128)(2,1)S(1)}, u32[]{:S(2)}, u32[]{:S(2)}) collective-permute-start(bf16[32,4096]{1,0:T(8,128)(2,1)S(1)} %add_convert_fusion.2), channel_id=1, source_target_pairs={{0,2},{1,5},{2,0},{3,7},{4,6},{5,1},{6,4},{7,3},{8,10},{9,13},{10,... | collective-permute-start | bytes 786440 | tf_op jit(solution)/shard_map/ppermute | solution.py:244
  59.8 6.9 %collective-permute-start.17 = (f32[8,128]{1,0:T(8,128)S(1)}, f32[8,128]{1,0:T(8,128)S(1)}, u32[]{:S(2)}, u32[]{:S(2)}) collective-permute-start(f32[8,128]{1,0:T(8,128)S(1)} %add.49), channel_id=1, source_target_pairs={{0,2},{1,3},{2,0},{3,1},{4,6},{5,7},{6,4},{7,5},{8,10},{9,11},{10,... | collective-permute-start | bytes 12296 | tf_op jit(solution)/shard_map/ppermute | solution.py:244
  60.4 10.3 %collective-permute-start.14 = (bf16[32,4096]{1,0:T(8,128)(2,1)S(1)}, bf16[32,4096]{1,0:T(8,128)(2,1)S(1)}, u32[]{:S(2)}, u32[]{:S(2)}) collective-permute-start(bf16[32,4096]{1,0:T(8,128)(2,1)S(1)} %get-tuple-element.57), channel_id=1, source_target_pairs={{0,4},{1,3},{2,6},{3,1},{4,0},{5,7},{6,2},{7,5},{8,12},{9,11},{10,... | collective-permute-start | bytes 786440 | tf_op jit(solution)/shard_map/ppermute | solution.py:244
  62.0 16.2 %collective-permute-start.20 = (bf16[32,4096]{1,0:T(8,128)(2,1)S(1)}, bf16[32,4096]{1,0:T(8,128)(2,1)S(1)}, u32[]{:S(2)}, u32[]{:S(2)}) collective-permute-start(bf16[32,4096]{1,0:T(8,128)(2,1)S(1)} %get-tuple-element.56), channel_id=1, source_target_pairs={{0,4},{1,3},{2,6},{3,1},{4,0},{5,7},{6,2},{7,5},{8,12},{9,11},{10,... | collective-permute-start | bytes 786440 | tf_op jit(solution)/shard_map/ppermute | solution.py:244
  66.7 4.1 %collective-permute-start.18 = (f32[8,128]{1,0:T(8,128)S(1)}, f32[8,128]{1,0:T(8,128)S(1)}, u32[]{:S(2)}, u32[]{:S(2)}) collective-permute-start(f32[8,128]{1,0:T(8,128)S(1)} %add.51), channel_id=1, source_target_pairs={{0,4},{1,5},{2,6},{3,7},{4,0},{5,1},{6,2},{7,3},{8,12},{9,13},{10,... | collective-permute-start | bytes 12296 | tf_op jit(solution)/shard_map/ppermute | solution.py:244
  69.2 5.1 %collective-permute-start.21 = (bf16[16,4096]{1,0:T(8,128)(2,1)S(1)}, bf16[16,4096]{1,0:T(8,128)(2,1)S(1)}, u32[]{:S(2)}, u32[]{:S(2)}) collective-permute-start(bf16[16,4096]{1,0:T(8,128)(2,1)S(1)} %slice.62), channel_id=1, source_target_pairs={{0,8},{1,9},{2,10},{3,11},{4,12},{5,13},{6,14},{7,15},{8,0},{9,1},... | collective-permute-start | bytes 393224 | tf_op jit(solution)/shard_map/ppermute | solution.py:244
  70.9 7.2 %collective-permute-start.19 = (bf16[32,4096]{1,0:T(8,128)(2,1)S(1)}, bf16[32,4096]{1,0:T(8,128)(2,1)S(1)}, u32[]{:S(2)}, u32[]{:S(2)}) collective-permute-start(bf16[32,4096]{1,0:T(8,128)(2,1)S(1)} %add_convert_fusion.1), channel_id=1, source_target_pairs={{0,2},{1,5},{2,0},{3,7},{4,6},{5,1},{6,4},{7,3},{8,10},{9,13},{10,... | collective-permute-start | bytes 786440 | tf_op jit(solution)/shard_map/ppermute | solution.py:244
  74.3 3.9 %collective-permute-start.22 = (f32[8,128]{1,0:T(8,128)S(1)}, f32[8,128]{1,0:T(8,128)S(1)}, u32[]{:S(2)}, u32[]{:S(2)}) collective-permute-start(f32[8,128]{1,0:T(8,128)S(1)} %add.55), channel_id=1, source_target_pairs={{0,8},{1,9},{2,10},{3,11},{4,12},{5,13},{6,14},{7,15},{8,0},{9,1},... | collective-permute-start | bytes 12296 | tf_op jit(solution)/shard_map/ppermute | solution.py:244
  75.8 8.0 %collective-permute-start.24 = (bf16[16,4096]{1,0:T(8,128)(2,1)S(1)}, bf16[16,4096]{1,0:T(8,128)(2,1)S(1)}, u32[]{:S(2)}, u32[]{:S(2)}) collective-permute-start(bf16[16,4096]{1,0:T(8,128)(2,1)S(1)} %add_convert_fusion.3), channel_id=1, source_target_pairs={{0,16},{1,17},{2,18},{3,19},{4,20},{5,21},{6,22},{7,23},{8,24},{9,... | collective-permute-start | bytes 393224 | tf_op jit(solution)/shard_map/ppermute | solution.py:244
  78.2 5.1 %collective-permute-start.25 = (f32[8,128]{1,0:T(8,128)S(1)}, f32[8,128]{1,0:T(8,128)S(1)}, u32[]{:S(2)}, u32[]{:S(2)}) collective-permute-start(f32[8,128]{1,0:T(8,128)S(1)} %add.62), channel_id=1, source_target_pairs={{0,16},{1,17},{2,18},{3,19},{4,20},{5,21},{6,22},{7,23},{8,24},{9,... | collective-permute-start | bytes 12296 | tf_op jit(solution)/shard_map/ppermute | solution.py:244
  81.8 5.0 %collective-permute-start.23 = (bf16[16,4096]{1,0:T(8,128)(2,1)S(1)}, bf16[16,4096]{1,0:T(8,128)(2,1)S(1)}, u32[]{:S(2)}, u32[]{:S(2)}) collective-permute-start(bf16[16,4096]{1,0:T(8,128)(2,1)S(1)} %slice.86), channel_id=1, source_target_pairs={{0,8},{1,9},{2,10},{3,11},{4,12},{5,13},{6,14},{7,15},{8,0},{9,1},... | collective-permute-start | bytes 393224 | tf_op jit(solution)/shard_map/ppermute | solution.py:244

commit v3 on v2

--- a/solution.py
+++ b/solution.py
@@ -157,22 +157,25 @@
     )(preview, row_owner)
 
 
-def join(a, b, flops):
-    def body(a_ref, b_ref, out):
-        out[: a.shape[0], :] = a_ref[...]
-        out[a.shape[0] :, :] = b_ref[...]
-
-    return call(body, jax.ShapeDtypeStruct((a.shape[0] + b.shape[0], a.shape[1]), a.dtype), (a, b), [], 4, flops)
+def join(arrays, flops):
+    rows = sum(a.shape[0] for a in arrays)
+
+    def body(*refs):
+        at = 0
+        for ref in refs[:-1]:
+            refs[-1][at : at + ref.shape[0], :] = ref[...]
+            at += ref.shape[0]
+
+    return call(body, jax.ShapeDtypeStruct((rows, arrays[0].shape[1]), arrays[0].dtype), arrays, [], 4, flops)
 
 
 def gate_up(pieces, places, gain, w_gate, w_up):
     rows, width = sum(p.shape[0] for p in pieces), gain.shape[1]
     units = w_gate.shape[0]
-    half = rows // 2
 
     def body(*refs):
         given = refs[: len(pieces)]
-        gain_ref, gate_ref, up_ref, near, far, squares, owner, x = refs[len(pieces) :]
+        gain_ref, gate_ref, up_ref, part, squares, owner, x = refs[len(pieces) :]
         for ref, blocks in zip(given, places):
             size = ref.shape[0] // len(blocks)
             for i, to in enumerate(blocks):
@@ -186,30 +189,36 @@
         def _(i):
             tile = pl.ds(pl.multiple_of(i * TILE, TILE), TILE)
             for k, w in enumerate((gate_ref, up_ref)):
-                product = lax.dot_general(x[...], w[tile, :], NT, preferred_element_type=F32).astype(BF16)
-                near[k, :, tile] = product[:half]
-                far[k, :, tile] = product[half:]
-
-    part = jax.ShapeDtypeStruct((2, half, units), BF16)
+                part[k, :, tile] = lax.dot_general(x[...], w[tile, :], NT, preferred_element_type=F32).astype(BF16)
+
     lanes = jax.ShapeDtypeStruct((rows, LANES), F32)
-    out_shape = (part, part, lanes, lanes)
+    out_shape = (jax.ShapeDtypeStruct((2, rows, units), BF16), lanes, lanes)
     scratch = [pltpu.VMEM((rows, width), BF16)]
     return call(body, out_shape, (*pieces, gain, w_gate, w_up), scratch, 12, 4 * rows * width * units)
 
 
-def down_rows(first, mine, theirs, squares, other_squares, owner, w_down, score, own, devices, flops):
+def split_lanes(total, rows):
+    high = total.astype(BF16).astype(F32)
+    middle = (total - high).astype(BF16).astype(F32)
+    low = total - high - middle
+    at = lax.broadcasted_iota(jnp.int32, (rows, LANES), 0)
+    return jnp.where(at == 0, high, jnp.where(at == 1, middle, jnp.where(at == 2, low, 0.0))).astype(BF16)
+
+
+def down_rows(mine, theirs, squares, other_squares, owner, w_down, score, own):
     units, width = w_down.shape
-    rows = squares.shape[0] // 2
-    q = rows // 4
-    wide = 2048
-
-    def body(a, b, sq, other_sq, owner_ref, w, score_ref, own_ref, down, totals, hidden):
-        for block, other in enumerate((0, 2, 1, 3)):
+    rows = squares.shape[0]
+    q = rows // 8
+    h = q // 2
+    wide = 1024
+
+    def body(a, b, sq, other_sq, owner_ref, w, score_ref, own_ref, *rest):
+        near, across, far, (totals, hidden) = rest[:4], rest[4], rest[5:9], rest[9:]
+        for block in range(8):
+            other = block ^ 3 if block % 4 in (1, 2) else block
             here = slice(block * q, (block + 1) * q)
             there = slice(other * q, (other + 1) * q)
-            both = sq[first + block * q : first + (block + 1) * q, :1]
-            both += other_sq[first + other * q : first + (other + 1) * q, :1]
-            scale = lax.rsqrt(both / (2 * width) + 1e-05)
+            scale = lax.rsqrt((sq[here, :1] + other_sq[there, :1]) / (2 * width) + 1e-05)
             for lo in range(0, units, TILE):
                 cols = slice(lo, lo + TILE)
                 g = (a[0, here, cols].astype(F32) + b[0, there, cols].astype(F32)) * scale
@@ -219,22 +228,59 @@
         for lo in range(0, width, wide):
             cols = slice(lo, lo + wide)
             product = jnp.dot(hidden[...], w[:, cols], preferred_element_type=F32)
-            down[:, cols] = product.astype(BF16)
+            product_bf16 = product.astype(BF16)
+            for block in range(4):
+                at = block * q
+                near[block][:, cols] = product_bf16[at : at + h]
+                across[block * h : (block + 1) * h, cols] = product_bf16[at + h : at + q]
+                far[block][:, cols] = product_bf16[4 * q + at : 5 * q + at]
             row_part += jnp.sum(product * score_ref[:, cols], axis=1, keepdims=True)
-        group = owner_ref[first : first + rows, :]
+        group = owner_ref[...]
         member = group == lax.broadcasted_iota(jnp.int32, group.shape, 1).astype(F32)
         total = jnp.sum(jnp.where(member, row_part, 0.0), axis=0, keepdims=True)
-        if first == 0:
-            h = own_ref.shape[0]
-            own_part = jnp.sum(own_ref[:, :width].astype(F32) * score_ref[...], axis=1, keepdims=True)
-            total += jnp.sum(jnp.where(member[:h], own_part, 0.0), axis=0, keepdims=True)
+        own_part = jnp.sum(own_ref[:, :width].astype(F32) * score_ref[...], axis=1, keepdims=True)
+        total += jnp.sum(jnp.where(member[:h], own_part, 0.0), axis=0, keepdims=True)
         totals[...] = jnp.zeros_like(totals)
         totals[0:1, :] = total
-        totals[1:2, :] = jnp.sum(member.astype(F32), axis=0, keepdims=True) / devices
-
-    out_shape = (jax.ShapeDtypeStruct((rows, width), BF16), jax.ShapeDtypeStruct((8, LANES), F32))
+        totals[1:2, :] = jnp.sum(member.astype(F32), axis=0, keepdims=True)
+        far[3][:, width:] = split_lanes(total, q)
+
+    shapes = [(h, width)] * 4 + [(4 * h, width)] + [(q, width)] * 3 + [(q, width + LANES)]
+    blocks = [jax.ShapeDtypeStruct(shape, BF16) for shape in shapes]
+    out_shape = (*blocks, jax.ShapeDtypeStruct((8, LANES), F32))
     args = (mine, theirs, squares, other_squares, owner, w_down, score, own)
-    return call(body, out_shape, args, [pltpu.VMEM((rows, units), BF16)], 12, flops)
+    return call(body, out_shape, args, [pltpu.VMEM((rows, units), BF16)], 14, 2 * rows * units * width)
+
+
+def carried(ref):
+    return sum(ref[i : i + 1, ref.shape[1] - LANES :].astype(F32) for i in range(3))
+
+
+def fold(terms, totals, carriers, cuts, width):
+    rows = terms[0].shape[0]
+    count = len(terms)
+
+    def body(*refs):
+        given, totals_ref, brought = refs[:count], refs[count], refs[count + 1 : count + 1 + len(carriers)]
+        outs, totals_out = refs[count + 1 + len(carriers) : -1], refs[-1]
+        total = totals_ref[0:1, :]
+        for ref in brought:
+            total += carried(ref)
+        totals_out[...] = totals_ref[...]
+        totals_out[0:1, :] = total
+        for (start, stop, sent), out in zip(cuts, outs):
+            for lo in range(start, stop, 16):
+                here = slice(lo, lo + 16)
+                v = given[0][here, :width].astype(F32)
+                for ref in given[1:]:
+                    v += ref[here, :width].astype(F32)
+                out[lo - start : lo - start + 16, :width] = v.astype(BF16)
+            if sent:
+                out[:, width:] = split_lanes(total, stop - start)
+
+    shapes = [jax.ShapeDtypeStruct((stop - start, width + (LANES if sent else 0)), BF16) for start, stop, sent in cuts]
+    out_shape = (*shapes, jax.ShapeDtypeStruct(totals.shape, F32))
+    return call(body, out_shape, (*terms, totals, *carriers), [], 8, 2 * rows * width * count)
 
 
 def paired(n, tp):
@@ -252,51 +298,48 @@
         rows = preview.shape[0]
         own = payload(preview, row_owner, 10**10)
         z2, z1 = swap(own, 8), swap(own, 4)
+        own_a, own_b = swap(own, 1, 2), swap(own, 2, 1)
         z3 = swap(z2, 4)
-        near = join(own, z1, 10**10)
-        near_a, near_b = swap(near, 1, 2), swap(near, 2, 1)
-        far = join(z2, z3, 10**10)
-        far_a, far_b = swap(far, 1, 2), swap(far, 2, 1)
-        near_a, near_b = after((near_a, near_b))
-        near_c = swap(near_a, 2, 1)
-        far_a, far_b = after((far_a, far_b))
-        far_c = swap(far_a, 2, 1)
-        pieces = [near, near_a, near_b, near_c, far, far_a, far_b, far_c]
-        q = near.shape[0]
-        places = [(i * q,) for i in range(len(pieces))]
-        half = 4 * q
+        pair = join((z1, z2), 10**10)
+        pair_a, pair_b = swap(pair, 1, 2), swap(pair, 2, 1)
+        own_a, own_b, pair = after((own_a, own_b, pair))
+        own_c = swap(own_a, 2, 1)
+        z3 = join((z3,), 10**10)
+        z3_a, z3_b = swap(z3, 1, 2), swap(z3, 2, 1)
+        pair_a = join((pair_a,), 10**10)
+        pair_c = swap(pair_a, 2, 1)
+        z3_c = swap(z3_a, 2, 1)
+
+        q, half = 2 * rows, 8 * rows
+        pieces, places = [], []
+        triples = ((own, pair, z3), (own_a, pair_a, z3_a), (own_b, pair_b, z3_b), (own_c, pair_c, z3_c))
+        for i, triple in enumerate(triples):
+            at = q * i
+            pieces += triple
+            places += [(at,), (at + rows, half + at), (half + at + rows,)]
         gain, score = norm_gain[None, :], score_vec[None, :]
-        part_near, part_far, squares, owner = gate_up(pieces, places, gain, w_gate, w_up)
-        other_squares, other_far, other_near = tp_swap(squares), tp_swap(part_far), tp_swap(part_near)
-
-        def down(first, mine, other, flops):
-            return down_rows(first, mine, other, squares, other_squares, owner, w_down, score, own, n * tp, flops)
-
-        f, totals_far = down(half, part_far, other_far, 10**9)
-        f, part_near = after((f, part_near))
-        g, totals_near = down(0, part_near, other_near, 10**10)
-        f3, f2 = swap(f[3 * q :], 2, 1), swap(f[2 * q : 3 * q], 2, 1)
-        totals = totals_far + totals_near
-        f3, g, t = after((f3, g, tp_swap(totals)))
-        totals = totals + t
-        f1 = swap(add(f[q : 2 * q], f3), 1, 2)
-        g3, g2 = swap(g[3 * q :], 2, 1), swap(g[2 * q : 3 * q], 2, 1)
-        f1, f2, t = after((f1, f2, swap(totals, 1)))
-        totals = totals + t
-        f = (f[:q].astype(F32) + f2.astype(F32) + f1.astype(F32)).astype(BF16)
-        z3 = swap(f[rows:], 4)
-        g3, t = after((g3, swap(totals, 2)))
-        totals = totals + t
-        g1 = swap(add(g[q : 2 * q], g3), 1, 2)
-        z3, totals = after((z3, totals))
-        z2 = swap(add(f[:rows], z3), 8)
-        g1, g2, t = after((g1, g2, swap(totals, 4)))
-        totals = totals + t
-        g = g[:q].astype(F32) + g2.astype(F32) + g1.astype(F32)
-        z1 = swap(g[rows:].astype(BF16), 4)
-        totals = totals + swap(totals, 8)
-        verified = (own[:, : preview.shape[1]].astype(F32) + g[:rows] + z1.astype(F32) + z2.astype(F32)).astype(BF16)
-        return verified, totals[0, :CAND] / totals[1, :CAND]
+        part, squares, owner = gate_up(pieces, places, gain, w_gate, w_up)
+        other, other_squares = tp_swap(part), tp_swap(squares)
+        *near, across, f0, f1, f2, f3, totals = down_rows(part, other, squares, other_squares, owner, w_down, score, own)
+        width = preview.shape[1]
+        counts = totals[1, :CAND]
+        f3 = swap(f3, 2, 1)
+        across = swap(across, 4)
+        f2 = swap(f2, 2, 1)
+        send, totals = fold([f1, f3], totals, [f3], [(0, q, True)], width)
+        f1 = swap(send, 1, 2)
+        keep, send, totals = fold([f0, f1, f2], totals, [f1], [(0, rows, False), (rows, q, True)], width)
+        z3 = swap(send, 4)
+        near = [add(v, across[i * rows : (i + 1) * rows]) for i, v in enumerate(near)]
+        n3, n2 = swap(near[3], 2, 1), swap(near[2], 2, 1)
+        send, totals = fold([keep, z3], totals, [z3], [(0, rows, True)], width)
+        z2 = swap(send, 8)
+        n1 = swap(add(near[1], n3), 1, 2)
+        total = totals[0, :] + jnp.sum(z2[:3, width:].astype(F32), axis=0)
+        total = total + tp_swap(total)
+        verified = own[:, :width].astype(F32) + near[0].astype(F32)
+        verified = verified + n2.astype(F32) + n1.astype(F32) + z2[:, :width].astype(F32)
+        return verified.astype(BF16), total[:CAND] / counts
 
     return shards
 

time: 87.7 us -> 82.6 us (0.942)
  starting transfers between devices: 37.4 us -> 31 us
  waiting for transfers between devices: 30.1 us -> 33 us
  local copies, waits for them, and re-layouts: 1.08 us -> 0.08 us
    ppermute x22 -> x21, starting transfers between devices: 36.6 us -> 30.3 us  [swap(): return lax.ppermute(v, BOTH, pairs)]
    ppermute x4 -> x3, waiting for transfers between devices: 2.08 us -> 3.79 us  [tp_swap(): return lax.ppermute(v, 'tp', [(0, 1), (1, 0)])]
    ppermute x22 -> x21, waiting for transfers between devices: 28 us -> 29.2 us  [swap(): return lax.ppermute(v, BOTH, pairs)]
    unnamed x32 -> x30, local copies, waits for them, and re-layouts: 0.98 us -> 0.08 us
    pallas_call x5 -> x8, Pallas kernels: 14.8 us -> 14.5 us  [call(): pl.pallas_call(body, out_shape=out_shape, in_specs=[VMEM] * len(args), ou...]
  transfers between devices with their start and end apart: 26 -> 24, of which waited for: 15 -> 13; matrix products, arithmetic and copies ran while one was open for 1% -> 1% of each run, Pallas kernels for 6% -> 0%
where the time goes in v3:
time: 82.6 us; the launch traced here: 82.4 us
  waiting for transfers between devices  33 us (40%)
  starting transfers between devices  31 us (38%)
  Pallas kernels  16 us (19%)
  other arithmetic  1.43 us (2%)
  between operations  0.91 us (1%)
    ppermute x21, starting transfers between devices, swap(): return lax.ppermute(v, BOTH, pairs)  30.3 us
    ppermute x21, waiting for transfers between devices, swap(): return lax.ppermute(v, BOTH, pairs)  29.2 us
    pallas_call x8, Pallas kernels, call(): pl.pallas_call(body, out_shape=out_shape, in_specs=[VMEM] * len(args), ou...  14.5 us
    ppermute x3, waiting for transfers between devices, tp_swap(): return lax.ppermute(v, 'tp', [(0, 1), (1, 0)])  3.79 us
  transfers between devices with their start and end apart: 24, of which 13 were waited for; matrix products, arithmetic and copies ran while one was open for 1% of the time, Pallas kernels for 0%

profile of v3, /device:TPU:0, one launch (start us, length us, event | category | flops | bytes accessed | tf_op | source)
XLA Modules:
  0.0 82.4 jit_solution(9018354904647455617)
XLA Ops:
  0.6 1.6 %shard_map.86.refs_0_.own_ref = bf16[16,4224]{1,0:T(8,128)(2,1)} custom-call(bf16[16,4096]{1,0:T(8,128)(2,1)} %rows_ref.1, s32[16]{0:T(128)} %owner_ref.1), custom_call_target="tpu_custom_call" | custom-call | flops 10000000000 | bytes 262144 | tf_op jit(solution)/shard_map/pallas_call | solution.py:151
  2.2 4.0 %collective-permute-start.3 = (bf16[16,4224]{1,0:T(8,128)(2,1)}, bf16[16,4224]{1,0:T(8,128)(2,1)S(1)}, u32[]{:S(2)}, u32[]{:S(2)}) collective-permute-start(bf16[16,4224]{1,0:T(8,128)(2,1)} %shard_map.86.refs_0_.own_ref), channel_id=1, source_target_pairs={{0,16},{1,17},{2,18},{3,19},{4,20},{5,21},{6,22},{7,23},{8,24},{9,... | collective-permute-start | bytes 405512 | tf_op jit(solution)/shard_map/ppermute | solution.py:290
  6.3 1.6 %collective-permute-start.2 = (bf16[16,4224]{1,0:T(8,128)(2,1)}, bf16[16,4224]{1,0:T(8,128)(2,1)S(1)}, u32[]{:S(2)}, u32[]{:S(2)}) collective-permute-start(bf16[16,4224]{1,0:T(8,128)(2,1)} %shard_map.86.refs_0_.own_ref), channel_id=1, source_target_pairs={{0,8},{1,9},{2,10},{3,11},{4,12},{5,13},{6,14},{7,15},{8,0},{9,1},... | collective-permute-start | bytes 405512 | tf_op jit(solution)/shard_map/ppermute | solution.py:290
  7.8 1.5 %collective-permute-start.1 = (bf16[16,4224]{1,0:T(8,128)(2,1)}, bf16[16,4224]{1,0:T(8,128)(2,1)S(1)}, u32[]{:S(2)}, u32[]{:S(2)}) collective-permute-start(bf16[16,4224]{1,0:T(8,128)(2,1)} %shard_map.86.refs_0_.own_ref), channel_id=1, source_target_pairs={{0,4},{1,3},{2,6},{3,1},{4,0},{5,7},{6,2},{7,5},{8,12},{9,11},{10,... | collective-permute-start | bytes 405512 | tf_op jit(solution)/shard_map/ppermute | solution.py:290
  9.3 1.5 %collective-permute-start = (bf16[16,4224]{1,0:T(8,128)(2,1)}, bf16[16,4224]{1,0:T(8,128)(2,1)S(1)}, u32[]{:S(2)}, u32[]{:S(2)}) collective-permute-start(bf16[16,4224]{1,0:T(8,128)(2,1)} %shard_map.86.refs_0_.own_ref), channel_id=1, source_target_pairs={{0,2},{1,5},{2,0},{3,7},{4,6},{5,1},{6,4},{7,3},{8,10},{9,13},{10,... | collective-permute-start | bytes 405512 | tf_op jit(solution)/shard_map/ppermute | solution.py:290
  10.8 2.2 %collective-permute-done.3.refs_1_ = bf16[16,4224]{1,0:T(8,128)(2,1)S(1)} collective-permute-done((bf16[16,4224]{1,0:T(8,128)(2,1)}, bf16[16,4224]{1,0:T(8,128)(2,1)S(1)}, u32[]{:S(2)}, u32[]{:S(2)}) %collective-permute-start.3) | collective-permute-done | bytes 135200 | tf_op jit(solution)/shard_map/ppermute | solution.py:290
  13.1 0.7 collective-permute-start.4
  13.8 0.0 collective-permute-done.2.refs_0_
  13.8 1.6 %collective-permute-start.7 = (bf16[32,4224]{1,0:T(8,128)(2,1)S(1)}, bf16[32,4224]{1,0:T(8,128)(2,1)S(1)}, u32[]{:S(2)}, u32[]{:S(2)}) collective-permute-start(bf16[32,4224]{1,0:T(8,128)(2,1)S(1)} %shard_map.87.refs_1_), channel_id=1, source_target_pairs={{0,4},{1,3},{2,6},{3,1},{4,0},{5,7},{6,2},{7,5},{8,12},{9,11},{10,... | collective-permute-start | bytes 811016 | tf_op jit(solution)/shard_map/ppermute | solution.py:290
  15.4 1.5 %collective-permute-start.5 = (bf16[32,4224]{1,0:T(8,128)(2,1)S(1)}, bf16[32,4224]{1,0:T(8,128)(2,1)S(1)}, u32[]{:S(2)}, u32[]{:S(2)}) collective-permute-start(bf16[32,4224]{1,0:T(8,128)(2,1)S(1)} %shard_map.87.refs_1_), channel_id=1, source_target_pairs={{0,2},{1,5},{2,0},{3,7},{4,6},{5,1},{6,4},{7,3},{8,10},{9,13},{10,... | collective-permute-start | bytes 811016 | tf_op jit(solution)/shard_map/ppermute | solution.py:290
  16.9 1.2 %collective-permute-done.4.refs_0_ = bf16[16,4224]{1,0:T(8,128)(2,1)S(1)} collective-permute-done((bf16[16,4224]{1,0:T(8,128)(2,1)S(1)}, bf16[16,4224]{1,0:T(8,128)(2,1)S(1)}, u32[]{:S(2)}, u32[]{:S(2)}) %collective-permute-start.4) | collective-permute-done | bytes 135200 | tf_op jit(solution)/shard_map/ppermute | solution.py:290
  18.1 0.0 slice-start.2
  18.1 0.0 slice-start.3
  18.1 0.0 slice-start.6
  18.1 0.0 slice-start.7
  18.2 0.0 copy-start.1
  18.2 1.6 %collective-permute-start.6 = (bf16[16,4224]{1,0:T(8,128)(2,1)S(1)}, bf16[16,4224]{1,0:T(8,128)(2,1)S(1)}, u32[]{:S(2)}, u32[]{:S(2)}) collective-permute-start(bf16[16,4224]{1,0:T(8,128)(2,1)S(1)} %shard_map.88.refs_2_), channel_id=1, source_target_pairs={{0,2},{1,5},{2,0},{3,7},{4,6},{5,1},{6,4},{7,3},{8,10},{9,13},{10,... | collective-permute-start | bytes 405512 | tf_op jit(solution)/shard_map/ppermute | solution.py:290
  19.8 2.2 %collective-permute-done.5.refs_0_ = bf16[32,4224]{1,0:T(8,128)(2,1)S(1)} collective-permute-done((bf16[32,4224]{1,0:T(8,128)(2,1)S(1)}, bf16[32,4224]{1,0:T(8,128)(2,1)S(1)}, u32[]{:S(2)}, u32[]{:S(2)}) %collective-permute-start.5) | collective-permute-done | bytes 270368 | tf_op jit(solution)/shard_map/ppermute | solution.py:290
  22.0 1.6 %collective-permute-start.10 = (bf16[32,4224]{1,0:T(8,128)(2,1)S(1)}, bf16[32,4224]{1,0:T(8,128)(2,1)S(1)}, u32[]{:S(2)}, u32[]{:S(2)}) collective-permute-start(bf16[32,4224]{1,0:T(8,128)(2,1)S(1)} %shard_map.89.refs_4_), channel_id=1, source_target_pairs={{0,4},{1,3},{2,6},{3,1},{4,0},{5,7},{6,2},{7,5},{8,12},{9,11},{10,... | collective-permute-start | bytes 811016 | tf_op jit(solution)/shard_map/ppermute | solution.py:290
  23.6 0.0 collective-permute-done.1.refs_6_
  23.6 0.0 collective-permute-done.refs_3_
  23.6 0.5 collective-permute-start.9
  24.1 1.5 %collective-permute-start.8 = (bf16[16,4224]{1,0:T(8,128)(2,1)S(1)}, bf16[16,4224]{1,0:T(8,128)(2,1)S(1)}, u32[]{:S(2)}, u32[]{:S(2)}) collective-permute-start(bf16[16,4224]{1,0:T(8,128)(2,1)S(1)} %shard_map.88.refs_2_), channel_id=1, source_target_pairs={{0,4},{1,3},{2,6},{3,1},{4,0},{5,7},{6,2},{7,5},{8,12},{9,11},{10,... | collective-permute-start | bytes 405512 | tf_op jit(solution)/shard_map/ppermute | solution.py:290
  25.6 0.0 collective-permute-done.6.refs_5_
  25.6 0.5 collective-permute-start.11
  26.1 3.8 %collective-permute-done.9.refs_9_ = bf16[16,4224]{1,0:T(8,128)(2,1)S(1)} collective-permute-done((bf16[16,4224]{1,0:T(8,128)(2,1)S(1)}, bf16[16,4224]{1,0:T(8,128)(2,1)S(1)}, u32[]{:S(2)}, u32[]{:S(2)}) %collective-permute-start.9) | collective-permute-done | bytes 135200 | tf_op jit(solution)/shard_map/ppermute | solution.py:290
  30.0 1.4 %collective-permute-done.8.refs_8_ = bf16[16,4224]{1,0:T(8,128)(2,1)S(1)} collective-permute-done((bf16[16,4224]{1,0:T(8,128)(2,1)S(1)}, bf16[16,4224]{1,0:T(8,128)(2,1)S(1)}, u32[]{:S(2)}, u32[]{:S(2)}) %collective-permute-start.8) | collective-permute-done | bytes 135200 | tf_op jit(solution)/shard_map/ppermute | solution.py:290
  31.4 0.0 collective-permute-done.7.refs_7_
  31.4 1.4 %collective-permute-done.11.refs_11_ = bf16[16,4224]{1,0:T(8,128)(2,1)S(1)} collective-permute-done((bf16[16,4224]{1,0:T(8,128)(2,1)S(1)}, bf16[16,4224]{1,0:T(8,128)(2,1)S(1)}, u32[]{:S(2)}, u32[]{:S(2)}) %collective-permute-start.11) | collective-permute-done | bytes 135200 | tf_op jit(solution)/shard_map/ppermute | solution.py:290
  32.9 0.0 collective-permute-done.10.refs_10_
  33.0 0.0 slice-start.11
  33.0 0.0 copy-start.2
  33.0 9.8 %shard_map.90 = (bf16[2,256,1792]{2,1,0:T(8,128)(2,1)S(1)}, f32[256,128]{1,0:T(8,128)S(1)}, f32[256,128]{1,0:T(8,128)S(1)}) custom-call(bf16[16,4224]{1,0:T(8,128)(2,1)S(1)} %copy-done, bf16[32,4224]{1,0:T(8,128)(2,1)S(1)} %shard_map.87.refs_1_, bf16[16,4224]{1,0:T(8,128)(2,1)S(1)} %shard_map.88.refs_2_, bf16[16,4224]{1,0:T(8,128)(2,1)S(1)} %collective-permute-done.refs_3_, ...), custom_call_target="tpu_custom_call" | custom-call | flops 7516192768 | bytes 31539200 | tf_op jit(solution)/shard_map/pallas_call | solution.py:129
  42.8 0.2 collective-permute-start.12
  43.0 0.4 collective-permute-start.13
  43.4 3.5 %collective-permute-done.13.other_sq = f32[256,128]{1,0:T(8,128)S(1)} collective-permute-done((f32[256,128]{1,0:T(8,128)S(1)}, f32[256,128]{1,0:T(8,128)S(1)}, u32[]{:S(2)}, u32[]{:S(2)}) %collective-permute-start.13) | collective-permute-done | bytes 131104 | tf_op jit(solution)/shard_map/ppermute | solution.py:293
  46.8 0.0 collective-permute-done.12.b
  46.9 4.4 %shard_map.91 = (bf16[16,4096]{1,0:T(8,128)(2,1)S(1)}, bf16[16,4096]{1,0:T(8,128)(2,1)S(1)}, bf16[16,4096]{1,0:T(8,128)(2,1)S(1)}, bf16[16,4096]{1,0:T(8,128)(2,...) custom-call(bf16[2,256,1792]{2,1,0:T(8,128)(2,1)S(1)} %get-tuple-ele, ...), custom_call_target="tpu_custom_call" | custom-call | flops 3758096384 | bytes 18894848 | tf_op jit(solution)/shard_map/pallas_call | solution.py:129
  51.3 1.6 %collective-permute-start.18 = (bf16[32,4224]{1,0:T(8,128)(2,1)S(1)}, bf16[32,4224]{1,0:T(8,128)(2,1)S(1)}, u32[]{:S(2)}, u32[]{:S(2)}) collective-permute-start(bf16[32,4224]{1,0:T(8,128)(2,1)S(1)} %get-tuple-element.38), channel_id=1, source_target_pairs={{0,4},{1,3},{2,6},{3,1},{4,0},{5,7},{6,2},{7,5},{8,12},{9,11},{10,... | collective-permute-start | bytes 811016 | tf_op jit(solution)/shard_map/ppermute | solution.py:290
  52.9 0.3 collective-permute-start.14
  53.2 4.7 %collective-permute-done.18.refs_1_.refs_3_ = bf16[32,4224]{1,0:T(8,128)(2,1)S(1)} collective-permute-done((bf16[32,4224]{1,0:T(8,128)(2,1)S(1)}, bf16[32,4224]{1,0:T(8,128)(2,1)S(1)}, u32[]{:S(2)}, u32[]{:S(2)}) %collective-permute-start.18) | collective-permute-done | bytes 270368 | tf_op jit(solution)/shard_map/ppermute | solution.py:290
  57.8 0.1 shard_map.92
  57.9 1.6 %collective-permute-start.19 = (bf16[32,4224]{1,0:T(8,128)(2,1)S(1)}, bf16[32,4224]{1,0:T(8,128)(2,1)S(1)}, u32[]{:S(2)}, u32[]{:S(2)}) collective-permute-start(bf16[32,4224]{1,0:T(8,128)(2,1)S(1)} %get-tuple-element.40), channel_id=1, source_target_pairs={{0,2},{1,5},{2,0},{3,7},{4,6},{5,1},{6,4},{7,3},{8,10},{9,13},{10,... | collective-permute-start | bytes 811016 | tf_op jit(solution)/shard_map/ppermute | solution.py:290
  59.5 1.5 %collective-permute-start.20 = (bf16[32,4096]{1,0:T(8,128)(2,1)S(1)}, bf16[32,4096]{1,0:T(8,128)(2,1)S(1)}, u32[]{:S(2)}, u32[]{:S(2)}) collective-permute-start(bf16[32,4096]{1,0:T(8,128)(2,1)S(1)} %get-tuple-element.41), channel_id=1, source_target_pairs={{0,4},{1,3},{2,6},{3,1},{4,0},{5,7},{6,2},{7,5},{8,12},{9,11},{10,... | collective-permute-start | bytes 786440 | tf_op jit(solution)/shard_map/ppermute | solution.py:290
  61.0 4.9 %collective-permute-done.20.refs_2_ = bf16[32,4096]{1,0:T(8,128)(2,1)S(1)} collective-permute-done((bf16[32,4096]{1,0:T(8,128)(2,1)S(1)}, bf16[32,4096]{1,0:T(8,128)(2,1)S(1)}, u32[]{:S(2)}, u32[]{:S(2)}) %collective-permute-start.20) | collective-permute-done | bytes 262176 | tf_op jit(solution)/shard_map/ppermute | solution.py:290
  65.8 1.0 %collective-permute-done.19.refs_1_.refs_4_ = bf16[32,4224]{1,0:T(8,128)(2,1)S(1)} collective-permute-done((bf16[32,4224]{1,0:T(8,128)(2,1)S(1)}, bf16[32,4224]{1,0:T(8,128)(2,1)S(1)}, u32[]{:S(2)}, u32[]{:S(2)}) %collective-permute-start.19) | collective-permute-done | bytes 270368 | tf_op jit(solution)/shard_map/ppermute | solution.py:290
  66.8 0.1 shard_map.93
  66.9 0.3 collective-permute-start.21
  67.2 0.0 collective-permute-done.14
  67.3 0.1 add_convert_fusion.4
  67.3 1.5 %collective-permute-start.16 = (bf16[16,4096]{1,0:T(8,128)(2,1)S(1)}, bf16[16,4096]{1,0:T(8,128)(2,1)S(1)}, u32[]{:S(2)}, u32[]{:S(2)}) collective-permute-start(bf16[16,4096]{1,0:T(8,128)(2,1)S(1)} %get-tuple-element.49), channel_id=1, source_target_pairs={{0,4},{1,3},{2,6},{3,1},{4,0},{5,7},{6,2},{7,5},{8,12},{9,11},{10,... | collective-permute-start | bytes 393224 | tf_op jit(solution)/shard_map/ppermute | solution.py:290
  68.8 0.6 collective-permute-start.15
  69.4 2.8 %collective-permute-done.21.refs_1_.refs_3_ = bf16[16,4224]{1,0:T(8,128)(2,1)S(1)} collective-permute-done((bf16[16,4224]{1,0:T(8,128)(2,1)S(1)}, bf16[16,4224]{1,0:T(8,128)(2,1)S(1)}, u32[]{:S(2)}, u32[]{:S(2)}) %collective-permute-start.21) | collective-permute-done | bytes 135200 | tf_op jit(solution)/shard_map/ppermute | solution.py:290
  72.2 3.3 %collective-permute-start.22 = (bf16[16,4224]{1,0:T(8,128)(2,1)S(1)}, bf16[16,4224]{1,0:T(8,128)(2,1)S(1)}, u32[]{:S(2)}, u32[]{:S(2)}) collective-permute-start(bf16[16,4224]{1,0:T(8,128)(2,1)S(1)} %get-tuple-element.46), channel_id=1, source_target_pairs={{0,16},{1,17},{2,18},{3,19},{4,20},{5,21},{6,22},{7,23},{8,24},{9,... | collective-permute-start | bytes 405512 | tf_op jit(solution)/shard_map/ppermute | solution.py:290
  75.5 0.0 collective-permute-done.16
  75.5 0.1 add_convert_fusion.1
  75.6 1.5 %collective-permute-start.17 = (bf16[16,4096]{1,0:T(8,128)(2,1)S(1)}, bf16[16,4096]{1,0:T(8,128)(2,1)S(1)}, u32[]{:S(2)}, u32[]{:S(2)}) collective-permute-start(bf16[16,4096]{1,0:T(8,128)(2,1)S(1)} %add_convert_fusion.1), channel_id=1, source_target_pairs={{0,2},{1,5},{2,0},{3,7},{4,6},{5,1},{6,4},{7,3},{8,10},{9,13},{10,... | collective-permute-start | bytes 393224 | tf_op jit(solution)/shard_map/ppermute | solution.py:290
  77.1 3.6 %collective-permute-done.22 = bf16[16,4224]{1,0:T(8,128)(2,1)S(1)} collective-permute-done((bf16[16,4224]{1,0:T(8,128)(2,1)S(1)}, bf16[16,4224]{1,0:T(8,128)(2,1)S(1)}, u32[]{:S(2)}, u32[]{:S(2)}) %collective-permute-start.22) | collective-permute-done | bytes 135200 | tf_op jit(solution)/shard_map/ppermute | solution.py:290
  80.7 0.1 collective-permute-start.23
  80.8 0.0 collective-permute-done.15
  80.8 0.0 collective-permute-done.17
  80.8 0.8 add_convert_fusion
  81.6 0.3 collective-permute-done.23
  81.9 0.5 bitcast_divide_fusion
  (33 shorter events, 0.2 us)
Async XLA Ops:
  2.2 10.8 %collective-permute-start.3 = (bf16[16,4224]{1,0:T(8,128)(2,1)}, bf16[16,4224]{1,0:T(8,128)(2,1)S(1)}, u32[]{:S(2)}, u32[]{:S(2)}) collective-permute-start(bf16[16,4224]{1,0:T(8,128)(2,1)} %shard_map.86.refs_0_.own_ref), channel_id=1, source_target_pairs={{0,16},{1,17},{2,18},{3,19},{4,20},{5,21},{6,22},{7,23},{8,24},{9,... | collective-permute-start | bytes 405512 | tf_op jit(solution)/shard_map/ppermute | solution.py:290
  6.3 7.5 %collective-permute-start.2 = (bf16[16,4224]{1,0:T(8,128)(2,1)}, bf16[16,4224]{1,0:T(8,128)(2,1)S(1)}, u32[]{:S(2)}, u32[]{:S(2)}) collective-permute-start(bf16[16,4224]{1,0:T(8,128)(2,1)} %shard_map.86.refs_0_.own_ref), channel_id=1, source_target_pairs={{0,8},{1,9},{2,10},{3,11},{4,12},{5,13},{6,14},{7,15},{8,0},{9,1},... | collective-permute-start | bytes 405512 | tf_op jit(solution)/shard_map/ppermute | solution.py:290
  7.8 15.8 %collective-permute-start.1 = (bf16[16,4224]{1,0:T(8,128)(2,1)}, bf16[16,4224]{1,0:T(8,128)(2,1)S(1)}, u32[]{:S(2)}, u32[]{:S(2)}) collective-permute-start(bf16[16,4224]{1,0:T(8,128)(2,1)} %shard_map.86.refs_0_.own_ref), channel_id=1, source_target_pairs={{0,4},{1,3},{2,6},{3,1},{4,0},{5,7},{6,2},{7,5},{8,12},{9,11},{10,... | collective-permute-start | bytes 405512 | tf_op jit(solution)/shard_map/ppermute | solution.py:290
  9.3 14.3 %collective-permute-start = (bf16[16,4224]{1,0:T(8,128)(2,1)}, bf16[16,4224]{1,0:T(8,128)(2,1)S(1)}, u32[]{:S(2)}, u32[]{:S(2)}) collective-permute-start(bf16[16,4224]{1,0:T(8,128)(2,1)} %shard_map.86.refs_0_.own_ref), channel_id=1, source_target_pairs={{0,2},{1,5},{2,0},{3,7},{4,6},{5,1},{6,4},{7,3},{8,10},{9,13},{10,... | collective-permute-start | bytes 405512 | tf_op jit(solution)/shard_map/ppermute | solution.py:290
  13.1 5.0 %collective-permute-start.4 = (bf16[16,4224]{1,0:T(8,128)(2,1)S(1)}, bf16[16,4224]{1,0:T(8,128)(2,1)S(1)}, u32[]{:S(2)}, u32[]{:S(2)}) collective-permute-start(bf16[16,4224]{1,0:T(8,128)(2,1)S(1)} %collective-permute-done.3.refs_1_), channel_id=1, source_target_pairs={{0,8},{1,9},{2,10},{3,11},{4,12},{5,13},{6,14},{7,15},{8,0},{9,1},... | collective-permute-start | bytes 405512 | tf_op jit(solution)/shard_map/ppermute | solution.py:290
  13.8 17.6 %collective-permute-start.7 = (bf16[32,4224]{1,0:T(8,128)(2,1)S(1)}, bf16[32,4224]{1,0:T(8,128)(2,1)S(1)}, u32[]{:S(2)}, u32[]{:S(2)}) collective-permute-start(bf16[32,4224]{1,0:T(8,128)(2,1)S(1)} %shard_map.87.refs_1_), channel_id=1, source_target_pairs={{0,4},{1,3},{2,6},{3,1},{4,0},{5,7},{6,2},{7,5},{8,12},{9,11},{10,... | collective-permute-start | bytes 811016 | tf_op jit(solution)/shard_map/ppermute | solution.py:290
  15.4 6.6 %collective-permute-start.5 = (bf16[32,4224]{1,0:T(8,128)(2,1)S(1)}, bf16[32,4224]{1,0:T(8,128)(2,1)S(1)}, u32[]{:S(2)}, u32[]{:S(2)}) collective-permute-start(bf16[32,4224]{1,0:T(8,128)(2,1)S(1)} %shard_map.87.refs_1_), channel_id=1, source_target_pairs={{0,2},{1,5},{2,0},{3,7},{4,6},{5,1},{6,4},{7,3},{8,10},{9,13},{10,... | collective-permute-start | bytes 811016 | tf_op jit(solution)/shard_map/ppermute | solution.py:290
  18.1 14.8 %slice-start = ((s8[14680064]{0:T(1024)(128)(4,1)}), s8[4194304]{0:T(1024)(128)(4,1)S(1)}, s32[]{:S(2)}) async-start(s8[14680064]{0:T(1024)(128)(4,1)} %bitcast.6), calls=%async_computation | async-start | bytes 8388608
  18.1 14.8 %slice-start.1 = ((s8[14680064]{0:T(1024)(128)(4,1)}), s8[4194304]{0:T(1024)(128)(4,1)S(1)}, s32[]{:S(2)}) async-start(s8[14680064]{0:T(1024)(128)(4,1)} %bitcast.6), calls=%async_computation.1 | async-start | bytes 8388608
  18.1 14.8 %slice-start.4 = ((s8[14680064]{0:T(1024)(128)(4,1)}), s8[4194304]{0:T(1024)(128)(4,1)S(1)}, s32[]{:S(2)}) async-start(s8[14680064]{0:T(1024)(128)(4,1)} %bitcast.8), calls=%async_computation.4 | async-start | bytes 8388608
  18.1 14.8 %slice-start.5 = ((s8[14680064]{0:T(1024)(128)(4,1)}), s8[4194304]{0:T(1024)(128)(4,1)S(1)}, s32[]{:S(2)}) async-start(s8[14680064]{0:T(1024)(128)(4,1)} %bitcast.8), calls=%async_computation.5 | async-start | bytes 8388608
  18.1 14.8 %slice-start.2 = ((s8[14680064]{0:T(1024)(128)(4,1)}), s8[4194304]{0:T(1024)(128)(4,1)S(1)}, s32[]{:S(2)}) async-start(s8[14680064]{0:T(1024)(128)(4,1)} %bitcast.6), calls=%async_computation.2 | async-start | bytes 8388608
  18.1 14.8 %slice-start.3 = ((s8[14680064]{0:T(1024)(128)(4,1)}), s8[2097152]{0:T(1024)(128)(4,1)S(1)}, s32[]{:S(2)}) async-start(s8[14680064]{0:T(1024)(128)(4,1)} %bitcast.6), calls=%async_computation.3 | async-start | bytes 4194304
  18.1 14.8 %slice-start.6 = ((s8[14680064]{0:T(1024)(128)(4,1)}), s8[4194304]{0:T(1024)(128)(4,1)S(1)}, s32[]{:S(2)}) async-start(s8[14680064]{0:T(1024)(128)(4,1)} %bitcast.8), calls=%async_computation.6 | async-start | bytes 8388608
  18.1 14.8 %slice-start.7 = ((s8[14680064]{0:T(1024)(128)(4,1)}), s8[2097152]{0:T(1024)(128)(4,1)S(1)}, s32[]{:S(2)}) async-start(s8[14680064]{0:T(1024)(128)(4,1)} %bitcast.8), calls=%async_computation.7 | async-start | bytes 4194304
  18.1 14.8 %copy-start = (bf16[16,4224]{1,0:T(8,128)(2,1)S(1)}, bf16[16,4224]{1,0:T(8,128)(2,1)}, u32[]{:S(2)}) copy-start(bf16[16,4224]{1,0:T(8,128)(2,1)} %shard_map.86.refs_0_.own_ref) | copy-start | bytes 405508
  18.2 14.8 %copy-start.1 = (f32[4096]{0:T(1024)S(1)}, f32[4096]{0:T(1024)}, u32[]{:S(2)}) copy-start(f32[4096]{0:T(1024)} %param.9) | copy-start | bytes 49156
  18.2 7.5 %collective-permute-start.6 = (bf16[16,4224]{1,0:T(8,128)(2,1)S(1)}, bf16[16,4224]{1,0:T(8,128)(2,1)S(1)}, u32[]{:S(2)}, u32[]{:S(2)}) collective-permute-start(bf16[16,4224]{1,0:T(8,128)(2,1)S(1)} %shard_map.88.refs_2_), channel_id=1, source_target_pairs={{0,2},{1,5},{2,0},{3,7},{4,6},{5,1},{6,4},{7,3},{8,10},{9,13},{10,... | collective-permute-start | bytes 405512 | tf_op jit(solution)/shard_map/ppermute | solution.py:290
  22.0 24.9 %slice-start.8 = ((s8[14680064]{0:T(1024)(128)(4,1)}), s8[4194304]{0:T(1024)(128)(4,1)S(1)}, s32[]{:S(2)}) async-start(s8[14680064]{0:T(1024)(128)(4,1)} %bitcast.10), calls=%async_computation.8 | async-start | bytes 8388608
  22.0 24.9 %slice-start.9 = ((s8[14680064]{0:T(1024)(128)(4,1)}), s8[4194304]{0:T(1024)(128)(4,1)S(1)}, s32[]{:S(2)}) async-start(s8[14680064]{0:T(1024)(128)(4,1)} %bitcast.10), calls=%async_computation.9 | async-start | bytes 8388608
  22.0 24.9 %slice-start.10 = ((s8[14680064]{0:T(1024)(128)(4,1)}), s8[4194304]{0:T(1024)(128)(4,1)S(1)}, s32[]{:S(2)}) async-start(s8[14680064]{0:T(1024)(128)(4,1)} %bitcast.10), calls=%async_computation.10 | async-start | bytes 8388608
  22.0 10.9 %collective-permute-start.10 = (bf16[32,4224]{1,0:T(8,128)(2,1)S(1)}, bf16[32,4224]{1,0:T(8,128)(2,1)S(1)}, u32[]{:S(2)}, u32[]{:S(2)}) collective-permute-start(bf16[32,4224]{1,0:T(8,128)(2,1)S(1)} %shard_map.89.refs_4_), channel_id=1, source_target_pairs={{0,4},{1,3},{2,6},{3,1},{4,0},{5,7},{6,2},{7,5},{8,12},{9,11},{10,... | collective-permute-start | bytes 811016 | tf_op jit(solution)/shard_map/ppermute | solution.py:290
  23.6 6.4 %collective-permute-start.9 = (bf16[16,4224]{1,0:T(8,128)(2,1)S(1)}, bf16[16,4224]{1,0:T(8,128)(2,1)S(1)}, u32[]{:S(2)}, u32[]{:S(2)}) collective-permute-start(bf16[16,4224]{1,0:T(8,128)(2,1)S(1)} %collective-permute-done.refs_3_), channel_id=1, source_target_pairs={{0,4},{1,3},{2,6},{3,1},{4,0},{5,7},{6,2},{7,5},{8,12},{9,11},{10,... | collective-permute-start | bytes 405512 | tf_op jit(solution)/shard_map/ppermute | solution.py:290
  24.1 7.3 %collective-permute-start.8 = (bf16[16,4224]{1,0:T(8,128)(2,1)S(1)}, bf16[16,4224]{1,0:T(8,128)(2,1)S(1)}, u32[]{:S(2)}, u32[]{:S(2)}) collective-permute-start(bf16[16,4224]{1,0:T(8,128)(2,1)S(1)} %shard_map.88.refs_2_), channel_id=1, source_target_pairs={{0,4},{1,3},{2,6},{3,1},{4,0},{5,7},{6,2},{7,5},{8,12},{9,11},{10,... | collective-permute-start | bytes 405512 | tf_op jit(solution)/shard_map/ppermute | solution.py:290
  25.6 7.2 %collective-permute-start.11 = (bf16[16,4224]{1,0:T(8,128)(2,1)S(1)}, bf16[16,4224]{1,0:T(8,128)(2,1)S(1)}, u32[]{:S(2)}, u32[]{:S(2)}) collective-permute-start(bf16[16,4224]{1,0:T(8,128)(2,1)S(1)} %collective-permute-done.6.refs_5_), channel_id=1, source_target_pairs={{0,4},{1,3},{2,6},{3,1},{4,0},{5,7},{6,2},{7,5},{8,12},{9,11},{10,... | collective-permute-start | bytes 405512 | tf_op jit(solution)/shard_map/ppermute | solution.py:290
  33.0 13.9 %slice-start.11 = ((s8[14680064]{0:T(1024)(128)(4,1)}), s8[2097152]{0:T(1024)(128)(4,1)S(1)}, s32[]{:S(2)}) async-start(s8[14680064]{0:T(1024)(128)(4,1)} %bitcast.10), calls=%async_computation.11 | async-start | bytes 4194304
  33.0 13.9 %copy-start.2 = (f32[4096]{0:T(1024)S(1)}, f32[4096]{0:T(1024)}, u32[]{:S(2)}) copy-start(f32[4096]{0:T(1024)} %param.13) | copy-start | bytes 49156
  42.8 4.0 %collective-permute-start.12 = (bf16[2,256,1792]{2,1,0:T(8,128)(2,1)S(1)}, bf16[2,256,1792]{2,1,0:T(8,128)(2,1)S(1)}, u32[]{:S(2)}, u32[]{:S(2)}) collective-permute-start(bf16[2,256,1792]{2,1,0:T(8,128)(2,1)S(1)} %get-tuple-element.28.a), channel_id=1, source_target_pairs={{0,1},{1,0},{2,3},{3,2},{4,5},{5,4},{6,7},{7,6},{8,9},{9,8},{10,11... | collective-permute-start | bytes 5505032 | tf_op jit(solution)/shard_map/ppermute | solution.py:293
  43.0 3.8 %collective-permute-start.13 = (f32[256,128]{1,0:T(8,128)S(1)}, f32[256,128]{1,0:T(8,128)S(1)}, u32[]{:S(2)}, u32[]{:S(2)}) collective-permute-start(f32[256,128]{1,0:T(8,128)S(1)} %get-tuple-element.29.sq), channel_id=1, source_target_pairs={{0,1},{1,0},{2,3},{3,2},{4,5},{5,4},{6,7},{7,6},{8,9},{9,8},{10,11... | collective-permute-start | bytes 393224 | tf_op jit(solution)/shard_map/ppermute | solution.py:293
  51.3 6.5 %collective-permute-start.18 = (bf16[32,4224]{1,0:T(8,128)(2,1)S(1)}, bf16[32,4224]{1,0:T(8,128)(2,1)S(1)}, u32[]{:S(2)}, u32[]{:S(2)}) collective-permute-start(bf16[32,4224]{1,0:T(8,128)(2,1)S(1)} %get-tuple-element.38), channel_id=1, source_target_pairs={{0,4},{1,3},{2,6},{3,1},{4,0},{5,7},{6,2},{7,5},{8,12},{9,11},{10,... | collective-permute-start | bytes 811016 | tf_op jit(solution)/shard_map/ppermute | solution.py:290
  52.9 14.3 %collective-permute-start.14 = (bf16[64,4096]{1,0:T(8,128)(2,1)S(1)}, bf16[64,4096]{1,0:T(8,128)(2,1)S(1)}, u32[]{:S(2)}, u32[]{:S(2)}) collective-permute-start(bf16[64,4096]{1,0:T(8,128)(2,1)S(1)} %get-tuple-element.32), channel_id=1, source_target_pairs={{0,8},{1,9},{2,10},{3,11},{4,12},{5,13},{6,14},{7,15},{8,0},{9,1},... | collective-permute-start | bytes 1572872 | tf_op jit(solution)/shard_map/ppermute | solution.py:290
  57.9 8.9 %collective-permute-start.19 = (bf16[32,4224]{1,0:T(8,128)(2,1)S(1)}, bf16[32,4224]{1,0:T(8,128)(2,1)S(1)}, u32[]{:S(2)}, u32[]{:S(2)}) collective-permute-start(bf16[32,4224]{1,0:T(8,128)(2,1)S(1)} %get-tuple-element.40), channel_id=1, source_target_pairs={{0,2},{1,5},{2,0},{3,7},{4,6},{5,1},{6,4},{7,3},{8,10},{9,13},{10,... | collective-permute-start | bytes 811016 | tf_op jit(solution)/shard_map/ppermute | solution.py:290
  59.5 6.4 %collective-permute-start.20 = (bf16[32,4096]{1,0:T(8,128)(2,1)S(1)}, bf16[32,4096]{1,0:T(8,128)(2,1)S(1)}, u32[]{:S(2)}, u32[]{:S(2)}) collective-permute-start(bf16[32,4096]{1,0:T(8,128)(2,1)S(1)} %get-tuple-element.41), channel_id=1, source_target_pairs={{0,4},{1,3},{2,6},{3,1},{4,0},{5,7},{6,2},{7,5},{8,12},{9,11},{10,... | collective-permute-start | bytes 786440 | tf_op jit(solution)/shard_map/ppermute | solution.py:290
  66.9 5.2 %collective-permute-start.21 = (bf16[16,4224]{1,0:T(8,128)(2,1)S(1)}, bf16[16,4224]{1,0:T(8,128)(2,1)S(1)}, u32[]{:S(2)}, u32[]{:S(2)}) collective-permute-start(bf16[16,4224]{1,0:T(8,128)(2,1)S(1)} %get-tuple-element.44), channel_id=1, source_target_pairs={{0,8},{1,9},{2,10},{3,11},{4,12},{5,13},{6,14},{7,15},{8,0},{9,1},... | collective-permute-start | bytes 405512 | tf_op jit(solution)/shard_map/ppermute | solution.py:290
  67.3 8.2 %collective-permute-start.16 = (bf16[16,4096]{1,0:T(8,128)(2,1)S(1)}, bf16[16,4096]{1,0:T(8,128)(2,1)S(1)}, u32[]{:S(2)}, u32[]{:S(2)}) collective-permute-start(bf16[16,4096]{1,0:T(8,128)(2,1)S(1)} %get-tuple-element.49), channel_id=1, source_target_pairs={{0,4},{1,3},{2,6},{3,1},{4,0},{5,7},{6,2},{7,5},{8,12},{9,11},{10,... | collective-permute-start | bytes 393224 | tf_op jit(solution)/shard_map/ppermute | solution.py:290
  68.8 12.0 %collective-permute-start.15 = (bf16[16,4096]{1,0:T(8,128)(2,1)S(1)}, bf16[16,4096]{1,0:T(8,128)(2,1)S(1)}, u32[]{:S(2)}, u32[]{:S(2)}) collective-permute-start(bf16[16,4096]{1,0:T(8,128)(2,1)S(1)} %get-tuple-element.48), channel_id=1, source_target_pairs={{0,4},{1,3},{2,6},{3,1},{4,0},{5,7},{6,2},{7,5},{8,12},{9,11},{10,... | collective-permute-start | bytes 393224 | tf_op jit(solution)/shard_map/ppermute | solution.py:290
  72.2 8.5 %collective-permute-start.22 = (bf16[16,4224]{1,0:T(8,128)(2,1)S(1)}, bf16[16,4224]{1,0:T(8,128)(2,1)S(1)}, u32[]{:S(2)}, u32[]{:S(2)}) collective-permute-start(bf16[16,4224]{1,0:T(8,128)(2,1)S(1)} %get-tuple-element.46), channel_id=1, source_target_pairs={{0,16},{1,17},{2,18},{3,19},{4,20},{5,21},{6,22},{7,23},{8,24},{9,... | collective-permute-start | bytes 405512 | tf_op jit(solution)/shard_map/ppermute | solution.py:290
  75.6 5.2 %collective-permute-start.17 = (bf16[16,4096]{1,0:T(8,128)(2,1)S(1)}, bf16[16,4096]{1,0:T(8,128)(2,1)S(1)}, u32[]{:S(2)}, u32[]{:S(2)}) collective-permute-start(bf16[16,4096]{1,0:T(8,128)(2,1)S(1)} %add_convert_fusion.1), channel_id=1, source_target_pairs={{0,2},{1,5},{2,0},{3,7},{4,6},{5,1},{6,4},{7,3},{8,10},{9,13},{10,... | collective-permute-start | bytes 393224 | tf_op jit(solution)/shard_map/ppermute | solution.py:290
  80.7 1.2 %collective-permute-start.23 = (f32[128]{0:T(128)S(1)}, f32[128]{0:T(128)S(1)}, u32[]{:S(2)}, u32[]{:S(2)}) collective-permute-start(f32[128]{0:T(128)S(1)} %bitcast_add_fusion), channel_id=1, source_target_pairs={{0,1},{1,0},{2,3},{3,2},{4,5},{5,4},{6,7},{7,6},{8,9},{9,8},{10,11... | collective-permute-start | bytes 1544 | tf_op jit(solution)/shard_map/ppermute | solution.py:293

commit v4 on v3

--- a/solution.py
+++ b/solution.py
@@ -150,7 +150,7 @@
 
     return pl.pallas_call(
         body,
-        out_shape=jax.ShapeDtypeStruct((rows, width + LANES), BF16),
+        out_shape=pltpu.VMEM((rows, width + LANES), BF16),
         in_specs=[VMEM, pl.BlockSpec(memory_space=pltpu.SMEM)],
         out_specs=VMEM,
         cost_estimate=pl.CostEstimate(flops=flops, bytes_accessed=4 * rows * width, transcendentals=0),
@@ -169,21 +169,38 @@
     return call(body, jax.ShapeDtypeStruct((rows, arrays[0].shape[1]), arrays[0].dtype), arrays, [], 4, flops)
 
 
-def gate_up(pieces, places, gain, w_gate, w_up):
-    rows, width = sum(p.shape[0] for p in pieces), gain.shape[1]
+def place_rows(pieces, places, gain_ref, x, squares, owner):
+    width = x.shape[1]
+    for ref, blocks in zip(pieces, places):
+        size = ref.shape[0] // len(blocks)
+        for i, to in enumerate(blocks):
+            v = ref[i * size : (i + 1) * size, :width].astype(F32)
+            here = slice(to, to + size)
+            owner[here, :] = ref[i * size : (i + 1) * size, width:].astype(F32)
+            squares[here, :] = jnp.broadcast_to(jnp.sum(v * v, axis=1, keepdims=True), (size, LANES))
+            x[here, :] = (v * gain_ref[...]).astype(BF16)
+
+
+def early_rows(pieces, places, gain, rows, flops):
+    def body(*refs):
+        place_rows(refs[: len(pieces)], places, *refs[len(pieces) :])
+
+    lanes = jax.ShapeDtypeStruct((rows, LANES), F32)
+    out_shape = (jax.ShapeDtypeStruct((rows, gain.shape[1]), BF16), lanes, lanes)
+    return call(body, out_shape, (*pieces, gain), [], 4, flops)
+
+
+def gate_up(early, early_places, pieces, places, gain, w_gate, w_up):
+    rows, width = early[0].shape
     units = w_gate.shape[0]
 
-    def body(*refs):
+    def body(x_in, squares_in, owner_in, *refs):
         given = refs[: len(pieces)]
         gain_ref, gate_ref, up_ref, part, squares, owner, x = refs[len(pieces) :]
-        for ref, blocks in zip(given, places):
-            size = ref.shape[0] // len(blocks)
-            for i, to in enumerate(blocks):
-                v = ref[i * size : (i + 1) * size, :width].astype(F32)
-                here = slice(to, to + size)
-                owner[here, :] = ref[i * size : (i + 1) * size, width:].astype(F32)
-                squares[here, :] = jnp.broadcast_to(jnp.sum(v * v, axis=1, keepdims=True), (size, LANES))
-                x[here, :] = (v * gain_ref[...]).astype(BF16)
+        for start, stop in early_places:
+            for source, to in ((x_in, x), (squares_in, squares), (owner_in, owner)):
+                to[start:stop, :] = source[start:stop, :]
+        place_rows(given, places, gain_ref, x, squares, owner)
 
         @pl.loop(0, units // TILE)
         def _(i):
@@ -194,7 +211,8 @@
     lanes = jax.ShapeDtypeStruct((rows, LANES), F32)
     out_shape = (jax.ShapeDtypeStruct((2, rows, units), BF16), lanes, lanes)
     scratch = [pltpu.VMEM((rows, width), BF16)]
-    return call(body, out_shape, (*pieces, gain, w_gate, w_up), scratch, 12, 4 * rows * width * units)
+    args = (*early, *pieces, gain, w_gate, w_up)
+    return call(body, out_shape, args, scratch, 7, 4 * rows * width * units)
 
 
 def split_lanes(total, rows):
@@ -256,8 +274,7 @@
     return sum(ref[i : i + 1, ref.shape[1] - LANES :].astype(F32) for i in range(3))
 
 
-def fold(terms, totals, carriers, cuts, width):
-    rows = terms[0].shape[0]
+def fold(terms, totals, carriers, cuts, width, flops=0):
     count = len(terms)
 
     def body(*refs):
@@ -280,7 +297,7 @@
 
     shapes = [jax.ShapeDtypeStruct((stop - start, width + (LANES if sent else 0)), BF16) for start, stop, sent in cuts]
     out_shape = (*shapes, jax.ShapeDtypeStruct(totals.shape, F32))
-    return call(body, out_shape, (*terms, totals, *carriers), [], 8, 2 * rows * width * count)
+    return call(body, out_shape, (*terms, totals, *carriers), [], 8, flops)
 
 
 def paired(n, tp):
@@ -297,28 +314,29 @@
     def shards(preview, row_owner, norm_gain, w_gate, w_up, w_down, score_vec):
         rows = preview.shape[0]
         own = payload(preview, row_owner, 10**10)
-        z2, z1 = swap(own, 8), swap(own, 4)
+        z2 = swap(own, 8)
         own_a, own_b = swap(own, 1, 2), swap(own, 2, 1)
         z3 = swap(z2, 4)
-        pair = join((z1, z2), 10**10)
-        pair_a, pair_b = swap(pair, 1, 2), swap(pair, 2, 1)
-        own_a, own_b, pair = after((own_a, own_b, pair))
+        z2, own_a, own_b = after((join((z2,), 10**10), own_a, own_b))
+        z2_a, z2_b = swap(z2, 1, 2), swap(z2, 2, 1)
         own_c = swap(own_a, 2, 1)
+        across = swap(join((own, own_a, own_b), 0), 4)
         z3 = join((z3,), 10**10)
         z3_a, z3_b = swap(z3, 1, 2), swap(z3, 2, 1)
-        pair_a = join((pair_a,), 10**10)
-        pair_c = swap(pair_a, 2, 1)
-        z3_c = swap(z3_a, 2, 1)
+        z2_a = join((z2_a,), 10**10)
+        z3_a, z3_b, z2_b, own_c = after((z3_a, z3_b, z2_b, own_c))
+        across_c = swap(own_c, 4)
+        far_c = swap(join((z2_a, z3_a), 0), 2, 1)
 
         q, half = 2 * rows, 8 * rows
-        pieces, places = [], []
-        triples = ((own, pair, z3), (own_a, pair_a, z3_a), (own_b, pair_b, z3_b), (own_c, pair_c, z3_c))
-        for i, triple in enumerate(triples):
-            at = q * i
-            pieces += triple
-            places += [(at,), (at + rows, half + at), (half + at + rows,)]
         gain, score = norm_gain[None, :], score_vec[None, :]
-        part, squares, owner = gate_up(pieces, places, gain, w_gate, w_up)
+        pieces = [own, own_a, own_b, own_c, across, z2, z2_a, z2_b, z3, z3_a, z3_b]
+        places = [(i * q,) for i in range(4)] + [tuple(i * q + rows for i in range(3))]
+        places += [(half + i * q,) for i in range(3)] + [(half + i * q + rows,) for i in range(3)]
+        early = early_rows(pieces, places, gain, 2 * half, 10**9)
+        early_places = [(0, half - rows), (half, half + 3 * q)]
+        late_places = [(half - rows,), (half + 3 * q,)]
+        part, squares, owner = gate_up(early, early_places, [across_c, far_c], late_places, gain, w_gate, w_up)
         other, other_squares = tp_swap(part), tp_swap(squares)
         *near, across, f0, f1, f2, f3, totals = down_rows(part, other, squares, other_squares, owner, w_down, score, own)
         width = preview.shape[1]
@@ -326,9 +344,10 @@
         f3 = swap(f3, 2, 1)
         across = swap(across, 4)
         f2 = swap(f2, 2, 1)
-        send, totals = fold([f1, f3], totals, [f3], [(0, q, True)], width)
+        send, totals = fold([f1, f3], totals, [f3], [(0, q, True)], width, 2 * 10**9)
         f1 = swap(send, 1, 2)
-        keep, send, totals = fold([f0, f1, f2], totals, [f1], [(0, rows, False), (rows, q, True)], width)
+        f0, _ = fold([f0, f2], totals, [], [(0, q, False)], width, 2 * 10**9)
+        keep, send, totals = fold([f0, f1], totals, [f1], [(0, rows, False), (rows, q, True)], width)
         z3 = swap(send, 4)
         near = [add(v, across[i * rows : (i + 1) * rows]) for i, v in enumerate(near)]
         n3, n2 = swap(near[3], 2, 1), swap(near[2], 2, 1)

time: 82.6 us -> 79 us (0.956)
  waiting for transfers between devices: 33 us -> 27.6 us
  starting transfers between devices: 31 us -> 32.4 us
    ppermute x21, waiting for transfers between devices: 29.2 us -> 23.8 us  [swap(): return lax.ppermute(v, BOTH, pairs)]
    ppermute x21, starting transfers between devices: 30.3 us -> 31.8 us  [swap(): return lax.ppermute(v, BOTH, pairs)]
    pallas_call x8 -> x12, Pallas kernels: 14.5 us -> 15.4 us  [call(): pl.pallas_call(body, out_shape=out_shape, in_specs=[VMEM] * len(args), ou...]
  transfers between devices with their start and end apart: 24 -> 24, of which waited for: 13 -> 14; matrix products, arithmetic and copies ran while one was open for 1% -> 1% of each run, Pallas kernels for 0% -> 2%
where the time goes in v4:
time: 79 us; the launch traced here: 78.8 us
  starting transfers between devices  32.4 us (41%)
  waiting for transfers between devices  27.6 us (35%)
  Pallas kernels  16.3 us (21%)
  other arithmetic  1.43 us (2%)
  between operations  0.94 us (1%)
    ppermute x21, starting transfers between devices, swap(): return lax.ppermute(v, BOTH, pairs)  31.8 us
    ppermute x21, waiting for transfers between devices, swap(): return lax.ppermute(v, BOTH, pairs)  23.8 us
    pallas_call x12, Pallas kernels, call(): pl.pallas_call(body, out_shape=out_shape, in_specs=[VMEM] * len(args), ou...  15.4 us
    ppermute x3, waiting for transfers between devices, tp_swap(): return lax.ppermute(v, 'tp', [(0, 1), (1, 0)])  3.79 us
  transfers between devices with their start and end apart: 24, of which 14 were waited for; matrix products, arithmetic and copies ran while one was open for 1% of the time, Pallas kernels for 2%

profile of v4, /device:TPU:0, one launch (start us, length us, event | category | flops | bytes accessed | tf_op | source)
XLA Modules:
  0.0 78.8 jit_solution(18181013693614679841)
XLA Ops:
  0.6 0.9 %shard_map.86.refs_0_.own_ref = bf16[16,4224]{1,0:T(8,128)(2,1)S(1)} custom-call(bf16[16,4096]{1,0:T(8,128)(2,1)} %rows_ref.1, s32[16]{0:T(128)} %owner_ref.1), custom_call_target="tpu_custom_call" | custom-call | flops 10000000000 | bytes 262144 | tf_op jit(solution)/shard_map/pallas_call | solution.py:151
  1.6 4.1 %collective-permute-start = (bf16[16,4224]{1,0:T(8,128)(2,1)S(1)}, bf16[16,4224]{1,0:T(8,128)(2,1)S(1)}, u32[]{:S(2)}, u32[]{:S(2)}) collective-permute-start(bf16[16,4224]{1,0:T(8,128)(2,1)S(1)} %shard_map.86.refs_0_.own_ref), channel_id=1, source_target_pairs={{0,16},{1,17},{2,18},{3,19},{4,20},{5,21},{6,22},{7,23},{8,24},{9,... | collective-permute-start | bytes 405512 | tf_op jit(solution)/shard_map/ppermute | solution.py:307
  5.7 1.5 %collective-permute-start.2 = (bf16[16,4224]{1,0:T(8,128)(2,1)S(1)}, bf16[16,4224]{1,0:T(8,128)(2,1)S(1)}, u32[]{:S(2)}, u32[]{:S(2)}) collective-permute-start(bf16[16,4224]{1,0:T(8,128)(2,1)S(1)} %shard_map.86.refs_0_.own_ref), channel_id=1, source_target_pairs={{0,4},{1,3},{2,6},{3,1},{4,0},{5,7},{6,2},{7,5},{8,12},{9,11},{10,... | collective-permute-start | bytes 405512 | tf_op jit(solution)/shard_map/ppermute | solution.py:307
  7.2 1.5 %collective-permute-start.1 = (bf16[16,4224]{1,0:T(8,128)(2,1)S(1)}, bf16[16,4224]{1,0:T(8,128)(2,1)S(1)}, u32[]{:S(2)}, u32[]{:S(2)}) collective-permute-start(bf16[16,4224]{1,0:T(8,128)(2,1)S(1)} %shard_map.86.refs_0_.own_ref), channel_id=1, source_target_pairs={{0,2},{1,5},{2,0},{3,7},{4,6},{5,1},{6,4},{7,3},{8,10},{9,13},{10,... | collective-permute-start | bytes 405512 | tf_op jit(solution)/shard_map/ppermute | solution.py:307
  8.7 3.5 %collective-permute-done.refs_0_ = bf16[16,4224]{1,0:T(8,128)(2,1)S(1)} collective-permute-done((bf16[16,4224]{1,0:T(8,128)(2,1)S(1)}, bf16[16,4224]{1,0:T(8,128)(2,1)S(1)}, u32[]{:S(2)}, u32[]{:S(2)}) %collective-permute-start) | collective-permute-done | bytes 135200 | tf_op jit(solution)/shard_map/ppermute | solution.py:307
  12.2 0.7 collective-permute-start.3
  12.9 0.0 collective-permute-done.2.refs_2_
  12.9 0.0 collective-permute-done.1.refs_1_
  12.9 1.6 %collective-permute-start.9 = (bf16[16,4224]{1,0:T(8,128)(2,1)S(1)}, bf16[16,4224]{1,0:T(8,128)(2,1)S(1)}, u32[]{:S(2)}, u32[]{:S(2)}) collective-permute-start(bf16[16,4224]{1,0:T(8,128)(2,1)S(1)} %shard_map.87.refs_5_), channel_id=1, source_target_pairs={{0,2},{1,5},{2,0},{3,7},{4,6},{5,1},{6,4},{7,3},{8,10},{9,13},{10,... | collective-permute-start | bytes 405512 | tf_op jit(solution)/shard_map/ppermute | solution.py:307
  14.5 1.5 %collective-permute-start.6 = (bf16[16,4224]{1,0:T(8,128)(2,1)S(1)}, bf16[16,4224]{1,0:T(8,128)(2,1)S(1)}, u32[]{:S(2)}, u32[]{:S(2)}) collective-permute-start(bf16[16,4224]{1,0:T(8,128)(2,1)S(1)} %shard_map.87.refs_5_), channel_id=1, source_target_pairs={{0,4},{1,3},{2,6},{3,1},{4,0},{5,7},{6,2},{7,5},{8,12},{9,11},{10,... | collective-permute-start | bytes 405512 | tf_op jit(solution)/shard_map/ppermute | solution.py:307
  16.0 0.5 collective-permute-start.7
  16.5 1.4 %collective-permute-start.8 = (bf16[48,4224]{1,0:T(8,128)(2,1)S(1)}, bf16[48,4224]{1,0:T(8,128)(2,1)S(1)}, u32[]{:S(2)}, u32[]{:S(2)}) collective-permute-start(bf16[48,4224]{1,0:T(8,128)(2,1)S(1)} %shard_map.89), channel_id=1, source_target_pairs={{0,8},{1,9},{2,10},{3,11},{4,12},{5,13},{6,14},{7,15},{8,0},{9,1},... | collective-permute-start | bytes 1216520 | tf_op jit(solution)/shard_map/ppermute | solution.py:307
  17.9 0.0 collective-permute-done.3.refs_0_
  18.0 0.0 slice-start.5
  18.0 0.0 copy-start
  18.0 0.0 slice-start.2
  18.0 0.0 slice-start.3
  18.0 0.0 slice-start.6
  18.0 0.0 slice-start.7
  18.0 1.6 %collective-permute-start.5 = (bf16[16,4224]{1,0:T(8,128)(2,1)S(1)}, bf16[16,4224]{1,0:T(8,128)(2,1)S(1)}, u32[]{:S(2)}, u32[]{:S(2)}) collective-permute-start(bf16[16,4224]{1,0:T(8,128)(2,1)S(1)} %shard_map.88.refs_8_), channel_id=1, source_target_pairs={{0,4},{1,3},{2,6},{3,1},{4,0},{5,7},{6,2},{7,5},{8,12},{9,11},{10,... | collective-permute-start | bytes 405512 | tf_op jit(solution)/shard_map/ppermute | solution.py:307
  19.6 1.3 %collective-permute-start.4 = (bf16[16,4224]{1,0:T(8,128)(2,1)S(1)}, bf16[16,4224]{1,0:T(8,128)(2,1)S(1)}, u32[]{:S(2)}, u32[]{:S(2)}) collective-permute-start(bf16[16,4224]{1,0:T(8,128)(2,1)S(1)} %shard_map.88.refs_8_), channel_id=1, source_target_pairs={{0,2},{1,5},{2,0},{3,7},{4,6},{5,1},{6,4},{7,3},{8,10},{9,13},{10,... | collective-permute-start | bytes 405512 | tf_op jit(solution)/shard_map/ppermute | solution.py:307
  20.9 1.5 %collective-permute-done.7.refs_3_ = bf16[16,4224]{1,0:T(8,128)(2,1)S(1)} collective-permute-done((bf16[16,4224]{1,0:T(8,128)(2,1)S(1)}, bf16[16,4224]{1,0:T(8,128)(2,1)S(1)}, u32[]{:S(2)}, u32[]{:S(2)}) %collective-permute-start.7) | collective-permute-done | bytes 135200 | tf_op jit(solution)/shard_map/ppermute | solution.py:307
  22.4 0.0 collective-permute-done.6.refs_7_
  22.4 1.4 %collective-permute-done.5.refs_10_ = bf16[16,4224]{1,0:T(8,128)(2,1)S(1)} collective-permute-done((bf16[16,4224]{1,0:T(8,128)(2,1)S(1)}, bf16[16,4224]{1,0:T(8,128)(2,1)S(1)}, u32[]{:S(2)}, u32[]{:S(2)}) %collective-permute-start.5) | collective-permute-done | bytes 135200 | tf_op jit(solution)/shard_map/ppermute | solution.py:307
  23.9 0.8 collective-permute-done.4.refs_9_.refs_1_
  24.7 1.4 %collective-permute-start.11 = (bf16[32,4224]{1,0:T(8,128)(2,1)S(1)}, bf16[32,4224]{1,0:T(8,128)(2,1)S(1)}, u32[]{:S(2)}, u32[]{:S(2)}) collective-permute-start(bf16[32,4224]{1,0:T(8,128)(2,1)S(1)} %shard_map.92), channel_id=1, source_target_pairs={{0,4},{1,3},{2,6},{3,1},{4,0},{5,7},{6,2},{7,5},{8,12},{9,11},{10,... | collective-permute-start | bytes 811016 | tf_op jit(solution)/shard_map/ppermute | solution.py:307
  26.1 1.3 %collective-permute-start.10 = (bf16[16,4224]{1,0:T(8,128)(2,1)S(1)}, bf16[16,4224]{1,0:T(8,128)(2,1)S(1)}, u32[]{:S(2)}, u32[]{:S(2)}) collective-permute-start(bf16[16,4224]{1,0:T(8,128)(2,1)S(1)} %collective-permute-done.7.refs_3_), channel_id=1, source_target_pairs={{0,8},{1,9},{2,10},{3,11},{4,12},{5,13},{6,14},{7,15},{8,0},{9,1},... | collective-permute-start | bytes 405512 | tf_op jit(solution)/shard_map/ppermute | solution.py:307
  27.4 0.0 collective-permute-done.8.refs_4_
  27.4 0.7 shard_map.91
  28.1 3.0 %collective-permute-done.10.refs_0_ = bf16[16,4224]{1,0:T(8,128)(2,1)S(1)} collective-permute-done((bf16[16,4224]{1,0:T(8,128)(2,1)S(1)}, bf16[16,4224]{1,0:T(8,128)(2,1)S(1)}, u32[]{:S(2)}, u32[]{:S(2)}) %collective-permute-start.10) | collective-permute-done | bytes 135200 | tf_op jit(solution)/shard_map/ppermute | solution.py:307
  31.1 0.1 collective-permute-done.11.refs_1_
  31.3 0.0 slice-start.9
  31.3 0.0 slice-start.11
  31.3 0.0 copy-start.1
  31.3 9.3 %shard_map.93 = (bf16[2,256,1792]{2,1,0:T(8,128)(2,1)S(1)}, f32[256,128]{1,0:T(8,128)S(1)}, f32[256,128]{1,0:T(8,128)S(1)}) custom-call(bf16[256,4096]{1,0:T(8,128)(2,1)S(1)} %get-tuple-element.40.x_in, f32[256,128]{1,0:T(8,128)S(1)} %get-tuple-element.41.squares_in, f32[256,128]{1,0:T(8,128)S(1)} %get-tuple-element.42.owner_in, ...), custom_call_target="tpu_custom_call" | custom-call | flops 7516192768 | bytes 32141312 | tf_op jit(solution)/shard_map/pallas_call | solution.py:129
  40.6 0.1 collective-permute-start.12
  40.7 0.5 collective-permute-start.13
  41.2 3.5 %collective-permute-done.13.other_sq = f32[256,128]{1,0:T(8,128)S(1)} collective-permute-done((f32[256,128]{1,0:T(8,128)S(1)}, f32[256,128]{1,0:T(8,128)S(1)}, u32[]{:S(2)}, u32[]{:S(2)}) %collective-permute-start.13) | collective-permute-done | bytes 131104 | tf_op jit(solution)/shard_map/ppermute | solution.py:310
  44.7 4.6 %shard_map.94 = (bf16[16,4096]{1,0:T(8,128)(2,1)S(1)}, bf16[16,4096]{1,0:T(8,128)(2,1)S(1)}, bf16[16,4096]{1,0:T(8,128)(2,1)S(1)}, bf16[16,4096]{1,0:T(8,128)(2,...) custom-call(bf16[2,256,1792]{2,1,0:T(8,128)(2,1)S(1)} %get-tuple-ele, ...), custom_call_target="tpu_custom_call" | custom-call | flops 3758096384 | bytes 18894848 | tf_op jit(solution)/shard_map/pallas_call | solution.py:129
  49.3 1.4 %collective-permute-start.19 = (bf16[32,4224]{1,0:T(8,128)(2,1)S(1)}, bf16[32,4224]{1,0:T(8,128)(2,1)S(1)}, u32[]{:S(2)}, u32[]{:S(2)}) collective-permute-start(bf16[32,4224]{1,0:T(8,128)(2,1)S(1)} %get-tuple-element.54), channel_id=1, source_target_pairs={{0,4},{1,3},{2,6},{3,1},{4,0},{5,7},{6,2},{7,5},{8,12},{9,11},{10,... | collective-permute-start | bytes 811016 | tf_op jit(solution)/shard_map/ppermute | solution.py:307
  50.7 1.4 %collective-permute-start.14 = (bf16[64,4096]{1,0:T(8,128)(2,1)S(1)}, bf16[64,4096]{1,0:T(8,128)(2,1)S(1)}, u32[]{:S(2)}, u32[]{:S(2)}) collective-permute-start(bf16[64,4096]{1,0:T(8,128)(2,1)S(1)} %get-tuple-element.47), channel_id=1, source_target_pairs={{0,8},{1,9},{2,10},{3,11},{4,12},{5,13},{6,14},{7,15},{8,0},{9,1},... | collective-permute-start | bytes 1572872 | tf_op jit(solution)/shard_map/ppermute | solution.py:307
  52.0 0.6 collective-permute-start.18
  52.6 3.2 %collective-permute-done.19.refs_1_.refs_3_ = bf16[32,4224]{1,0:T(8,128)(2,1)S(1)} collective-permute-done((bf16[32,4224]{1,0:T(8,128)(2,1)S(1)}, bf16[32,4224]{1,0:T(8,128)(2,1)S(1)}, u32[]{:S(2)}, u32[]{:S(2)}) %collective-permute-start.19) | collective-permute-done | bytes 270368 | tf_op jit(solution)/shard_map/ppermute | solution.py:307
  55.8 0.1 shard_map.95
  55.9 1.4 %collective-permute-start.20 = (bf16[32,4224]{1,0:T(8,128)(2,1)S(1)}, bf16[32,4224]{1,0:T(8,128)(2,1)S(1)}, u32[]{:S(2)}, u32[]{:S(2)}) collective-permute-start(bf16[32,4224]{1,0:T(8,128)(2,1)S(1)} %get-tuple-element.58), channel_id=1, source_target_pairs={{0,2},{1,5},{2,0},{3,7},{4,6},{5,1},{6,4},{7,3},{8,10},{9,13},{10,... | collective-permute-start | bytes 811016 | tf_op jit(solution)/shard_map/ppermute | solution.py:307
  57.3 2.0 %collective-permute-done.18.refs_1_ = bf16[32,4096]{1,0:T(8,128)(2,1)S(1)} collective-permute-done((bf16[32,4096]{1,0:T(8,128)(2,1)S(1)}, bf16[32,4096]{1,0:T(8,128)(2,1)S(1)}, u32[]{:S(2)}, u32[]{:S(2)}) %collective-permute-start.18) | collective-permute-done | bytes 262176 | tf_op jit(solution)/shard_map/ppermute | solution.py:307
  59.4 0.6 shard_map.96
  60.0 2.4 %collective-permute-done.20.refs_1_.refs_3_ = bf16[32,4224]{1,0:T(8,128)(2,1)S(1)} collective-permute-done((bf16[32,4224]{1,0:T(8,128)(2,1)S(1)}, bf16[32,4224]{1,0:T(8,128)(2,1)S(1)}, u32[]{:S(2)}, u32[]{:S(2)}) %collective-permute-start.20) | collective-permute-done | bytes 270368 | tf_op jit(solution)/shard_map/ppermute | solution.py:307
  62.4 0.1 shard_map.97
  62.5 1.3 %collective-permute-start.21 = (bf16[16,4224]{1,0:T(8,128)(2,1)S(1)}, bf16[16,4224]{1,0:T(8,128)(2,1)S(1)}, u32[]{:S(2)}, u32[]{:S(2)}) collective-permute-start(bf16[16,4224]{1,0:T(8,128)(2,1)S(1)} %get-tuple-element.60), channel_id=1, source_target_pairs={{0,8},{1,9},{2,10},{3,11},{4,12},{5,13},{6,14},{7,15},{8,0},{9,1},... | collective-permute-start | bytes 405512 | tf_op jit(solution)/shard_map/ppermute | solution.py:307
  63.8 0.6 collective-permute-done.14
  64.4 0.1 add_convert_fusion.4
  64.5 1.6 %collective-permute-start.16 = (bf16[16,4096]{1,0:T(8,128)(2,1)S(1)}, bf16[16,4096]{1,0:T(8,128)(2,1)S(1)}, u32[]{:S(2)}, u32[]{:S(2)}) collective-permute-start(bf16[16,4096]{1,0:T(8,128)(2,1)S(1)} %get-tuple-element.65), channel_id=1, source_target_pairs={{0,4},{1,3},{2,6},{3,1},{4,0},{5,7},{6,2},{7,5},{8,12},{9,11},{10,... | collective-permute-start | bytes 393224 | tf_op jit(solution)/shard_map/ppermute | solution.py:307
  66.1 0.5 collective-permute-start.15
  66.6 1.0 %collective-permute-done.21.refs_1_.refs_3_ = bf16[16,4224]{1,0:T(8,128)(2,1)S(1)} collective-permute-done((bf16[16,4224]{1,0:T(8,128)(2,1)S(1)}, bf16[16,4224]{1,0:T(8,128)(2,1)S(1)}, u32[]{:S(2)}, u32[]{:S(2)}) %collective-permute-start.21) | collective-permute-done | bytes 135200 | tf_op jit(solution)/shard_map/ppermute | solution.py:307
  67.6 3.8 %collective-permute-start.22 = (bf16[16,4224]{1,0:T(8,128)(2,1)S(1)}, bf16[16,4224]{1,0:T(8,128)(2,1)S(1)}, u32[]{:S(2)}, u32[]{:S(2)}) collective-permute-start(bf16[16,4224]{1,0:T(8,128)(2,1)S(1)} %get-tuple-element.62), channel_id=1, source_target_pairs={{0,16},{1,17},{2,18},{3,19},{4,20},{5,21},{6,22},{7,23},{8,24},{9,... | collective-permute-start | bytes 405512 | tf_op jit(solution)/shard_map/ppermute | solution.py:307
  71.5 0.1 add_convert_fusion.1
  71.5 1.4 %collective-permute-start.17 = (bf16[16,4096]{1,0:T(8,128)(2,1)S(1)}, bf16[16,4096]{1,0:T(8,128)(2,1)S(1)}, u32[]{:S(2)}, u32[]{:S(2)}) collective-permute-start(bf16[16,4096]{1,0:T(8,128)(2,1)S(1)} %add_convert_fusion.1), channel_id=1, source_target_pairs={{0,2},{1,5},{2,0},{3,7},{4,6},{5,1},{6,4},{7,3},{8,10},{9,13},{10,... | collective-permute-start | bytes 393224 | tf_op jit(solution)/shard_map/ppermute | solution.py:307
  72.9 4.2 %collective-permute-done.22 = bf16[16,4224]{1,0:T(8,128)(2,1)S(1)} collective-permute-done((bf16[16,4224]{1,0:T(8,128)(2,1)S(1)}, bf16[16,4224]{1,0:T(8,128)(2,1)S(1)}, u32[]{:S(2)}, u32[]{:S(2)}) %collective-permute-start.22) | collective-permute-done | bytes 135200 | tf_op jit(solution)/shard_map/ppermute | solution.py:307
  77.1 0.1 collective-permute-start.23
  77.2 0.0 collective-permute-done.15
  77.2 0.8 add_convert_fusion
  78.0 0.3 collective-permute-done.23
  78.3 0.5 bitcast_divide_fusion
  (35 shorter events, 0.2 us)
Async XLA Ops:
  1.6 10.6 %collective-permute-start = (bf16[16,4224]{1,0:T(8,128)(2,1)S(1)}, bf16[16,4224]{1,0:T(8,128)(2,1)S(1)}, u32[]{:S(2)}, u32[]{:S(2)}) collective-permute-start(bf16[16,4224]{1,0:T(8,128)(2,1)S(1)} %shard_map.86.refs_0_.own_ref), channel_id=1, source_target_pairs={{0,16},{1,17},{2,18},{3,19},{4,20},{5,21},{6,22},{7,23},{8,24},{9,... | collective-permute-start | bytes 405512 | tf_op jit(solution)/shard_map/ppermute | solution.py:307
  5.7 7.2 %collective-permute-start.2 = (bf16[16,4224]{1,0:T(8,128)(2,1)S(1)}, bf16[16,4224]{1,0:T(8,128)(2,1)S(1)}, u32[]{:S(2)}, u32[]{:S(2)}) collective-permute-start(bf16[16,4224]{1,0:T(8,128)(2,1)S(1)} %shard_map.86.refs_0_.own_ref), channel_id=1, source_target_pairs={{0,4},{1,3},{2,6},{3,1},{4,0},{5,7},{6,2},{7,5},{8,12},{9,11},{10,... | collective-permute-start | bytes 405512 | tf_op jit(solution)/shard_map/ppermute | solution.py:307
  7.2 5.7 %collective-permute-start.1 = (bf16[16,4224]{1,0:T(8,128)(2,1)S(1)}, bf16[16,4224]{1,0:T(8,128)(2,1)S(1)}, u32[]{:S(2)}, u32[]{:S(2)}) collective-permute-start(bf16[16,4224]{1,0:T(8,128)(2,1)S(1)} %shard_map.86.refs_0_.own_ref), channel_id=1, source_target_pairs={{0,2},{1,5},{2,0},{3,7},{4,6},{5,1},{6,4},{7,3},{8,10},{9,13},{10,... | collective-permute-start | bytes 405512 | tf_op jit(solution)/shard_map/ppermute | solution.py:307
  12.2 5.8 %collective-permute-start.3 = (bf16[16,4224]{1,0:T(8,128)(2,1)S(1)}, bf16[16,4224]{1,0:T(8,128)(2,1)S(1)}, u32[]{:S(2)}, u32[]{:S(2)}) collective-permute-start(bf16[16,4224]{1,0:T(8,128)(2,1)S(1)} %collective-permute-done.refs_0_), channel_id=1, source_target_pairs={{0,8},{1,9},{2,10},{3,11},{4,12},{5,13},{6,14},{7,15},{8,0},{9,1},... | collective-permute-start | bytes 405512 | tf_op jit(solution)/shard_map/ppermute | solution.py:307
  12.9 6.7 %collective-permute-start.9 = (bf16[16,4224]{1,0:T(8,128)(2,1)S(1)}, bf16[16,4224]{1,0:T(8,128)(2,1)S(1)}, u32[]{:S(2)}, u32[]{:S(2)}) collective-permute-start(bf16[16,4224]{1,0:T(8,128)(2,1)S(1)} %shard_map.87.refs_5_), channel_id=1, source_target_pairs={{0,2},{1,5},{2,0},{3,7},{4,6},{5,1},{6,4},{7,3},{8,10},{9,13},{10,... | collective-permute-start | bytes 405512 | tf_op jit(solution)/shard_map/ppermute | solution.py:307
  14.5 8.0 %collective-permute-start.6 = (bf16[16,4224]{1,0:T(8,128)(2,1)S(1)}, bf16[16,4224]{1,0:T(8,128)(2,1)S(1)}, u32[]{:S(2)}, u32[]{:S(2)}) collective-permute-start(bf16[16,4224]{1,0:T(8,128)(2,1)S(1)} %shard_map.87.refs_5_), channel_id=1, source_target_pairs={{0,4},{1,3},{2,6},{3,1},{4,0},{5,7},{6,2},{7,5},{8,12},{9,11},{10,... | collective-permute-start | bytes 405512 | tf_op jit(solution)/shard_map/ppermute | solution.py:307
  16.0 6.5 %collective-permute-start.7 = (bf16[16,4224]{1,0:T(8,128)(2,1)S(1)}, bf16[16,4224]{1,0:T(8,128)(2,1)S(1)}, u32[]{:S(2)}, u32[]{:S(2)}) collective-permute-start(bf16[16,4224]{1,0:T(8,128)(2,1)S(1)} %collective-permute-done.1.refs_1_), channel_id=1, source_target_pairs={{0,4},{1,3},{2,6},{3,1},{4,0},{5,7},{6,2},{7,5},{8,12},{9,11},{10,... | collective-permute-start | bytes 405512 | tf_op jit(solution)/shard_map/ppermute | solution.py:307
  16.5 10.9 %collective-permute-start.8 = (bf16[48,4224]{1,0:T(8,128)(2,1)S(1)}, bf16[48,4224]{1,0:T(8,128)(2,1)S(1)}, u32[]{:S(2)}, u32[]{:S(2)}) collective-permute-start(bf16[48,4224]{1,0:T(8,128)(2,1)S(1)} %shard_map.89), channel_id=1, source_target_pairs={{0,8},{1,9},{2,10},{3,11},{4,12},{5,13},{6,14},{7,15},{8,0},{9,1},... | collective-permute-start | bytes 1216520 | tf_op jit(solution)/shard_map/ppermute | solution.py:307
  17.9 13.3 %slice-start = ((s8[14680064]{0:T(1024)(128)(4,1)}), s8[4194304]{0:T(1024)(128)(4,1)S(1)}, s32[]{:S(2)}) async-start(s8[14680064]{0:T(1024)(128)(4,1)} %bitcast.6), calls=%async_computation | async-start | bytes 8388608
  17.9 13.3 %slice-start.1 = ((s8[14680064]{0:T(1024)(128)(4,1)}), s8[4194304]{0:T(1024)(128)(4,1)S(1)}, s32[]{:S(2)}) async-start(s8[14680064]{0:T(1024)(128)(4,1)} %bitcast.6), calls=%async_computation.1 | async-start | bytes 8388608
  17.9 13.3 %slice-start.4 = ((s8[14680064]{0:T(1024)(128)(4,1)}), s8[4194304]{0:T(1024)(128)(4,1)S(1)}, s32[]{:S(2)}) async-start(s8[14680064]{0:T(1024)(128)(4,1)} %bitcast.8), calls=%async_computation.4 | async-start | bytes 8388608
  18.0 13.3 %slice-start.5 = ((s8[14680064]{0:T(1024)(128)(4,1)}), s8[4194304]{0:T(1024)(128)(4,1)S(1)}, s32[]{:S(2)}) async-start(s8[14680064]{0:T(1024)(128)(4,1)} %bitcast.8), calls=%async_computation.5 | async-start | bytes 8388608
  18.0 9.4 %copy-start = (f32[4096]{0:T(1024)S(1)}, f32[4096]{0:T(1024)}, u32[]{:S(2)}) copy-start(f32[4096]{0:T(1024)} %param.9) | copy-start | bytes 49156
  18.0 13.2 %slice-start.2 = ((s8[14680064]{0:T(1024)(128)(4,1)}), s8[4194304]{0:T(1024)(128)(4,1)S(1)}, s32[]{:S(2)}) async-start(s8[14680064]{0:T(1024)(128)(4,1)} %bitcast.6), calls=%async_computation.2 | async-start | bytes 8388608
  18.0 13.2 %slice-start.3 = ((s8[14680064]{0:T(1024)(128)(4,1)}), s8[2097152]{0:T(1024)(128)(4,1)S(1)}, s32[]{:S(2)}) async-start(s8[14680064]{0:T(1024)(128)(4,1)} %bitcast.6), calls=%async_computation.3 | async-start | bytes 4194304
  18.0 13.2 %slice-start.6 = ((s8[14680064]{0:T(1024)(128)(4,1)}), s8[4194304]{0:T(1024)(128)(4,1)S(1)}, s32[]{:S(2)}) async-start(s8[14680064]{0:T(1024)(128)(4,1)} %bitcast.8), calls=%async_computation.6 | async-start | bytes 8388608
  18.0 13.2 %slice-start.7 = ((s8[14680064]{0:T(1024)(128)(4,1)}), s8[2097152]{0:T(1024)(128)(4,1)S(1)}, s32[]{:S(2)}) async-start(s8[14680064]{0:T(1024)(128)(4,1)} %bitcast.8), calls=%async_computation.7 | async-start | bytes 4194304
  18.0 5.8 %collective-permute-start.5 = (bf16[16,4224]{1,0:T(8,128)(2,1)S(1)}, bf16[16,4224]{1,0:T(8,128)(2,1)S(1)}, u32[]{:S(2)}, u32[]{:S(2)}) collective-permute-start(bf16[16,4224]{1,0:T(8,128)(2,1)S(1)} %shard_map.88.refs_8_), channel_id=1, source_target_pairs={{0,4},{1,3},{2,6},{3,1},{4,0},{5,7},{6,2},{7,5},{8,12},{9,11},{10,... | collective-permute-start | bytes 405512 | tf_op jit(solution)/shard_map/ppermute | solution.py:307
  19.6 5.0 %collective-permute-start.4 = (bf16[16,4224]{1,0:T(8,128)(2,1)S(1)}, bf16[16,4224]{1,0:T(8,128)(2,1)S(1)}, u32[]{:S(2)}, u32[]{:S(2)}) collective-permute-start(bf16[16,4224]{1,0:T(8,128)(2,1)S(1)} %shard_map.88.refs_8_), channel_id=1, source_target_pairs={{0,2},{1,5},{2,0},{3,7},{4,6},{5,1},{6,4},{7,3},{8,10},{9,13},{10,... | collective-permute-start | bytes 405512 | tf_op jit(solution)/shard_map/ppermute | solution.py:307
  24.7 6.5 %collective-permute-start.11 = (bf16[32,4224]{1,0:T(8,128)(2,1)S(1)}, bf16[32,4224]{1,0:T(8,128)(2,1)S(1)}, u32[]{:S(2)}, u32[]{:S(2)}) collective-permute-start(bf16[32,4224]{1,0:T(8,128)(2,1)S(1)} %shard_map.92), channel_id=1, source_target_pairs={{0,4},{1,3},{2,6},{3,1},{4,0},{5,7},{6,2},{7,5},{8,12},{9,11},{10,... | collective-permute-start | bytes 811016 | tf_op jit(solution)/shard_map/ppermute | solution.py:307
  26.1 5.0 %collective-permute-start.10 = (bf16[16,4224]{1,0:T(8,128)(2,1)S(1)}, bf16[16,4224]{1,0:T(8,128)(2,1)S(1)}, u32[]{:S(2)}, u32[]{:S(2)}) collective-permute-start(bf16[16,4224]{1,0:T(8,128)(2,1)S(1)} %collective-permute-done.7.refs_3_), channel_id=1, source_target_pairs={{0,8},{1,9},{2,10},{3,11},{4,12},{5,13},{6,14},{7,15},{8,0},{9,1},... | collective-permute-start | bytes 405512 | tf_op jit(solution)/shard_map/ppermute | solution.py:307
  27.4 17.3 %slice-start.8 = ((s8[14680064]{0:T(1024)(128)(4,1)}), s8[4194304]{0:T(1024)(128)(4,1)S(1)}, s32[]{:S(2)}) async-start(s8[14680064]{0:T(1024)(128)(4,1)} %bitcast.10), calls=%async_computation.8 | async-start | bytes 8388608
  31.3 13.4 %slice-start.9 = ((s8[14680064]{0:T(1024)(128)(4,1)}), s8[4194304]{0:T(1024)(128)(4,1)S(1)}, s32[]{:S(2)}) async-start(s8[14680064]{0:T(1024)(128)(4,1)} %bitcast.10), calls=%async_computation.9 | async-start | bytes 8388608
  31.3 13.4 %slice-start.10 = ((s8[14680064]{0:T(1024)(128)(4,1)}), s8[4194304]{0:T(1024)(128)(4,1)S(1)}, s32[]{:S(2)}) async-start(s8[14680064]{0:T(1024)(128)(4,1)} %bitcast.10), calls=%async_computation.10 | async-start | bytes 8388608
  31.3 13.4 %slice-start.11 = ((s8[14680064]{0:T(1024)(128)(4,1)}), s8[2097152]{0:T(1024)(128)(4,1)S(1)}, s32[]{:S(2)}) async-start(s8[14680064]{0:T(1024)(128)(4,1)} %bitcast.10), calls=%async_computation.11 | async-start | bytes 4194304
  31.3 13.4 %copy-start.1 = (f32[4096]{0:T(1024)S(1)}, f32[4096]{0:T(1024)}, u32[]{:S(2)}) copy-start(f32[4096]{0:T(1024)} %param.13) | copy-start | bytes 49156
  40.6 4.0 %collective-permute-start.12 = (bf16[2,256,1792]{2,1,0:T(8,128)(2,1)S(1)}, bf16[2,256,1792]{2,1,0:T(8,128)(2,1)S(1)}, u32[]{:S(2)}, u32[]{:S(2)}) collective-permute-start(bf16[2,256,1792]{2,1,0:T(8,128)(2,1)S(1)} %get-tuple-element.43.a), channel_id=1, source_target_pairs={{0,1},{1,0},{2,3},{3,2},{4,5},{5,4},{6,7},{7,6},{8,9},{9,8},{10,11... | collective-permute-start | bytes 5505032 | tf_op jit(solution)/shard_map/ppermute | solution.py:310
  40.7 4.0 %collective-permute-start.13 = (f32[256,128]{1,0:T(8,128)S(1)}, f32[256,128]{1,0:T(8,128)S(1)}, u32[]{:S(2)}, u32[]{:S(2)}) collective-permute-start(f32[256,128]{1,0:T(8,128)S(1)} %get-tuple-element.44.sq), channel_id=1, source_target_pairs={{0,1},{1,0},{2,3},{3,2},{4,5},{5,4},{6,7},{7,6},{8,9},{9,8},{10,11... | collective-permute-start | bytes 393224 | tf_op jit(solution)/shard_map/ppermute | solution.py:310
  49.3 6.5 %collective-permute-start.19 = (bf16[32,4224]{1,0:T(8,128)(2,1)S(1)}, bf16[32,4224]{1,0:T(8,128)(2,1)S(1)}, u32[]{:S(2)}, u32[]{:S(2)}) collective-permute-start(bf16[32,4224]{1,0:T(8,128)(2,1)S(1)} %get-tuple-element.54), channel_id=1, source_target_pairs={{0,4},{1,3},{2,6},{3,1},{4,0},{5,7},{6,2},{7,5},{8,12},{9,11},{10,... | collective-permute-start | bytes 811016 | tf_op jit(solution)/shard_map/ppermute | solution.py:307
  50.7 13.7 %collective-permute-start.14 = (bf16[64,4096]{1,0:T(8,128)(2,1)S(1)}, bf16[64,4096]{1,0:T(8,128)(2,1)S(1)}, u32[]{:S(2)}, u32[]{:S(2)}) collective-permute-start(bf16[64,4096]{1,0:T(8,128)(2,1)S(1)} %get-tuple-element.47), channel_id=1, source_target_pairs={{0,8},{1,9},{2,10},{3,11},{4,12},{5,13},{6,14},{7,15},{8,0},{9,1},... | collective-permute-start | bytes 1572872 | tf_op jit(solution)/shard_map/ppermute | solution.py:307
  52.0 7.3 %collective-permute-start.18 = (bf16[32,4096]{1,0:T(8,128)(2,1)S(1)}, bf16[32,4096]{1,0:T(8,128)(2,1)S(1)}, u32[]{:S(2)}, u32[]{:S(2)}) collective-permute-start(bf16[32,4096]{1,0:T(8,128)(2,1)S(1)} %get-tuple-element.52), channel_id=1, source_target_pairs={{0,4},{1,3},{2,6},{3,1},{4,0},{5,7},{6,2},{7,5},{8,12},{9,11},{10,... | collective-permute-start | bytes 786440 | tf_op jit(solution)/shard_map/ppermute | solution.py:307
  55.9 6.5 %collective-permute-start.20 = (bf16[32,4224]{1,0:T(8,128)(2,1)S(1)}, bf16[32,4224]{1,0:T(8,128)(2,1)S(1)}, u32[]{:S(2)}, u32[]{:S(2)}) collective-permute-start(bf16[32,4224]{1,0:T(8,128)(2,1)S(1)} %get-tuple-element.58), channel_id=1, source_target_pairs={{0,2},{1,5},{2,0},{3,7},{4,6},{5,1},{6,4},{7,3},{8,10},{9,13},{10,... | collective-permute-start | bytes 811016 | tf_op jit(solution)/shard_map/ppermute | solution.py:307
  62.5 5.1 %collective-permute-start.21 = (bf16[16,4224]{1,0:T(8,128)(2,1)S(1)}, bf16[16,4224]{1,0:T(8,128)(2,1)S(1)}, u32[]{:S(2)}, u32[]{:S(2)}) collective-permute-start(bf16[16,4224]{1,0:T(8,128)(2,1)S(1)} %get-tuple-element.60), channel_id=1, source_target_pairs={{0,8},{1,9},{2,10},{3,11},{4,12},{5,13},{6,14},{7,15},{8,0},{9,1},... | collective-permute-start | bytes 405512 | tf_op jit(solution)/shard_map/ppermute | solution.py:307
  64.5 7.0 %collective-permute-start.16 = (bf16[16,4096]{1,0:T(8,128)(2,1)S(1)}, bf16[16,4096]{1,0:T(8,128)(2,1)S(1)}, u32[]{:S(2)}, u32[]{:S(2)}) collective-permute-start(bf16[16,4096]{1,0:T(8,128)(2,1)S(1)} %get-tuple-element.65), channel_id=1, source_target_pairs={{0,4},{1,3},{2,6},{3,1},{4,0},{5,7},{6,2},{7,5},{8,12},{9,11},{10,... | collective-permute-start | bytes 393224 | tf_op jit(solution)/shard_map/ppermute | solution.py:307
  66.1 11.1 %collective-permute-start.15 = (bf16[16,4096]{1,0:T(8,128)(2,1)S(1)}, bf16[16,4096]{1,0:T(8,128)(2,1)S(1)}, u32[]{:S(2)}, u32[]{:S(2)}) collective-permute-start(bf16[16,4096]{1,0:T(8,128)(2,1)S(1)} %get-tuple-element.64), channel_id=1, source_target_pairs={{0,4},{1,3},{2,6},{3,1},{4,0},{5,7},{6,2},{7,5},{8,12},{9,11},{10,... | collective-permute-start | bytes 393224 | tf_op jit(solution)/shard_map/ppermute | solution.py:307
  67.6 9.5 %collective-permute-start.22 = (bf16[16,4224]{1,0:T(8,128)(2,1)S(1)}, bf16[16,4224]{1,0:T(8,128)(2,1)S(1)}, u32[]{:S(2)}, u32[]{:S(2)}) collective-permute-start(bf16[16,4224]{1,0:T(8,128)(2,1)S(1)} %get-tuple-element.62), channel_id=1, source_target_pairs={{0,16},{1,17},{2,18},{3,19},{4,20},{5,21},{6,22},{7,23},{8,24},{9,... | collective-permute-start | bytes 405512 | tf_op jit(solution)/shard_map/ppermute | solution.py:307
  71.5 5.7 %collective-permute-start.17 = (bf16[16,4096]{1,0:T(8,128)(2,1)S(1)}, bf16[16,4096]{1,0:T(8,128)(2,1)S(1)}, u32[]{:S(2)}, u32[]{:S(2)}) collective-permute-start(bf16[16,4096]{1,0:T(8,128)(2,1)S(1)} %add_convert_fusion.1), channel_id=1, source_target_pairs={{0,2},{1,5},{2,0},{3,7},{4,6},{5,1},{6,4},{7,3},{8,10},{9,13},{10,... | collective-permute-start | bytes 393224 | tf_op jit(solution)/shard_map/ppermute | solution.py:307
  77.1 1.2 %collective-permute-start.23 = (f32[128]{0:T(128)S(1)}, f32[128]{0:T(128)S(1)}, u32[]{:S(2)}, u32[]{:S(2)}) collective-permute-start(f32[128]{0:T(128)S(1)} %bitcast_add_fusion), channel_id=1, source_target_pairs={{0,1},{1,0},{2,3},{3,2},{4,5},{5,4},{6,7},{7,6},{8,9},{9,8},{10,11... | collective-permute-start | bytes 1544 | tf_op jit(solution)/shard_map/ppermute | solution.py:310

commit v5 on v4

--- a/solution.py
+++ b/solution.py
@@ -323,10 +323,10 @@
         across = swap(join((own, own_a, own_b), 0), 4)
         z3 = join((z3,), 10**10)
         z3_a, z3_b = swap(z3, 1, 2), swap(z3, 2, 1)
-        z2_a = join((z2_a,), 10**10)
-        z3_a, z3_b, z2_b, own_c = after((z3_a, z3_b, z2_b, own_c))
+        z2_a, own_c = after((join((z2_a,), 10**10), own_c))
         across_c = swap(own_c, 4)
-        far_c = swap(join((z2_a, z3_a), 0), 2, 1)
+        z2_c = swap(z2_a, 2, 1)
+        z3_c = swap(z3_a, 2, 1)
 
         q, half = 2 * rows, 8 * rows
         gain, score = norm_gain[None, :], score_vec[None, :]
@@ -335,8 +335,8 @@
         places += [(half + i * q,) for i in range(3)] + [(half + i * q + rows,) for i in range(3)]
         early = early_rows(pieces, places, gain, 2 * half, 10**9)
         early_places = [(0, half - rows), (half, half + 3 * q)]
-        late_places = [(half - rows,), (half + 3 * q,)]
-        part, squares, owner = gate_up(early, early_places, [across_c, far_c], late_places, gain, w_gate, w_up)
+        late_places = [(half - rows,), (half + 3 * q,), (half + 3 * q + rows,)]
+        part, squares, owner = gate_up(early, early_places, [across_c, z2_c, z3_c], late_places, gain, w_gate, w_up)
         other, other_squares = tp_swap(part), tp_swap(squares)
         *near, across, f0, f1, f2, f3, totals = down_rows(part, other, squares, other_squares, owner, w_down, score, own)
         width = preview.shape[1]

time: 79 us -> 77.9 us (0.986)
  starting transfers between devices: 32.4 us -> 30.8 us
    ppermute x21 -> x22, starting transfers between devices: 31.8 us -> 30.1 us  [swap(): return lax.ppermute(v, BOTH, pairs)]
    ppermute x21 -> x22, waiting for transfers between devices: 23.8 us -> 24.7 us  [swap(): return lax.ppermute(v, BOTH, pairs)]
    pallas_call x12 -> x11, Pallas kernels: 15.4 us -> 15.4 us  [call(): pl.pallas_call(body, out_shape=out_shape, in_specs=[VMEM] * len(args), ou...]
  transfers between devices with their start and end apart: 24 -> 25, of which waited for: 14 -> 14; matrix products, arithmetic and copies ran while one was open for 1% -> 1% of each run, Pallas kernels for 2% -> 2%
where the time goes in v5:
time: 77.9 us; the launch traced here: 77.7 us
  starting transfers between devices  30.8 us (40%)
  waiting for transfers between devices  28.2 us (36%)
  Pallas kernels  16.3 us (21%)
  other arithmetic  1.43 us (2%)
  between operations  0.94 us (1%)
    ppermute x22, starting transfers between devices, swap(): return lax.ppermute(v, BOTH, pairs)  30.1 us
    ppermute x22, waiting for transfers between devices, swap(): return lax.ppermute(v, BOTH, pairs)  24.7 us
    pallas_call x11, Pallas kernels, call(): pl.pallas_call(body, out_shape=out_shape, in_specs=[VMEM] * len(args), ou...  15.4 us
    ppermute x3, waiting for transfers between devices, tp_swap(): return lax.ppermute(v, 'tp', [(0, 1), (1, 0)])  3.54 us
  transfers between devices with their start and end apart: 25, of which 14 were waited for; matrix products, arithmetic and copies ran while one was open for 1% of the time, Pallas kernels for 2%

profile of v5, /device:TPU:0, one launch (start us, length us, event | category | flops | bytes accessed | tf_op | source)
XLA Modules:
  0.0 77.7 jit_solution(2347174271181363622)
XLA Ops:
  0.6 0.9 %shard_map.86.refs_0_.own_ref = bf16[16,4224]{1,0:T(8,128)(2,1)S(1)} custom-call(bf16[16,4096]{1,0:T(8,128)(2,1)} %rows_ref.1, s32[16]{0:T(128)} %owner_ref.1), custom_call_target="tpu_custom_call" | custom-call | flops 10000000000 | bytes 262144 | tf_op jit(solution)/shard_map/pallas_call | solution.py:151
  1.6 4.1 %collective-permute-start = (bf16[16,4224]{1,0:T(8,128)(2,1)S(1)}, bf16[16,4224]{1,0:T(8,128)(2,1)S(1)}, u32[]{:S(2)}, u32[]{:S(2)}) collective-permute-start(bf16[16,4224]{1,0:T(8,128)(2,1)S(1)} %shard_map.86.refs_0_.own_ref), channel_id=1, source_target_pairs={{0,16},{1,17},{2,18},{3,19},{4,20},{5,21},{6,22},{7,23},{8,24},{9,... | collective-permute-start | bytes 405512 | tf_op jit(solution)/shard_map/ppermute | solution.py:307
  5.7 1.5 %collective-permute-start.2 = (bf16[16,4224]{1,0:T(8,128)(2,1)S(1)}, bf16[16,4224]{1,0:T(8,128)(2,1)S(1)}, u32[]{:S(2)}, u32[]{:S(2)}) collective-permute-start(bf16[16,4224]{1,0:T(8,128)(2,1)S(1)} %shard_map.86.refs_0_.own_ref), channel_id=1, source_target_pairs={{0,4},{1,3},{2,6},{3,1},{4,0},{5,7},{6,2},{7,5},{8,12},{9,11},{10,... | collective-permute-start | bytes 405512 | tf_op jit(solution)/shard_map/ppermute | solution.py:307
  7.2 1.5 %collective-permute-start.1 = (bf16[16,4224]{1,0:T(8,128)(2,1)S(1)}, bf16[16,4224]{1,0:T(8,128)(2,1)S(1)}, u32[]{:S(2)}, u32[]{:S(2)}) collective-permute-start(bf16[16,4224]{1,0:T(8,128)(2,1)S(1)} %shard_map.86.refs_0_.own_ref), channel_id=1, source_target_pairs={{0,2},{1,5},{2,0},{3,7},{4,6},{5,1},{6,4},{7,3},{8,10},{9,13},{10,... | collective-permute-start | bytes 405512 | tf_op jit(solution)/shard_map/ppermute | solution.py:307
  8.7 3.5 %collective-permute-done.refs_0_ = bf16[16,4224]{1,0:T(8,128)(2,1)S(1)} collective-permute-done((bf16[16,4224]{1,0:T(8,128)(2,1)S(1)}, bf16[16,4224]{1,0:T(8,128)(2,1)S(1)}, u32[]{:S(2)}, u32[]{:S(2)}) %collective-permute-start) | collective-permute-done | bytes 135200 | tf_op jit(solution)/shard_map/ppermute | solution.py:307
  12.2 0.7 collective-permute-start.7
  12.9 0.0 collective-permute-done.2.refs_2_
  12.9 0.0 collective-permute-done.1.refs_1_
  12.9 1.6 %collective-permute-start.6 = (bf16[16,4224]{1,0:T(8,128)(2,1)S(1)}, bf16[16,4224]{1,0:T(8,128)(2,1)S(1)}, u32[]{:S(2)}, u32[]{:S(2)}) collective-permute-start(bf16[16,4224]{1,0:T(8,128)(2,1)S(1)} %shard_map.87.refs_5_), channel_id=1, source_target_pairs={{0,4},{1,3},{2,6},{3,1},{4,0},{5,7},{6,2},{7,5},{8,12},{9,11},{10,... | collective-permute-start | bytes 405512 | tf_op jit(solution)/shard_map/ppermute | solution.py:307
  14.5 1.5 %collective-permute-start.3 = (bf16[16,4224]{1,0:T(8,128)(2,1)S(1)}, bf16[16,4224]{1,0:T(8,128)(2,1)S(1)}, u32[]{:S(2)}, u32[]{:S(2)}) collective-permute-start(bf16[16,4224]{1,0:T(8,128)(2,1)S(1)} %shard_map.87.refs_5_), channel_id=1, source_target_pairs={{0,2},{1,5},{2,0},{3,7},{4,6},{5,1},{6,4},{7,3},{8,10},{9,13},{10,... | collective-permute-start | bytes 405512 | tf_op jit(solution)/shard_map/ppermute | solution.py:307
  16.0 0.5 collective-permute-start.4
  16.5 1.4 %collective-permute-start.5 = (bf16[48,4224]{1,0:T(8,128)(2,1)S(1)}, bf16[48,4224]{1,0:T(8,128)(2,1)S(1)}, u32[]{:S(2)}, u32[]{:S(2)}) collective-permute-start(bf16[48,4224]{1,0:T(8,128)(2,1)S(1)} %shard_map.89), channel_id=1, source_target_pairs={{0,8},{1,9},{2,10},{3,11},{4,12},{5,13},{6,14},{7,15},{8,0},{9,1},... | collective-permute-start | bytes 1216520 | tf_op jit(solution)/shard_map/ppermute | solution.py:307
  17.9 0.0 collective-permute-done.7.refs_0_
  18.0 0.0 slice-start.5
  18.0 0.0 copy-start
  18.0 0.0 slice-start.2
  18.0 0.0 slice-start.3
  18.0 0.0 slice-start.6
  18.0 0.0 slice-start.7
  18.0 1.6 %collective-permute-start.9 = (bf16[16,4224]{1,0:T(8,128)(2,1)S(1)}, bf16[16,4224]{1,0:T(8,128)(2,1)S(1)}, u32[]{:S(2)}, u32[]{:S(2)}) collective-permute-start(bf16[16,4224]{1,0:T(8,128)(2,1)S(1)} %shard_map.90.refs_8_), channel_id=1, source_target_pairs={{0,4},{1,3},{2,6},{3,1},{4,0},{5,7},{6,2},{7,5},{8,12},{9,11},{10,... | collective-permute-start | bytes 405512 | tf_op jit(solution)/shard_map/ppermute | solution.py:307
  19.6 1.3 %collective-permute-done.3.refs_0_ = bf16[16,4224]{1,0:T(8,128)(2,1)S(1)} collective-permute-done((bf16[16,4224]{1,0:T(8,128)(2,1)S(1)}, bf16[16,4224]{1,0:T(8,128)(2,1)S(1)}, u32[]{:S(2)}, u32[]{:S(2)}) %collective-permute-start.3) | collective-permute-done | bytes 135200 | tf_op jit(solution)/shard_map/ppermute | solution.py:307
  20.9 1.5 %collective-permute-start.8 = (bf16[16,4224]{1,0:T(8,128)(2,1)S(1)}, bf16[16,4224]{1,0:T(8,128)(2,1)S(1)}, u32[]{:S(2)}, u32[]{:S(2)}) collective-permute-start(bf16[16,4224]{1,0:T(8,128)(2,1)S(1)} %shard_map.90.refs_8_), channel_id=1, source_target_pairs={{0,2},{1,5},{2,0},{3,7},{4,6},{5,1},{6,4},{7,3},{8,10},{9,13},{10,... | collective-permute-start | bytes 405512 | tf_op jit(solution)/shard_map/ppermute | solution.py:307
  22.5 0.0 collective-permute-done.4.refs_3_
  22.5 0.7 collective-permute-start.10
  23.2 3.2 %collective-permute-done.8.refs_9_ = bf16[16,4224]{1,0:T(8,128)(2,1)S(1)} collective-permute-done((bf16[16,4224]{1,0:T(8,128)(2,1)S(1)}, bf16[16,4224]{1,0:T(8,128)(2,1)S(1)}, u32[]{:S(2)}, u32[]{:S(2)}) %collective-permute-start.8) | collective-permute-done | bytes 135200 | tf_op jit(solution)/shard_map/ppermute | solution.py:307
  26.4 0.5 collective-permute-start.12
  26.9 0.0 collective-permute-done.9.refs_10_
  26.9 1.3 %collective-permute-done.5.refs_4_ = bf16[48,4224]{1,0:T(8,128)(2,1)S(1)} collective-permute-done((bf16[48,4224]{1,0:T(8,128)(2,1)S(1)}, bf16[48,4224]{1,0:T(8,128)(2,1)S(1)}, u32[]{:S(2)}, u32[]{:S(2)}) %collective-permute-start.5) | collective-permute-done | bytes 405536 | tf_op jit(solution)/shard_map/ppermute | solution.py:307
  28.2 0.7 shard_map.91
  28.9 0.8 %collective-permute-done.10.refs_0_ = bf16[16,4224]{1,0:T(8,128)(2,1)S(1)} collective-permute-done((bf16[16,4224]{1,0:T(8,128)(2,1)S(1)}, bf16[16,4224]{1,0:T(8,128)(2,1)S(1)}, u32[]{:S(2)}, u32[]{:S(2)}) %collective-permute-start.10) | collective-permute-done | bytes 135200 | tf_op jit(solution)/shard_map/ppermute | solution.py:307
  29.7 1.7 %collective-permute-done.12.refs_2_ = bf16[16,4224]{1,0:T(8,128)(2,1)S(1)} collective-permute-done((bf16[16,4224]{1,0:T(8,128)(2,1)S(1)}, bf16[16,4224]{1,0:T(8,128)(2,1)S(1)}, u32[]{:S(2)}, u32[]{:S(2)}) %collective-permute-start.12) | collective-permute-done | bytes 135200 | tf_op jit(solution)/shard_map/ppermute | solution.py:307
  31.5 0.0 slice-start.9
  31.5 0.0 slice-start.11
  31.5 0.0 copy-start.1
  31.5 9.3 %shard_map.92 = (bf16[2,256,1792]{2,1,0:T(8,128)(2,1)S(1)}, f32[256,128]{1,0:T(8,128)S(1)}, f32[256,128]{1,0:T(8,128)S(1)}) custom-call(bf16[256,4096]{1,0:T(8,128)(2,1)S(1)} %get-tuple-element.36.x_in, f32[256,128]{1,0:T(8,128)S(1)} %get-tuple-element.37.squares_in, f32[256,128]{1,0:T(8,128)S(1)} %get-tuple-element.38.owner_in, ...), custom_call_target="tpu_custom_call" | custom-call | flops 7516192768 | bytes 32141312 | tf_op jit(solution)/shard_map/pallas_call | solution.py:129
  40.9 0.1 collective-permute-start.13
  40.9 0.5 collective-permute-start.14
  41.4 3.5 %collective-permute-done.14.other_sq = f32[256,128]{1,0:T(8,128)S(1)} collective-permute-done((f32[256,128]{1,0:T(8,128)S(1)}, f32[256,128]{1,0:T(8,128)S(1)}, u32[]{:S(2)}, u32[]{:S(2)}) %collective-permute-start.14) | collective-permute-done | bytes 131104 | tf_op jit(solution)/shard_map/ppermute | solution.py:310
  45.0 4.6 %shard_map.93 = (bf16[16,4096]{1,0:T(8,128)(2,1)S(1)}, bf16[16,4096]{1,0:T(8,128)(2,1)S(1)}, bf16[16,4096]{1,0:T(8,128)(2,1)S(1)}, bf16[16,4096]{1,0:T(8,128)(2,...) custom-call(bf16[2,256,1792]{2,1,0:T(8,128)(2,1)S(1)} %get-tuple-ele, ...), custom_call_target="tpu_custom_call" | custom-call | flops 3758096384 | bytes 18894848 | tf_op jit(solution)/shard_map/pallas_call | solution.py:129
  49.5 0.6 collective-permute-start.20
  50.1 1.3 %collective-permute-start.15 = (bf16[64,4096]{1,0:T(8,128)(2,1)S(1)}, bf16[64,4096]{1,0:T(8,128)(2,1)S(1)}, u32[]{:S(2)}, u32[]{:S(2)}) collective-permute-start(bf16[64,4096]{1,0:T(8,128)(2,1)S(1)} %get-tuple-element.43), channel_id=1, source_target_pairs={{0,8},{1,9},{2,10},{3,11},{4,12},{5,13},{6,14},{7,15},{8,0},{9,1},... | collective-permute-start | bytes 1572872 | tf_op jit(solution)/shard_map/ppermute | solution.py:307
  51.3 1.9 %collective-permute-start.19 = (bf16[32,4096]{1,0:T(8,128)(2,1)S(1)}, bf16[32,4096]{1,0:T(8,128)(2,1)S(1)}, u32[]{:S(2)}, u32[]{:S(2)}) collective-permute-start(bf16[32,4096]{1,0:T(8,128)(2,1)S(1)} %get-tuple-element.48), channel_id=1, source_target_pairs={{0,4},{1,3},{2,6},{3,1},{4,0},{5,7},{6,2},{7,5},{8,12},{9,11},{10,... | collective-permute-start | bytes 786440 | tf_op jit(solution)/shard_map/ppermute | solution.py:307
  53.3 2.7 %collective-permute-done.20.refs_1_.refs_3_ = bf16[32,4224]{1,0:T(8,128)(2,1)S(1)} collective-permute-done((bf16[32,4224]{1,0:T(8,128)(2,1)S(1)}, bf16[32,4224]{1,0:T(8,128)(2,1)S(1)}, u32[]{:S(2)}, u32[]{:S(2)}) %collective-permute-start.20) | collective-permute-done | bytes 270368 | tf_op jit(solution)/shard_map/ppermute | solution.py:307
  56.0 0.1 shard_map.94
  56.1 1.1 %collective-permute-start.21 = (bf16[32,4224]{1,0:T(8,128)(2,1)S(1)}, bf16[32,4224]{1,0:T(8,128)(2,1)S(1)}, u32[]{:S(2)}, u32[]{:S(2)}) collective-permute-start(bf16[32,4224]{1,0:T(8,128)(2,1)S(1)} %get-tuple-element.54), channel_id=1, source_target_pairs={{0,2},{1,5},{2,0},{3,7},{4,6},{5,1},{6,4},{7,3},{8,10},{9,13},{10,... | collective-permute-start | bytes 811016 | tf_op jit(solution)/shard_map/ppermute | solution.py:307
  57.2 2.3 %collective-permute-done.19.refs_1_ = bf16[32,4096]{1,0:T(8,128)(2,1)S(1)} collective-permute-done((bf16[32,4096]{1,0:T(8,128)(2,1)S(1)}, bf16[32,4096]{1,0:T(8,128)(2,1)S(1)}, u32[]{:S(2)}, u32[]{:S(2)}) %collective-permute-start.19) | collective-permute-done | bytes 262176 | tf_op jit(solution)/shard_map/ppermute | solution.py:307
  59.6 0.6 shard_map.95
  60.2 2.4 %collective-permute-done.21.refs_1_.refs_3_ = bf16[32,4224]{1,0:T(8,128)(2,1)S(1)} collective-permute-done((bf16[32,4224]{1,0:T(8,128)(2,1)S(1)}, bf16[32,4224]{1,0:T(8,128)(2,1)S(1)}, u32[]{:S(2)}, u32[]{:S(2)}) %collective-permute-start.21) | collective-permute-done | bytes 270368 | tf_op jit(solution)/shard_map/ppermute | solution.py:307
  62.6 0.1 shard_map.96
  62.7 1.8 %collective-permute-start.22 = (bf16[16,4224]{1,0:T(8,128)(2,1)S(1)}, bf16[16,4224]{1,0:T(8,128)(2,1)S(1)}, u32[]{:S(2)}, u32[]{:S(2)}) collective-permute-start(bf16[16,4224]{1,0:T(8,128)(2,1)S(1)} %get-tuple-element.56), channel_id=1, source_target_pairs={{0,8},{1,9},{2,10},{3,11},{4,12},{5,13},{6,14},{7,15},{8,0},{9,1},... | collective-permute-start | bytes 405512 | tf_op jit(solution)/shard_map/ppermute | solution.py:307
  64.5 0.0 collective-permute-done.15
  64.5 0.1 add_convert_fusion.4
  64.5 0.5 collective-permute-start.17
  65.0 1.6 %collective-permute-start.16 = (bf16[16,4096]{1,0:T(8,128)(2,1)S(1)}, bf16[16,4096]{1,0:T(8,128)(2,1)S(1)}, u32[]{:S(2)}, u32[]{:S(2)}) collective-permute-start(bf16[16,4096]{1,0:T(8,128)(2,1)S(1)} %get-tuple-element.60), channel_id=1, source_target_pairs={{0,4},{1,3},{2,6},{3,1},{4,0},{5,7},{6,2},{7,5},{8,12},{9,11},{10,... | collective-permute-start | bytes 393224 | tf_op jit(solution)/shard_map/ppermute | solution.py:307
  66.6 1.1 %collective-permute-done.22.refs_1_.refs_3_ = bf16[16,4224]{1,0:T(8,128)(2,1)S(1)} collective-permute-done((bf16[16,4224]{1,0:T(8,128)(2,1)S(1)}, bf16[16,4224]{1,0:T(8,128)(2,1)S(1)}, u32[]{:S(2)}, u32[]{:S(2)}) %collective-permute-start.22) | collective-permute-done | bytes 135200 | tf_op jit(solution)/shard_map/ppermute | solution.py:307
  67.8 3.4 %collective-permute-start.23 = (bf16[16,4224]{1,0:T(8,128)(2,1)S(1)}, bf16[16,4224]{1,0:T(8,128)(2,1)S(1)}, u32[]{:S(2)}, u32[]{:S(2)}) collective-permute-start(bf16[16,4224]{1,0:T(8,128)(2,1)S(1)} %get-tuple-element.58), channel_id=1, source_target_pairs={{0,16},{1,17},{2,18},{3,19},{4,20},{5,21},{6,22},{7,23},{8,24},{9,... | collective-permute-start | bytes 405512 | tf_op jit(solution)/shard_map/ppermute | solution.py:307
  71.3 0.1 add_convert_fusion.1
  71.3 0.7 collective-permute-start.18
  72.0 4.0 %collective-permute-done.23 = bf16[16,4224]{1,0:T(8,128)(2,1)S(1)} collective-permute-done((bf16[16,4224]{1,0:T(8,128)(2,1)S(1)}, bf16[16,4224]{1,0:T(8,128)(2,1)S(1)}, u32[]{:S(2)}, u32[]{:S(2)}) %collective-permute-start.23) | collective-permute-done | bytes 135200 | tf_op jit(solution)/shard_map/ppermute | solution.py:307
  76.0 0.1 collective-permute-start.24
  76.1 0.3 collective-permute-done.18
  76.4 0.8 add_convert_fusion
  77.1 0.1 collective-permute-done.24
  77.2 0.5 bitcast_divide_fusion
  (36 shorter events, 0.2 us)
Async XLA Ops:
  1.6 10.6 %collective-permute-start = (bf16[16,4224]{1,0:T(8,128)(2,1)S(1)}, bf16[16,4224]{1,0:T(8,128)(2,1)S(1)}, u32[]{:S(2)}, u32[]{:S(2)}) collective-permute-start(bf16[16,4224]{1,0:T(8,128)(2,1)S(1)} %shard_map.86.refs_0_.own_ref), channel_id=1, source_target_pairs={{0,16},{1,17},{2,18},{3,19},{4,20},{5,21},{6,22},{7,23},{8,24},{9,... | collective-permute-start | bytes 405512 | tf_op jit(solution)/shard_map/ppermute | solution.py:307
  5.7 7.2 %collective-permute-start.2 = (bf16[16,4224]{1,0:T(8,128)(2,1)S(1)}, bf16[16,4224]{1,0:T(8,128)(2,1)S(1)}, u32[]{:S(2)}, u32[]{:S(2)}) collective-permute-start(bf16[16,4224]{1,0:T(8,128)(2,1)S(1)} %shard_map.86.refs_0_.own_ref), channel_id=1, source_target_pairs={{0,4},{1,3},{2,6},{3,1},{4,0},{5,7},{6,2},{7,5},{8,12},{9,11},{10,... | collective-permute-start | bytes 405512 | tf_op jit(solution)/shard_map/ppermute | solution.py:307
  7.2 5.7 %collective-permute-start.1 = (bf16[16,4224]{1,0:T(8,128)(2,1)S(1)}, bf16[16,4224]{1,0:T(8,128)(2,1)S(1)}, u32[]{:S(2)}, u32[]{:S(2)}) collective-permute-start(bf16[16,4224]{1,0:T(8,128)(2,1)S(1)} %shard_map.86.refs_0_.own_ref), channel_id=1, source_target_pairs={{0,2},{1,5},{2,0},{3,7},{4,6},{5,1},{6,4},{7,3},{8,10},{9,13},{10,... | collective-permute-start | bytes 405512 | tf_op jit(solution)/shard_map/ppermute | solution.py:307
  12.2 5.8 %collective-permute-start.7 = (bf16[16,4224]{1,0:T(8,128)(2,1)S(1)}, bf16[16,4224]{1,0:T(8,128)(2,1)S(1)}, u32[]{:S(2)}, u32[]{:S(2)}) collective-permute-start(bf16[16,4224]{1,0:T(8,128)(2,1)S(1)} %collective-permute-done.refs_0_), channel_id=1, source_target_pairs={{0,8},{1,9},{2,10},{3,11},{4,12},{5,13},{6,14},{7,15},{8,0},{9,1},... | collective-permute-start | bytes 405512 | tf_op jit(solution)/shard_map/ppermute | solution.py:307
  12.9 10.3 %collective-permute-start.6 = (bf16[16,4224]{1,0:T(8,128)(2,1)S(1)}, bf16[16,4224]{1,0:T(8,128)(2,1)S(1)}, u32[]{:S(2)}, u32[]{:S(2)}) collective-permute-start(bf16[16,4224]{1,0:T(8,128)(2,1)S(1)} %shard_map.87.refs_5_), channel_id=1, source_target_pairs={{0,4},{1,3},{2,6},{3,1},{4,0},{5,7},{6,2},{7,5},{8,12},{9,11},{10,... | collective-permute-start | bytes 405512 | tf_op jit(solution)/shard_map/ppermute | solution.py:307
  14.5 6.5 %collective-permute-start.3 = (bf16[16,4224]{1,0:T(8,128)(2,1)S(1)}, bf16[16,4224]{1,0:T(8,128)(2,1)S(1)}, u32[]{:S(2)}, u32[]{:S(2)}) collective-permute-start(bf16[16,4224]{1,0:T(8,128)(2,1)S(1)} %shard_map.87.refs_5_), channel_id=1, source_target_pairs={{0,2},{1,5},{2,0},{3,7},{4,6},{5,1},{6,4},{7,3},{8,10},{9,13},{10,... | collective-permute-start | bytes 405512 | tf_op jit(solution)/shard_map/ppermute | solution.py:307
  16.0 6.5 %collective-permute-start.4 = (bf16[16,4224]{1,0:T(8,128)(2,1)S(1)}, bf16[16,4224]{1,0:T(8,128)(2,1)S(1)}, u32[]{:S(2)}, u32[]{:S(2)}) collective-permute-start(bf16[16,4224]{1,0:T(8,128)(2,1)S(1)} %collective-permute-done.1.refs_1_), channel_id=1, source_target_pairs={{0,4},{1,3},{2,6},{3,1},{4,0},{5,7},{6,2},{7,5},{8,12},{9,11},{10,... | collective-permute-start | bytes 405512 | tf_op jit(solution)/shard_map/ppermute | solution.py:307
  16.5 11.7 %collective-permute-start.5 = (bf16[48,4224]{1,0:T(8,128)(2,1)S(1)}, bf16[48,4224]{1,0:T(8,128)(2,1)S(1)}, u32[]{:S(2)}, u32[]{:S(2)}) collective-permute-start(bf16[48,4224]{1,0:T(8,128)(2,1)S(1)} %shard_map.89), channel_id=1, source_target_pairs={{0,8},{1,9},{2,10},{3,11},{4,12},{5,13},{6,14},{7,15},{8,0},{9,1},... | collective-permute-start | bytes 1216520 | tf_op jit(solution)/shard_map/ppermute | solution.py:307
  17.9 13.5 %slice-start = ((s8[14680064]{0:T(1024)(128)(4,1)}), s8[4194304]{0:T(1024)(128)(4,1)S(1)}, s32[]{:S(2)}) async-start(s8[14680064]{0:T(1024)(128)(4,1)} %bitcast.6), calls=%async_computation | async-start | bytes 8388608
  17.9 13.5 %slice-start.1 = ((s8[14680064]{0:T(1024)(128)(4,1)}), s8[4194304]{0:T(1024)(128)(4,1)S(1)}, s32[]{:S(2)}) async-start(s8[14680064]{0:T(1024)(128)(4,1)} %bitcast.6), calls=%async_computation.1 | async-start | bytes 8388608
  17.9 13.5 %slice-start.4 = ((s8[14680064]{0:T(1024)(128)(4,1)}), s8[4194304]{0:T(1024)(128)(4,1)S(1)}, s32[]{:S(2)}) async-start(s8[14680064]{0:T(1024)(128)(4,1)} %bitcast.8), calls=%async_computation.4 | async-start | bytes 8388608
  18.0 13.5 %slice-start.5 = ((s8[14680064]{0:T(1024)(128)(4,1)}), s8[4194304]{0:T(1024)(128)(4,1)S(1)}, s32[]{:S(2)}) async-start(s8[14680064]{0:T(1024)(128)(4,1)} %bitcast.8), calls=%async_computation.5 | async-start | bytes 8388608
  18.0 10.3 %copy-start = (f32[4096]{0:T(1024)S(1)}, f32[4096]{0:T(1024)}, u32[]{:S(2)}) copy-start(f32[4096]{0:T(1024)} %param.9) | copy-start | bytes 49156
  18.0 13.4 %slice-start.2 = ((s8[14680064]{0:T(1024)(128)(4,1)}), s8[4194304]{0:T(1024)(128)(4,1)S(1)}, s32[]{:S(2)}) async-start(s8[14680064]{0:T(1024)(128)(4,1)} %bitcast.6), calls=%async_computation.2 | async-start | bytes 8388608
  18.0 13.4 %slice-start.3 = ((s8[14680064]{0:T(1024)(128)(4,1)}), s8[2097152]{0:T(1024)(128)(4,1)S(1)}, s32[]{:S(2)}) async-start(s8[14680064]{0:T(1024)(128)(4,1)} %bitcast.6), calls=%async_computation.3 | async-start | bytes 4194304
  18.0 13.4 %slice-start.6 = ((s8[14680064]{0:T(1024)(128)(4,1)}), s8[4194304]{0:T(1024)(128)(4,1)S(1)}, s32[]{:S(2)}) async-start(s8[14680064]{0:T(1024)(128)(4,1)} %bitcast.8), calls=%async_computation.6 | async-start | bytes 8388608
  18.0 13.4 %slice-start.7 = ((s8[14680064]{0:T(1024)(128)(4,1)}), s8[2097152]{0:T(1024)(128)(4,1)S(1)}, s32[]{:S(2)}) async-start(s8[14680064]{0:T(1024)(128)(4,1)} %bitcast.8), calls=%async_computation.7 | async-start | bytes 4194304
  18.0 8.9 %collective-permute-start.9 = (bf16[16,4224]{1,0:T(8,128)(2,1)S(1)}, bf16[16,4224]{1,0:T(8,128)(2,1)S(1)}, u32[]{:S(2)}, u32[]{:S(2)}) collective-permute-start(bf16[16,4224]{1,0:T(8,128)(2,1)S(1)} %shard_map.90.refs_8_), channel_id=1, source_target_pairs={{0,4},{1,3},{2,6},{3,1},{4,0},{5,7},{6,2},{7,5},{8,12},{9,11},{10,... | collective-permute-start | bytes 405512 | tf_op jit(solution)/shard_map/ppermute | solution.py:307
  20.9 5.5 %collective-permute-start.8 = (bf16[16,4224]{1,0:T(8,128)(2,1)S(1)}, bf16[16,4224]{1,0:T(8,128)(2,1)S(1)}, u32[]{:S(2)}, u32[]{:S(2)}) collective-permute-start(bf16[16,4224]{1,0:T(8,128)(2,1)S(1)} %shard_map.90.refs_8_), channel_id=1, source_target_pairs={{0,2},{1,5},{2,0},{3,7},{4,6},{5,1},{6,4},{7,3},{8,10},{9,13},{10,... | collective-permute-start | bytes 405512 | tf_op jit(solution)/shard_map/ppermute | solution.py:307
  22.5 7.2 %collective-permute-start.10 = (bf16[16,4224]{1,0:T(8,128)(2,1)S(1)}, bf16[16,4224]{1,0:T(8,128)(2,1)S(1)}, u32[]{:S(2)}, u32[]{:S(2)}) collective-permute-start(bf16[16,4224]{1,0:T(8,128)(2,1)S(1)} %collective-permute-done.4.refs_3_), channel_id=1, source_target_pairs={{0,8},{1,9},{2,10},{3,11},{4,12},{5,13},{6,14},{7,15},{8,0},{9,1},... | collective-permute-start | bytes 405512 | tf_op jit(solution)/shard_map/ppermute | solution.py:307
  23.2 6.5 %collective-permute-start.11 = (bf16[16,4224]{1,0:T(8,128)(2,1)S(1)}, bf16[16,4224]{1,0:T(8,128)(2,1)S(1)}, u32[]{:S(2)}, u32[]{:S(2)}) collective-permute-start(bf16[16,4224]{1,0:T(8,128)(2,1)S(1)} %shard_map.88.refs_6_), channel_id=1, source_target_pairs={{0,4},{1,3},{2,6},{3,1},{4,0},{5,7},{6,2},{7,5},{8,12},{9,11},{10,... | collective-permute-start | bytes 405512 | tf_op jit(solution)/shard_map/ppermute | solution.py:307
  26.4 5.0 %collective-permute-start.12 = (bf16[16,4224]{1,0:T(8,128)(2,1)S(1)}, bf16[16,4224]{1,0:T(8,128)(2,1)S(1)}, u32[]{:S(2)}, u32[]{:S(2)}) collective-permute-start(bf16[16,4224]{1,0:T(8,128)(2,1)S(1)} %collective-permute-done.8.refs_9_), channel_id=1, source_target_pairs={{0,4},{1,3},{2,6},{3,1},{4,0},{5,7},{6,2},{7,5},{8,12},{9,11},{10,... | collective-permute-start | bytes 405512 | tf_op jit(solution)/shard_map/ppermute | solution.py:307
  28.2 16.7 %slice-start.8 = ((s8[14680064]{0:T(1024)(128)(4,1)}), s8[4194304]{0:T(1024)(128)(4,1)S(1)}, s32[]{:S(2)}) async-start(s8[14680064]{0:T(1024)(128)(4,1)} %bitcast.10), calls=%async_computation.8 | async-start | bytes 8388608
  31.5 13.4 %slice-start.9 = ((s8[14680064]{0:T(1024)(128)(4,1)}), s8[4194304]{0:T(1024)(128)(4,1)S(1)}, s32[]{:S(2)}) async-start(s8[14680064]{0:T(1024)(128)(4,1)} %bitcast.10), calls=%async_computation.9 | async-start | bytes 8388608
  31.5 13.4 %slice-start.10 = ((s8[14680064]{0:T(1024)(128)(4,1)}), s8[4194304]{0:T(1024)(128)(4,1)S(1)}, s32[]{:S(2)}) async-start(s8[14680064]{0:T(1024)(128)(4,1)} %bitcast.10), calls=%async_computation.10 | async-start | bytes 8388608
  31.5 13.4 %slice-start.11 = ((s8[14680064]{0:T(1024)(128)(4,1)}), s8[2097152]{0:T(1024)(128)(4,1)S(1)}, s32[]{:S(2)}) async-start(s8[14680064]{0:T(1024)(128)(4,1)} %bitcast.10), calls=%async_computation.11 | async-start | bytes 4194304
  31.5 13.4 %copy-start.1 = (f32[4096]{0:T(1024)S(1)}, f32[4096]{0:T(1024)}, u32[]{:S(2)}) copy-start(f32[4096]{0:T(1024)} %param.13) | copy-start | bytes 49156
  40.9 4.0 %collective-permute-start.13 = (bf16[2,256,1792]{2,1,0:T(8,128)(2,1)S(1)}, bf16[2,256,1792]{2,1,0:T(8,128)(2,1)S(1)}, u32[]{:S(2)}, u32[]{:S(2)}) collective-permute-start(bf16[2,256,1792]{2,1,0:T(8,128)(2,1)S(1)} %get-tuple-element.39.a), channel_id=1, source_target_pairs={{0,1},{1,0},{2,3},{3,2},{4,5},{5,4},{6,7},{7,6},{8,9},{9,8},{10,11... | collective-permute-start | bytes 5505032 | tf_op jit(solution)/shard_map/ppermute | solution.py:310
  40.9 4.0 %collective-permute-start.14 = (f32[256,128]{1,0:T(8,128)S(1)}, f32[256,128]{1,0:T(8,128)S(1)}, u32[]{:S(2)}, u32[]{:S(2)}) collective-permute-start(f32[256,128]{1,0:T(8,128)S(1)} %get-tuple-element.40.sq), channel_id=1, source_target_pairs={{0,1},{1,0},{2,3},{3,2},{4,5},{5,4},{6,7},{7,6},{8,9},{9,8},{10,11... | collective-permute-start | bytes 393224 | tf_op jit(solution)/shard_map/ppermute | solution.py:310
  49.5 6.5 %collective-permute-start.20 = (bf16[32,4224]{1,0:T(8,128)(2,1)S(1)}, bf16[32,4224]{1,0:T(8,128)(2,1)S(1)}, u32[]{:S(2)}, u32[]{:S(2)}) collective-permute-start(bf16[32,4224]{1,0:T(8,128)(2,1)S(1)} %get-tuple-element.50), channel_id=1, source_target_pairs={{0,4},{1,3},{2,6},{3,1},{4,0},{5,7},{6,2},{7,5},{8,12},{9,11},{10,... | collective-permute-start | bytes 811016 | tf_op jit(solution)/shard_map/ppermute | solution.py:307
  50.1 14.4 %collective-permute-start.15 = (bf16[64,4096]{1,0:T(8,128)(2,1)S(1)}, bf16[64,4096]{1,0:T(8,128)(2,1)S(1)}, u32[]{:S(2)}, u32[]{:S(2)}) collective-permute-start(bf16[64,4096]{1,0:T(8,128)(2,1)S(1)} %get-tuple-element.43), channel_id=1, source_target_pairs={{0,8},{1,9},{2,10},{3,11},{4,12},{5,13},{6,14},{7,15},{8,0},{9,1},... | collective-permute-start | bytes 1572872 | tf_op jit(solution)/shard_map/ppermute | solution.py:307
  51.3 8.2 %collective-permute-start.19 = (bf16[32,4096]{1,0:T(8,128)(2,1)S(1)}, bf16[32,4096]{1,0:T(8,128)(2,1)S(1)}, u32[]{:S(2)}, u32[]{:S(2)}) collective-permute-start(bf16[32,4096]{1,0:T(8,128)(2,1)S(1)} %get-tuple-element.48), channel_id=1, source_target_pairs={{0,4},{1,3},{2,6},{3,1},{4,0},{5,7},{6,2},{7,5},{8,12},{9,11},{10,... | collective-permute-start | bytes 786440 | tf_op jit(solution)/shard_map/ppermute | solution.py:307
  56.1 6.5 %collective-permute-start.21 = (bf16[32,4224]{1,0:T(8,128)(2,1)S(1)}, bf16[32,4224]{1,0:T(8,128)(2,1)S(1)}, u32[]{:S(2)}, u32[]{:S(2)}) collective-permute-start(bf16[32,4224]{1,0:T(8,128)(2,1)S(1)} %get-tuple-element.54), channel_id=1, source_target_pairs={{0,2},{1,5},{2,0},{3,7},{4,6},{5,1},{6,4},{7,3},{8,10},{9,13},{10,... | collective-permute-start | bytes 811016 | tf_op jit(solution)/shard_map/ppermute | solution.py:307
  62.7 5.1 %collective-permute-start.22 = (bf16[16,4224]{1,0:T(8,128)(2,1)S(1)}, bf16[16,4224]{1,0:T(8,128)(2,1)S(1)}, u32[]{:S(2)}, u32[]{:S(2)}) collective-permute-start(bf16[16,4224]{1,0:T(8,128)(2,1)S(1)} %get-tuple-element.56), channel_id=1, source_target_pairs={{0,8},{1,9},{2,10},{3,11},{4,12},{5,13},{6,14},{7,15},{8,0},{9,1},... | collective-permute-start | bytes 405512 | tf_op jit(solution)/shard_map/ppermute | solution.py:307
  64.5 6.7 %collective-permute-start.17 = (bf16[16,4096]{1,0:T(8,128)(2,1)S(1)}, bf16[16,4096]{1,0:T(8,128)(2,1)S(1)}, u32[]{:S(2)}, u32[]{:S(2)}) collective-permute-start(bf16[16,4096]{1,0:T(8,128)(2,1)S(1)} %get-tuple-element.61), channel_id=1, source_target_pairs={{0,4},{1,3},{2,6},{3,1},{4,0},{5,7},{6,2},{7,5},{8,12},{9,11},{10,... | collective-permute-start | bytes 393224 | tf_op jit(solution)/shard_map/ppermute | solution.py:307
  65.0 11.1 %collective-permute-start.16 = (bf16[16,4096]{1,0:T(8,128)(2,1)S(1)}, bf16[16,4096]{1,0:T(8,128)(2,1)S(1)}, u32[]{:S(2)}, u32[]{:S(2)}) collective-permute-start(bf16[16,4096]{1,0:T(8,128)(2,1)S(1)} %get-tuple-element.60), channel_id=1, source_target_pairs={{0,4},{1,3},{2,6},{3,1},{4,0},{5,7},{6,2},{7,5},{8,12},{9,11},{10,... | collective-permute-start | bytes 393224 | tf_op jit(solution)/shard_map/ppermute | solution.py:307
  67.8 8.2 %collective-permute-start.23 = (bf16[16,4224]{1,0:T(8,128)(2,1)S(1)}, bf16[16,4224]{1,0:T(8,128)(2,1)S(1)}, u32[]{:S(2)}, u32[]{:S(2)}) collective-permute-start(bf16[16,4224]{1,0:T(8,128)(2,1)S(1)} %get-tuple-element.58), channel_id=1, source_target_pairs={{0,16},{1,17},{2,18},{3,19},{4,20},{5,21},{6,22},{7,23},{8,24},{9,... | collective-permute-start | bytes 405512 | tf_op jit(solution)/shard_map/ppermute | solution.py:307
  71.3 5.0 %collective-permute-start.18 = (bf16[16,4096]{1,0:T(8,128)(2,1)S(1)}, bf16[16,4096]{1,0:T(8,128)(2,1)S(1)}, u32[]{:S(2)}, u32[]{:S(2)}) collective-permute-start(bf16[16,4096]{1,0:T(8,128)(2,1)S(1)} %add_convert_fusion.1), channel_id=1, source_target_pairs={{0,2},{1,5},{2,0},{3,7},{4,6},{5,1},{6,4},{7,3},{8,10},{9,13},{10,... | collective-permute-start | bytes 393224 | tf_op jit(solution)/shard_map/ppermute | solution.py:307
  76.0 1.2 %collective-permute-start.24 = (f32[128]{0:T(128)S(1)}, f32[128]{0:T(128)S(1)}, u32[]{:S(2)}, u32[]{:S(2)}) collective-permute-start(f32[128]{0:T(128)S(1)} %bitcast_add_fusion), channel_id=1, source_target_pairs={{0,1},{1,0},{2,3},{3,2},{4,5},{5,4},{6,7},{7,6},{8,9},{9,8},{10,11... | collective-permute-start | bytes 1544 | tf_op jit(solution)/shard_map/ppermute | solution.py:310

commit v6 on v5

--- a/solution.py
+++ b/solution.py
@@ -193,26 +193,72 @@
 def gate_up(early, early_places, pieces, places, gain, w_gate, w_up):
     rows, width = early[0].shape
     units = w_gate.shape[0]
+    first_units = 5 * TILE
 
     def body(x_in, squares_in, owner_in, *refs):
         given = refs[: len(pieces)]
-        gain_ref, gate_ref, up_ref, part, squares, owner, x = refs[len(pieces) :]
+        gain_ref, gate_ref, up_ref, head, tail, owner, x, squares = refs[len(pieces) :]
         for start, stop in early_places:
             for source, to in ((x_in, x), (squares_in, squares), (owner_in, owner)):
                 to[start:stop, :] = source[start:stop, :]
         place_rows(given, places, gain_ref, x, squares, owner)
 
-        @pl.loop(0, units // TILE)
-        def _(i):
-            tile = pl.ds(pl.multiple_of(i * TILE, TILE), TILE)
-            for k, w in enumerate((gate_ref, up_ref)):
-                part[k, :, tile] = lax.dot_general(x[...], w[tile, :], NT, preferred_element_type=F32).astype(BF16)
+        total = squares[...]
+        high = total.astype(BF16).astype(F32)
+        middle = (total - high).astype(BF16).astype(F32)
+        low = total - high - middle
+        at = lax.broadcasted_iota(jnp.int32, (rows, LANES), 1)
+        pieces_of = jnp.where(at == 0, high, jnp.where(at == 1, middle, jnp.where(at == 2, low, 0.0)))
+        head[0, :, first_units:] = pieces_of.astype(BF16)
+        head[1, :, first_units:] = jnp.zeros((rows, LANES), BF16)
+        for part, first in ((head, 0), (tail, first_units)):
+
+            @pl.loop(0, part.shape[2] // TILE)
+            def _(i):
+                tile = pl.ds(pl.multiple_of(i * TILE, TILE), TILE)
+                row = pl.ds(pl.multiple_of(first + i * TILE, TILE), TILE)
+                for k, w in enumerate((gate_ref, up_ref)):
+                    part[k, :, tile] = lax.dot_general(x[...], w[row, :], NT, preferred_element_type=F32).astype(BF16)
 
     lanes = jax.ShapeDtypeStruct((rows, LANES), F32)
-    out_shape = (jax.ShapeDtypeStruct((2, rows, units), BF16), lanes, lanes)
-    scratch = [pltpu.VMEM((rows, width), BF16)]
+    parts = [jax.ShapeDtypeStruct((2, rows, n), BF16) for n in (first_units + LANES, units - first_units)]
+    out_shape = (*parts, lanes)
+    scratch = [pltpu.VMEM((rows, width), BF16), pltpu.VMEM((rows, LANES), F32)]
     args = (*early, *pieces, gain, w_gate, w_up)
     return call(body, out_shape, args, scratch, 7, 4 * rows * width * units)
+
+
+def hidden_units(part, other, scales, hidden):
+    units = hidden.shape[1]
+    q = hidden.shape[0] // 8
+    for block in range(8):
+        mate = block ^ 3 if block % 4 in (1, 2) else block
+        here = slice(block * q, (block + 1) * q)
+        there = slice(mate * q, (mate + 1) * q)
+        scale = scales[here, :1]
+        for lo in range(0, units, TILE):
+            cols = slice(lo, lo + TILE)
+            g = (part[0, here, cols].astype(F32) + other[0, there, cols].astype(F32)) * scale
+            u = (part[1, here, cols].astype(F32) + other[1, there, cols].astype(F32)) * scale
+            hidden[here, cols] = (jax.nn.silu(g) * u).astype(BF16)
+
+
+def first_hidden(part, other, width):
+    rows, units = part.shape[1], part.shape[2] - LANES
+    q = rows // 8
+
+    def body(part_ref, other_ref, hidden, scales):
+        for block in range(8):
+            mate = block ^ 3 if block % 4 in (1, 2) else block
+            here = slice(block * q, (block + 1) * q)
+            there = slice(mate * q, (mate + 1) * q)
+            squares = part_ref[0, here, units:].astype(F32) + other_ref[0, there, units:].astype(F32)
+            scale = lax.rsqrt(jnp.sum(squares, axis=1, keepdims=True) / (2 * width) + 1e-05)
+            scales[here, :] = jnp.broadcast_to(scale, (q, LANES))
+        hidden_units(part_ref, other_ref, scales, hidden)
+
+    out_shape = (jax.ShapeDtypeStruct((rows, units), BF16), jax.ShapeDtypeStruct((rows, LANES), F32))
+    return call(body, out_shape, (part, other), [], 4, 10**8)
 
 
 def split_lanes(total, rows):
@@ -223,29 +269,22 @@
     return jnp.where(at == 0, high, jnp.where(at == 1, middle, jnp.where(at == 2, low, 0.0))).astype(BF16)
 
 
-def down_rows(mine, theirs, squares, other_squares, owner, w_down, score, own):
+def down_rows(first, mine, theirs, scales, owner, w_down, score, own):
     units, width = w_down.shape
-    rows = squares.shape[0]
+    rows = owner.shape[0]
     q = rows // 8
     h = q // 2
     wide = 1024
-
-    def body(a, b, sq, other_sq, owner_ref, w, score_ref, own_ref, *rest):
+    split = first.shape[1]
+
+    def body(first_ref, a, b, scales_ref, owner_ref, w, score_ref, own_ref, *rest):
         near, across, far, (totals, hidden) = rest[:4], rest[4], rest[5:9], rest[9:]
-        for block in range(8):
-            other = block ^ 3 if block % 4 in (1, 2) else block
-            here = slice(block * q, (block + 1) * q)
-            there = slice(other * q, (other + 1) * q)
-            scale = lax.rsqrt((sq[here, :1] + other_sq[there, :1]) / (2 * width) + 1e-05)
-            for lo in range(0, units, TILE):
-                cols = slice(lo, lo + TILE)
-                g = (a[0, here, cols].astype(F32) + b[0, there, cols].astype(F32)) * scale
-                u = (a[1, here, cols].astype(F32) + b[1, there, cols].astype(F32)) * scale
-                hidden[here, cols] = (jax.nn.silu(g) * u).astype(BF16)
+        hidden_units(a, b, scales_ref, hidden)
         row_part = jnp.zeros((rows, 1), F32)
         for lo in range(0, width, wide):
             cols = slice(lo, lo + wide)
-            product = jnp.dot(hidden[...], w[:, cols], preferred_element_type=F32)
+            product = jnp.dot(first_ref[...], w[:split, cols], preferred_element_type=F32)
+            product += jnp.dot(hidden[...], w[split:, cols], preferred_element_type=F32)
             product_bf16 = product.astype(BF16)
             for block in range(4):
                 at = block * q
@@ -266,8 +305,8 @@
     shapes = [(h, width)] * 4 + [(4 * h, width)] + [(q, width)] * 3 + [(q, width + LANES)]
     blocks = [jax.ShapeDtypeStruct(shape, BF16) for shape in shapes]
     out_shape = (*blocks, jax.ShapeDtypeStruct((8, LANES), F32))
-    args = (mine, theirs, squares, other_squares, owner, w_down, score, own)
-    return call(body, out_shape, args, [pltpu.VMEM((rows, units), BF16)], 14, 2 * rows * units * width)
+    args = (first, mine, theirs, scales, owner, w_down, score, own)
+    return call(body, out_shape, args, [pltpu.VMEM((rows, units - split), BF16)], 14, 2 * rows * units * width)
 
 
 def carried(ref):
@@ -336,9 +375,13 @@
         early = early_rows(pieces, places, gain, 2 * half, 10**9)
         early_places = [(0, half - rows), (half, half + 3 * q)]
         late_places = [(half - rows,), (half + 3 * q,), (half + 3 * q + rows,)]
-        part, squares, owner = gate_up(early, early_places, [across_c, z2_c, z3_c], late_places, gain, w_gate, w_up)
-        other, other_squares = tp_swap(part), tp_swap(squares)
-        *near, across, f0, f1, f2, f3, totals = down_rows(part, other, squares, other_squares, owner, w_down, score, own)
+        late = [across_c, z2_c, z3_c]
+        head, tail, owner = gate_up(early, early_places, late, late_places, gain, w_gate, w_up)
+        other_head, other_tail = tp_swap(head), tp_swap(tail)
+        first, scales = first_hidden(head, other_head, preview.shape[1])
+        *near, across, f0, f1, f2, f3, totals = down_rows(
+            first, tail, other_tail, scales, owner, w_down, score, own
+        )
         width = preview.shape[1]
         counts = totals[1, :CAND]
         f3 = swap(f3, 2, 1)

time: 77.9 us -> 77.7 us (level)
    pallas_call x11 -> x12, Pallas kernels: 15.4 us -> 15.9 us  [call(): pl.pallas_call(body, out_shape=out_shape, in_specs=[VMEM] * len(args), ou...]
  transfers between devices with their start and end apart: 25 -> 25, of which waited for: 14 -> 15; matrix products, arithmetic and copies ran while one was open for 1% -> 1% of each run, Pallas kernels for 2% -> 3%
where the time goes in v6:
time: 77.7 us; the launch traced here: 77.5 us
  starting transfers between devices  30.8 us (40%)
  waiting for transfers between devices  27.5 us (35%)
  Pallas kernels  16.8 us (22%)
  other arithmetic  1.43 us (2%)
  between operations  0.94 us (1%)
    ppermute x22, starting transfers between devices, swap(): return lax.ppermute(v, BOTH, pairs)  30.1 us
    ppermute x22, waiting for transfers between devices, swap(): return lax.ppermute(v, BOTH, pairs)  24.6 us
    pallas_call x12, Pallas kernels, call(): pl.pallas_call(body, out_shape=out_shape, in_specs=[VMEM] * len(args), ou...  15.9 us
    ppermute x3, waiting for transfers between devices, tp_swap(): return lax.ppermute(v, 'tp', [(0, 1), (1, 0)])  2.87 us
  transfers between devices with their start and end apart: 25, of which 15 were waited for; matrix products, arithmetic and copies ran while one was open for 1% of the time, Pallas kernels for 3%

profile of v6, /device:TPU:0, one launch (start us, length us, event | category | flops | bytes accessed | tf_op | source)
XLA Modules:
  0.0 77.5 jit_solution(16788750765263331172)
XLA Ops:
  0.6 0.9 %shard_map.86.refs_0_.own_ref = bf16[16,4224]{1,0:T(8,128)(2,1)S(1)} custom-call(bf16[16,4096]{1,0:T(8,128)(2,1)} %rows_ref.1, s32[16]{0:T(128)} %owner_ref.1), custom_call_target="tpu_custom_call" | custom-call | flops 10000000000 | bytes 262144 | tf_op jit(solution)/shard_map/pallas_call | solution.py:151
  1.6 4.1 %collective-permute-start = (bf16[16,4224]{1,0:T(8,128)(2,1)S(1)}, bf16[16,4224]{1,0:T(8,128)(2,1)S(1)}, u32[]{:S(2)}, u32[]{:S(2)}) collective-permute-start(bf16[16,4224]{1,0:T(8,128)(2,1)S(1)} %shard_map.86.refs_0_.own_ref), channel_id=1, source_target_pairs={{0,16},{1,17},{2,18},{3,19},{4,20},{5,21},{6,22},{7,23},{8,24},{9,... | collective-permute-start | bytes 405512 | tf_op jit(solution)/shard_map/ppermute | solution.py:346
  5.7 1.5 %collective-permute-start.2 = (bf16[16,4224]{1,0:T(8,128)(2,1)S(1)}, bf16[16,4224]{1,0:T(8,128)(2,1)S(1)}, u32[]{:S(2)}, u32[]{:S(2)}) collective-permute-start(bf16[16,4224]{1,0:T(8,128)(2,1)S(1)} %shard_map.86.refs_0_.own_ref), channel_id=1, source_target_pairs={{0,4},{1,3},{2,6},{3,1},{4,0},{5,7},{6,2},{7,5},{8,12},{9,11},{10,... | collective-permute-start | bytes 405512 | tf_op jit(solution)/shard_map/ppermute | solution.py:346
  7.2 1.5 %collective-permute-start.1 = (bf16[16,4224]{1,0:T(8,128)(2,1)S(1)}, bf16[16,4224]{1,0:T(8,128)(2,1)S(1)}, u32[]{:S(2)}, u32[]{:S(2)}) collective-permute-start(bf16[16,4224]{1,0:T(8,128)(2,1)S(1)} %shard_map.86.refs_0_.own_ref), channel_id=1, source_target_pairs={{0,2},{1,5},{2,0},{3,7},{4,6},{5,1},{6,4},{7,3},{8,10},{9,13},{10,... | collective-permute-start | bytes 405512 | tf_op jit(solution)/shard_map/ppermute | solution.py:346
  8.7 3.5 %collective-permute-done.refs_0_ = bf16[16,4224]{1,0:T(8,128)(2,1)S(1)} collective-permute-done((bf16[16,4224]{1,0:T(8,128)(2,1)S(1)}, bf16[16,4224]{1,0:T(8,128)(2,1)S(1)}, u32[]{:S(2)}, u32[]{:S(2)}) %collective-permute-start) | collective-permute-done | bytes 135200 | tf_op jit(solution)/shard_map/ppermute | solution.py:346
  12.2 0.7 collective-permute-start.7
  12.9 0.0 collective-permute-done.2.refs_2_
  12.9 0.0 collective-permute-done.1.refs_1_
  12.9 1.6 %collective-permute-start.6 = (bf16[16,4224]{1,0:T(8,128)(2,1)S(1)}, bf16[16,4224]{1,0:T(8,128)(2,1)S(1)}, u32[]{:S(2)}, u32[]{:S(2)}) collective-permute-start(bf16[16,4224]{1,0:T(8,128)(2,1)S(1)} %shard_map.87.refs_5_), channel_id=1, source_target_pairs={{0,4},{1,3},{2,6},{3,1},{4,0},{5,7},{6,2},{7,5},{8,12},{9,11},{10,... | collective-permute-start | bytes 405512 | tf_op jit(solution)/shard_map/ppermute | solution.py:346
  14.5 1.5 %collective-permute-start.3 = (bf16[16,4224]{1,0:T(8,128)(2,1)S(1)}, bf16[16,4224]{1,0:T(8,128)(2,1)S(1)}, u32[]{:S(2)}, u32[]{:S(2)}) collective-permute-start(bf16[16,4224]{1,0:T(8,128)(2,1)S(1)} %shard_map.87.refs_5_), channel_id=1, source_target_pairs={{0,2},{1,5},{2,0},{3,7},{4,6},{5,1},{6,4},{7,3},{8,10},{9,13},{10,... | collective-permute-start | bytes 405512 | tf_op jit(solution)/shard_map/ppermute | solution.py:346
  16.0 0.5 collective-permute-start.4
  16.5 1.4 %collective-permute-start.5 = (bf16[48,4224]{1,0:T(8,128)(2,1)S(1)}, bf16[48,4224]{1,0:T(8,128)(2,1)S(1)}, u32[]{:S(2)}, u32[]{:S(2)}) collective-permute-start(bf16[48,4224]{1,0:T(8,128)(2,1)S(1)} %shard_map.89), channel_id=1, source_target_pairs={{0,8},{1,9},{2,10},{3,11},{4,12},{5,13},{6,14},{7,15},{8,0},{9,1},... | collective-permute-start | bytes 1216520 | tf_op jit(solution)/shard_map/ppermute | solution.py:346
  17.9 0.0 collective-permute-done.7.refs_0_
  18.0 0.0 slice-start.5
  18.0 0.0 copy-start
  18.0 0.0 slice-start.2
  18.0 0.0 slice-start.3
  18.0 0.0 slice-start.6
  18.0 1.6 %collective-permute-start.9 = (bf16[16,4224]{1,0:T(8,128)(2,1)S(1)}, bf16[16,4224]{1,0:T(8,128)(2,1)S(1)}, u32[]{:S(2)}, u32[]{:S(2)}) collective-permute-start(bf16[16,4224]{1,0:T(8,128)(2,1)S(1)} %shard_map.90.refs_8_), channel_id=1, source_target_pairs={{0,4},{1,3},{2,6},{3,1},{4,0},{5,7},{6,2},{7,5},{8,12},{9,11},{10,... | collective-permute-start | bytes 405512 | tf_op jit(solution)/shard_map/ppermute | solution.py:346
  19.6 1.3 %collective-permute-done.3.refs_0_ = bf16[16,4224]{1,0:T(8,128)(2,1)S(1)} collective-permute-done((bf16[16,4224]{1,0:T(8,128)(2,1)S(1)}, bf16[16,4224]{1,0:T(8,128)(2,1)S(1)}, u32[]{:S(2)}, u32[]{:S(2)}) %collective-permute-start.3) | collective-permute-done | bytes 135200 | tf_op jit(solution)/shard_map/ppermute | solution.py:346
  20.9 1.5 %collective-permute-start.8 = (bf16[16,4224]{1,0:T(8,128)(2,1)S(1)}, bf16[16,4224]{1,0:T(8,128)(2,1)S(1)}, u32[]{:S(2)}, u32[]{:S(2)}) collective-permute-start(bf16[16,4224]{1,0:T(8,128)(2,1)S(1)} %shard_map.90.refs_8_), channel_id=1, source_target_pairs={{0,2},{1,5},{2,0},{3,7},{4,6},{5,1},{6,4},{7,3},{8,10},{9,13},{10,... | collective-permute-start | bytes 405512 | tf_op jit(solution)/shard_map/ppermute | solution.py:346
  22.5 0.0 collective-permute-done.4.refs_3_
  22.5 0.7 collective-permute-start.10
  23.2 3.2 %collective-permute-done.8.refs_9_ = bf16[16,4224]{1,0:T(8,128)(2,1)S(1)} collective-permute-done((bf16[16,4224]{1,0:T(8,128)(2,1)S(1)}, bf16[16,4224]{1,0:T(8,128)(2,1)S(1)}, u32[]{:S(2)}, u32[]{:S(2)}) %collective-permute-start.8) | collective-permute-done | bytes 135200 | tf_op jit(solution)/shard_map/ppermute | solution.py:346
  26.4 0.5 collective-permute-start.12
  26.9 1.3 %collective-permute-done.5.refs_4_ = bf16[48,4224]{1,0:T(8,128)(2,1)S(1)} collective-permute-done((bf16[48,4224]{1,0:T(8,128)(2,1)S(1)}, bf16[48,4224]{1,0:T(8,128)(2,1)S(1)}, u32[]{:S(2)}, u32[]{:S(2)}) %collective-permute-start.5) | collective-permute-done | bytes 405536 | tf_op jit(solution)/shard_map/ppermute | solution.py:346
  28.2 0.7 shard_map.91
  28.9 0.8 %collective-permute-done.10.refs_0_ = bf16[16,4224]{1,0:T(8,128)(2,1)S(1)} collective-permute-done((bf16[16,4224]{1,0:T(8,128)(2,1)S(1)}, bf16[16,4224]{1,0:T(8,128)(2,1)S(1)}, u32[]{:S(2)}, u32[]{:S(2)}) %collective-permute-start.10) | collective-permute-done | bytes 135200 | tf_op jit(solution)/shard_map/ppermute | solution.py:346
  29.7 0.0 collective-permute-done.11.refs_1_
  29.7 1.7 %collective-permute-done.12.refs_2_ = bf16[16,4224]{1,0:T(8,128)(2,1)S(1)} collective-permute-done((bf16[16,4224]{1,0:T(8,128)(2,1)S(1)}, bf16[16,4224]{1,0:T(8,128)(2,1)S(1)}, u32[]{:S(2)}, u32[]{:S(2)}) %collective-permute-start.12) | collective-permute-done | bytes 135200 | tf_op jit(solution)/shard_map/ppermute | solution.py:346
  31.5 0.0 slice-start.9
  31.5 0.0 copy-start.1
  31.5 9.3 %shard_map.92 = (bf16[2,256,1408]{2,1,0:T(8,128)(2,1)S(1)}, bf16[2,256,512]{2,1,0:T(8,128)(2,1)S(1)}, f32[256,128]{1,0:T(8,128)S(1)}) custom-call(bf16[256,4096]{1,0:T(8,128)(2,1)S(1)} %get-tuple-element.38.x_in, f32[256,128]{1,0:T(8,128)S(1)} %get-tuple-element.39.squares_in, f32[256,128]{1,0:T(8,128)S(1)} %get-tuple-element.40.owner_in, ...), custom_call_target="tpu_custom_call" | custom-call | flops 7516192768 | bytes 32141312 | tf_op jit(solution)/shard_map/pallas_call | solution.py:129
  40.9 0.1 collective-permute-start.13
  41.0 0.5 collective-permute-start.14
  41.5 2.7 %collective-permute-done.13.other_ref = bf16[2,256,1408]{2,1,0:T(8,128)(2,1)S(1)} collective-permute-done((bf16[2,256,1408]{2,1,0:T(8,128)(2,1)S(1)}, bf16[2,256,1408]{2,1,0:T(8,128)(2,1)S(1)}, u32[]{:S(2)}, u32[]{:S(2)}) %collective-permute-start.13) | collective-permute-done | bytes 1441824 | tf_op jit(solution)/shard_map/ppermute | solution.py:349
  44.2 0.7 shard_map.93
  44.8 0.1 collective-permute-done.14.b
  45.0 4.4 %shard_map.94 = (bf16[16,4096]{1,0:T(8,128)(2,1)S(1)}, bf16[16,4096]{1,0:T(8,128)(2,1)S(1)}, bf16[16,4096]{1,0:T(8,128)(2,1)S(1)}, bf16[16,4096]{1,0:T(8,128)(2,...) custom-call(bf16[256,1280]{1,0:T(8,128)(2,1)S(1)} %get-tuple-element, ...), custom_call_target="tpu_custom_call" | custom-call | flops 3758096384 | bytes 16797696 | tf_op jit(solution)/shard_map/pallas_call | solution.py:129
  49.3 0.6 collective-permute-start.20
  49.9 1.3 %collective-permute-start.15 = (bf16[64,4096]{1,0:T(8,128)(2,1)S(1)}, bf16[64,4096]{1,0:T(8,128)(2,1)S(1)}, u32[]{:S(2)}, u32[]{:S(2)}) collective-permute-start(bf16[64,4096]{1,0:T(8,128)(2,1)S(1)} %get-tuple-element.47), channel_id=1, source_target_pairs={{0,8},{1,9},{2,10},{3,11},{4,12},{5,13},{6,14},{7,15},{8,0},{9,1},... | collective-permute-start | bytes 1572872 | tf_op jit(solution)/shard_map/ppermute | solution.py:346
  51.2 1.9 %collective-permute-start.19 = (bf16[32,4096]{1,0:T(8,128)(2,1)S(1)}, bf16[32,4096]{1,0:T(8,128)(2,1)S(1)}, u32[]{:S(2)}, u32[]{:S(2)}) collective-permute-start(bf16[32,4096]{1,0:T(8,128)(2,1)S(1)} %get-tuple-element.52), channel_id=1, source_target_pairs={{0,4},{1,3},{2,6},{3,1},{4,0},{5,7},{6,2},{7,5},{8,12},{9,11},{10,... | collective-permute-start | bytes 786440 | tf_op jit(solution)/shard_map/ppermute | solution.py:346
  53.1 2.7 %collective-permute-done.20.refs_1_.refs_3_ = bf16[32,4224]{1,0:T(8,128)(2,1)S(1)} collective-permute-done((bf16[32,4224]{1,0:T(8,128)(2,1)S(1)}, bf16[32,4224]{1,0:T(8,128)(2,1)S(1)}, u32[]{:S(2)}, u32[]{:S(2)}) %collective-permute-start.20) | collective-permute-done | bytes 270368 | tf_op jit(solution)/shard_map/ppermute | solution.py:346
  55.9 0.1 shard_map.95
  55.9 1.1 %collective-permute-start.21 = (bf16[32,4224]{1,0:T(8,128)(2,1)S(1)}, bf16[32,4224]{1,0:T(8,128)(2,1)S(1)}, u32[]{:S(2)}, u32[]{:S(2)}) collective-permute-start(bf16[32,4224]{1,0:T(8,128)(2,1)S(1)} %get-tuple-element.58), channel_id=1, source_target_pairs={{0,2},{1,5},{2,0},{3,7},{4,6},{5,1},{6,4},{7,3},{8,10},{9,13},{10,... | collective-permute-start | bytes 811016 | tf_op jit(solution)/shard_map/ppermute | solution.py:346
  57.1 2.3 %collective-permute-done.19.refs_1_ = bf16[32,4096]{1,0:T(8,128)(2,1)S(1)} collective-permute-done((bf16[32,4096]{1,0:T(8,128)(2,1)S(1)}, bf16[32,4096]{1,0:T(8,128)(2,1)S(1)}, u32[]{:S(2)}, u32[]{:S(2)}) %collective-permute-start.19) | collective-permute-done | bytes 262176 | tf_op jit(solution)/shard_map/ppermute | solution.py:346
  59.4 0.6 shard_map.96
  60.0 2.4 %collective-permute-done.21.refs_1_.refs_3_ = bf16[32,4224]{1,0:T(8,128)(2,1)S(1)} collective-permute-done((bf16[32,4224]{1,0:T(8,128)(2,1)S(1)}, bf16[32,4224]{1,0:T(8,128)(2,1)S(1)}, u32[]{:S(2)}, u32[]{:S(2)}) %collective-permute-start.21) | collective-permute-done | bytes 270368 | tf_op jit(solution)/shard_map/ppermute | solution.py:346
  62.5 0.1 shard_map.97
  62.5 1.8 %collective-permute-start.22 = (bf16[16,4224]{1,0:T(8,128)(2,1)S(1)}, bf16[16,4224]{1,0:T(8,128)(2,1)S(1)}, u32[]{:S(2)}, u32[]{:S(2)}) collective-permute-start(bf16[16,4224]{1,0:T(8,128)(2,1)S(1)} %get-tuple-element.60), channel_id=1, source_target_pairs={{0,8},{1,9},{2,10},{3,11},{4,12},{5,13},{6,14},{7,15},{8,0},{9,1},... | collective-permute-start | bytes 405512 | tf_op jit(solution)/shard_map/ppermute | solution.py:346
  64.3 0.0 collective-permute-done.15
  64.3 0.1 add_convert_fusion.4
  64.4 0.5 collective-permute-start.17
  64.8 1.6 %collective-permute-start.16 = (bf16[16,4096]{1,0:T(8,128)(2,1)S(1)}, bf16[16,4096]{1,0:T(8,128)(2,1)S(1)}, u32[]{:S(2)}, u32[]{:S(2)}) collective-permute-start(bf16[16,4096]{1,0:T(8,128)(2,1)S(1)} %get-tuple-element.64), channel_id=1, source_target_pairs={{0,4},{1,3},{2,6},{3,1},{4,0},{5,7},{6,2},{7,5},{8,12},{9,11},{10,... | collective-permute-start | bytes 393224 | tf_op jit(solution)/shard_map/ppermute | solution.py:346
  66.5 1.1 %collective-permute-done.22.refs_1_.refs_3_ = bf16[16,4224]{1,0:T(8,128)(2,1)S(1)} collective-permute-done((bf16[16,4224]{1,0:T(8,128)(2,1)S(1)}, bf16[16,4224]{1,0:T(8,128)(2,1)S(1)}, u32[]{:S(2)}, u32[]{:S(2)}) %collective-permute-start.22) | collective-permute-done | bytes 135200 | tf_op jit(solution)/shard_map/ppermute | solution.py:346
  67.6 3.4 %collective-permute-start.23 = (bf16[16,4224]{1,0:T(8,128)(2,1)S(1)}, bf16[16,4224]{1,0:T(8,128)(2,1)S(1)}, u32[]{:S(2)}, u32[]{:S(2)}) collective-permute-start(bf16[16,4224]{1,0:T(8,128)(2,1)S(1)} %get-tuple-element.62), channel_id=1, source_target_pairs={{0,16},{1,17},{2,18},{3,19},{4,20},{5,21},{6,22},{7,23},{8,24},{9,... | collective-permute-start | bytes 405512 | tf_op jit(solution)/shard_map/ppermute | solution.py:346
  71.1 0.1 add_convert_fusion.1
  71.1 0.7 collective-permute-start.18
  71.9 4.0 %collective-permute-done.23 = bf16[16,4224]{1,0:T(8,128)(2,1)S(1)} collective-permute-done((bf16[16,4224]{1,0:T(8,128)(2,1)S(1)}, bf16[16,4224]{1,0:T(8,128)(2,1)S(1)}, u32[]{:S(2)}, u32[]{:S(2)}) %collective-permute-start.23) | collective-permute-done | bytes 135200 | tf_op jit(solution)/shard_map/ppermute | solution.py:346
  75.8 0.1 collective-permute-start.24
  75.9 0.3 collective-permute-done.18
  76.2 0.8 add_convert_fusion
  76.9 0.1 collective-permute-done.24
  77.0 0.5 bitcast_divide_fusion
  (37 shorter events, 0.2 us)
Async XLA Ops:
  1.6 10.6 %collective-permute-start = (bf16[16,4224]{1,0:T(8,128)(2,1)S(1)}, bf16[16,4224]{1,0:T(8,128)(2,1)S(1)}, u32[]{:S(2)}, u32[]{:S(2)}) collective-permute-start(bf16[16,4224]{1,0:T(8,128)(2,1)S(1)} %shard_map.86.refs_0_.own_ref), channel_id=1, source_target_pairs={{0,16},{1,17},{2,18},{3,19},{4,20},{5,21},{6,22},{7,23},{8,24},{9,... | collective-permute-start | bytes 405512 | tf_op jit(solution)/shard_map/ppermute | solution.py:346
  5.7 7.2 %collective-permute-start.2 = (bf16[16,4224]{1,0:T(8,128)(2,1)S(1)}, bf16[16,4224]{1,0:T(8,128)(2,1)S(1)}, u32[]{:S(2)}, u32[]{:S(2)}) collective-permute-start(bf16[16,4224]{1,0:T(8,128)(2,1)S(1)} %shard_map.86.refs_0_.own_ref), channel_id=1, source_target_pairs={{0,4},{1,3},{2,6},{3,1},{4,0},{5,7},{6,2},{7,5},{8,12},{9,11},{10,... | collective-permute-start | bytes 405512 | tf_op jit(solution)/shard_map/ppermute | solution.py:346
  7.2 5.7 %collective-permute-start.1 = (bf16[16,4224]{1,0:T(8,128)(2,1)S(1)}, bf16[16,4224]{1,0:T(8,128)(2,1)S(1)}, u32[]{:S(2)}, u32[]{:S(2)}) collective-permute-start(bf16[16,4224]{1,0:T(8,128)(2,1)S(1)} %shard_map.86.refs_0_.own_ref), channel_id=1, source_target_pairs={{0,2},{1,5},{2,0},{3,7},{4,6},{5,1},{6,4},{7,3},{8,10},{9,13},{10,... | collective-permute-start | bytes 405512 | tf_op jit(solution)/shard_map/ppermute | solution.py:346
  12.2 5.8 %collective-permute-start.7 = (bf16[16,4224]{1,0:T(8,128)(2,1)S(1)}, bf16[16,4224]{1,0:T(8,128)(2,1)S(1)}, u32[]{:S(2)}, u32[]{:S(2)}) collective-permute-start(bf16[16,4224]{1,0:T(8,128)(2,1)S(1)} %collective-permute-done.refs_0_), channel_id=1, source_target_pairs={{0,8},{1,9},{2,10},{3,11},{4,12},{5,13},{6,14},{7,15},{8,0},{9,1},... | collective-permute-start | bytes 405512 | tf_op jit(solution)/shard_map/ppermute | solution.py:346
  12.9 10.3 %collective-permute-start.6 = (bf16[16,4224]{1,0:T(8,128)(2,1)S(1)}, bf16[16,4224]{1,0:T(8,128)(2,1)S(1)}, u32[]{:S(2)}, u32[]{:S(2)}) collective-permute-start(bf16[16,4224]{1,0:T(8,128)(2,1)S(1)} %shard_map.87.refs_5_), channel_id=1, source_target_pairs={{0,4},{1,3},{2,6},{3,1},{4,0},{5,7},{6,2},{7,5},{8,12},{9,11},{10,... | collective-permute-start | bytes 405512 | tf_op jit(solution)/shard_map/ppermute | solution.py:346
  14.5 6.5 %collective-permute-start.3 = (bf16[16,4224]{1,0:T(8,128)(2,1)S(1)}, bf16[16,4224]{1,0:T(8,128)(2,1)S(1)}, u32[]{:S(2)}, u32[]{:S(2)}) collective-permute-start(bf16[16,4224]{1,0:T(8,128)(2,1)S(1)} %shard_map.87.refs_5_), channel_id=1, source_target_pairs={{0,2},{1,5},{2,0},{3,7},{4,6},{5,1},{6,4},{7,3},{8,10},{9,13},{10,... | collective-permute-start | bytes 405512 | tf_op jit(solution)/shard_map/ppermute | solution.py:346
  16.0 6.5 %collective-permute-start.4 = (bf16[16,4224]{1,0:T(8,128)(2,1)S(1)}, bf16[16,4224]{1,0:T(8,128)(2,1)S(1)}, u32[]{:S(2)}, u32[]{:S(2)}) collective-permute-start(bf16[16,4224]{1,0:T(8,128)(2,1)S(1)} %collective-permute-done.1.refs_1_), channel_id=1, source_target_pairs={{0,4},{1,3},{2,6},{3,1},{4,0},{5,7},{6,2},{7,5},{8,12},{9,11},{10,... | collective-permute-start | bytes 405512 | tf_op jit(solution)/shard_map/ppermute | solution.py:346
  16.5 11.7 %collective-permute-start.5 = (bf16[48,4224]{1,0:T(8,128)(2,1)S(1)}, bf16[48,4224]{1,0:T(8,128)(2,1)S(1)}, u32[]{:S(2)}, u32[]{:S(2)}) collective-permute-start(bf16[48,4224]{1,0:T(8,128)(2,1)S(1)} %shard_map.89), channel_id=1, source_target_pairs={{0,8},{1,9},{2,10},{3,11},{4,12},{5,13},{6,14},{7,15},{8,0},{9,1},... | collective-permute-start | bytes 1216520 | tf_op jit(solution)/shard_map/ppermute | solution.py:346
  17.9 13.5 %slice-start = ((s8[14680064]{0:T(1024)(128)(4,1)}), s8[4194304]{0:T(1024)(128)(4,1)S(1)}, s32[]{:S(2)}) async-start(s8[14680064]{0:T(1024)(128)(4,1)} %bitcast.6), calls=%async_computation | async-start | bytes 8388608
  17.9 13.5 %slice-start.1 = ((s8[14680064]{0:T(1024)(128)(4,1)}), s8[4194304]{0:T(1024)(128)(4,1)S(1)}, s32[]{:S(2)}) async-start(s8[14680064]{0:T(1024)(128)(4,1)} %bitcast.6), calls=%async_computation.1 | async-start | bytes 8388608
  17.9 13.5 %slice-start.4 = ((s8[14680064]{0:T(1024)(128)(4,1)}), s8[4194304]{0:T(1024)(128)(4,1)S(1)}, s32[]{:S(2)}) async-start(s8[14680064]{0:T(1024)(128)(4,1)} %bitcast.8), calls=%async_computation.4 | async-start | bytes 8388608
  18.0 13.5 %slice-start.5 = ((s8[14680064]{0:T(1024)(128)(4,1)}), s8[4194304]{0:T(1024)(128)(4,1)S(1)}, s32[]{:S(2)}) async-start(s8[14680064]{0:T(1024)(128)(4,1)} %bitcast.8), calls=%async_computation.5 | async-start | bytes 8388608
  18.0 10.3 %copy-start = (f32[4096]{0:T(1024)S(1)}, f32[4096]{0:T(1024)}, u32[]{:S(2)}) copy-start(f32[4096]{0:T(1024)} %param.9) | copy-start | bytes 49156
  18.0 13.4 %slice-start.2 = ((s8[14680064]{0:T(1024)(128)(4,1)}), s8[4194304]{0:T(1024)(128)(4,1)S(1)}, s32[]{:S(2)}) async-start(s8[14680064]{0:T(1024)(128)(4,1)} %bitcast.6), calls=%async_computation.2 | async-start | bytes 8388608
  18.0 13.4 %slice-start.3 = ((s8[14680064]{0:T(1024)(128)(4,1)}), s8[2097152]{0:T(1024)(128)(4,1)S(1)}, s32[]{:S(2)}) async-start(s8[14680064]{0:T(1024)(128)(4,1)} %bitcast.6), calls=%async_computation.3 | async-start | bytes 4194304
  18.0 13.4 %slice-start.6 = ((s8[14680064]{0:T(1024)(128)(4,1)}), s8[4194304]{0:T(1024)(128)(4,1)S(1)}, s32[]{:S(2)}) async-start(s8[14680064]{0:T(1024)(128)(4,1)} %bitcast.8), calls=%async_computation.6 | async-start | bytes 8388608
  18.0 13.4 %slice-start.7 = ((s8[14680064]{0:T(1024)(128)(4,1)}), s8[2097152]{0:T(1024)(128)(4,1)S(1)}, s32[]{:S(2)}) async-start(s8[14680064]{0:T(1024)(128)(4,1)} %bitcast.8), calls=%async_computation.7 | async-start | bytes 4194304
  18.0 8.9 %collective-permute-start.9 = (bf16[16,4224]{1,0:T(8,128)(2,1)S(1)}, bf16[16,4224]{1,0:T(8,128)(2,1)S(1)}, u32[]{:S(2)}, u32[]{:S(2)}) collective-permute-start(bf16[16,4224]{1,0:T(8,128)(2,1)S(1)} %shard_map.90.refs_8_), channel_id=1, source_target_pairs={{0,4},{1,3},{2,6},{3,1},{4,0},{5,7},{6,2},{7,5},{8,12},{9,11},{10,... | collective-permute-start | bytes 405512 | tf_op jit(solution)/shard_map/ppermute | solution.py:346
  20.9 5.5 %collective-permute-start.8 = (bf16[16,4224]{1,0:T(8,128)(2,1)S(1)}, bf16[16,4224]{1,0:T(8,128)(2,1)S(1)}, u32[]{:S(2)}, u32[]{:S(2)}) collective-permute-start(bf16[16,4224]{1,0:T(8,128)(2,1)S(1)} %shard_map.90.refs_8_), channel_id=1, source_target_pairs={{0,2},{1,5},{2,0},{3,7},{4,6},{5,1},{6,4},{7,3},{8,10},{9,13},{10,... | collective-permute-start | bytes 405512 | tf_op jit(solution)/shard_map/ppermute | solution.py:346
  22.5 7.2 %collective-permute-start.10 = (bf16[16,4224]{1,0:T(8,128)(2,1)S(1)}, bf16[16,4224]{1,0:T(8,128)(2,1)S(1)}, u32[]{:S(2)}, u32[]{:S(2)}) collective-permute-start(bf16[16,4224]{1,0:T(8,128)(2,1)S(1)} %collective-permute-done.4.refs_3_), channel_id=1, source_target_pairs={{0,8},{1,9},{2,10},{3,11},{4,12},{5,13},{6,14},{7,15},{8,0},{9,1},... | collective-permute-start | bytes 405512 | tf_op jit(solution)/shard_map/ppermute | solution.py:346
  23.2 6.5 %collective-permute-start.11 = (bf16[16,4224]{1,0:T(8,128)(2,1)S(1)}, bf16[16,4224]{1,0:T(8,128)(2,1)S(1)}, u32[]{:S(2)}, u32[]{:S(2)}) collective-permute-start(bf16[16,4224]{1,0:T(8,128)(2,1)S(1)} %shard_map.88.refs_6_), channel_id=1, source_target_pairs={{0,4},{1,3},{2,6},{3,1},{4,0},{5,7},{6,2},{7,5},{8,12},{9,11},{10,... | collective-permute-start | bytes 405512 | tf_op jit(solution)/shard_map/ppermute | solution.py:346
  26.4 5.0 %collective-permute-start.12 = (bf16[16,4224]{1,0:T(8,128)(2,1)S(1)}, bf16[16,4224]{1,0:T(8,128)(2,1)S(1)}, u32[]{:S(2)}, u32[]{:S(2)}) collective-permute-start(bf16[16,4224]{1,0:T(8,128)(2,1)S(1)} %collective-permute-done.8.refs_9_), channel_id=1, source_target_pairs={{0,4},{1,3},{2,6},{3,1},{4,0},{5,7},{6,2},{7,5},{8,12},{9,11},{10,... | collective-permute-start | bytes 405512 | tf_op jit(solution)/shard_map/ppermute | solution.py:346
  28.2 16.7 %slice-start.8 = ((s8[14680064]{0:T(1024)(128)(4,1)}), s8[4194304]{0:T(1024)(128)(4,1)S(1)}, s32[]{:S(2)}) async-start(s8[14680064]{0:T(1024)(128)(4,1)} %bitcast.10), calls=%async_computation.8 | async-start | bytes 8388608
  31.5 13.4 %slice-start.9 = ((s8[14680064]{0:T(1024)(128)(4,1)}), s8[4194304]{0:T(1024)(128)(4,1)S(1)}, s32[]{:S(2)}) async-start(s8[14680064]{0:T(1024)(128)(4,1)} %bitcast.10), calls=%async_computation.9 | async-start | bytes 8388608
  31.5 13.4 %slice-start.10 = ((s8[14680064]{0:T(1024)(128)(4,1)}), s8[4194304]{0:T(1024)(128)(4,1)S(1)}, s32[]{:S(2)}) async-start(s8[14680064]{0:T(1024)(128)(4,1)} %bitcast.10), calls=%async_computation.10 | async-start | bytes 8388608
  31.5 13.4 %slice-start.11 = ((s8[14680064]{0:T(1024)(128)(4,1)}), s8[2097152]{0:T(1024)(128)(4,1)S(1)}, s32[]{:S(2)}) async-start(s8[14680064]{0:T(1024)(128)(4,1)} %bitcast.10), calls=%async_computation.11 | async-start | bytes 4194304
  31.5 13.4 %copy-start.1 = (f32[4096]{0:T(1024)S(1)}, f32[4096]{0:T(1024)}, u32[]{:S(2)}) copy-start(f32[4096]{0:T(1024)} %param.13) | copy-start | bytes 49156
  40.9 3.3 %collective-permute-start.13 = (bf16[2,256,1408]{2,1,0:T(8,128)(2,1)S(1)}, bf16[2,256,1408]{2,1,0:T(8,128)(2,1)S(1)}, u32[]{:S(2)}, u32[]{:S(2)}) collective-permute-start(bf16[2,256,1408]{2,1,0:T(8,128)(2,1)S(1)} %get-tuple-element.41.part_ref), channel_id=1, source_target_pairs={{0,1},{1,0},{2,3},{3,2},{4,5},{5,4},{6,7},{7,6},{8,9},{9,8},{10,11... | collective-permute-start | bytes 4325384 | tf_op jit(solution)/shard_map/ppermute | solution.py:349
  41.0 4.0 %collective-permute-start.14 = (bf16[2,256,512]{2,1,0:T(8,128)(2,1)S(1)}, bf16[2,256,512]{2,1,0:T(8,128)(2,1)S(1)}, u32[]{:S(2)}, u32[]{:S(2)}) collective-permute-start(bf16[2,256,512]{2,1,0:T(8,128)(2,1)S(1)} %get-tuple-element.43.a), channel_id=1, source_target_pairs={{0,1},{1,0},{2,3},{3,2},{4,5},{5,4},{6,7},{7,6},{8,9},{9,8},{10,11... | collective-permute-start | bytes 1572872 | tf_op jit(solution)/shard_map/ppermute | solution.py:349
  49.3 6.5 %collective-permute-start.20 = (bf16[32,4224]{1,0:T(8,128)(2,1)S(1)}, bf16[32,4224]{1,0:T(8,128)(2,1)S(1)}, u32[]{:S(2)}, u32[]{:S(2)}) collective-permute-start(bf16[32,4224]{1,0:T(8,128)(2,1)S(1)} %get-tuple-element.54), channel_id=1, source_target_pairs={{0,4},{1,3},{2,6},{3,1},{4,0},{5,7},{6,2},{7,5},{8,12},{9,11},{10,... | collective-permute-start | bytes 811016 | tf_op jit(solution)/shard_map/ppermute | solution.py:346
  49.9 14.4 %collective-permute-start.15 = (bf16[64,4096]{1,0:T(8,128)(2,1)S(1)}, bf16[64,4096]{1,0:T(8,128)(2,1)S(1)}, u32[]{:S(2)}, u32[]{:S(2)}) collective-permute-start(bf16[64,4096]{1,0:T(8,128)(2,1)S(1)} %get-tuple-element.47), channel_id=1, source_target_pairs={{0,8},{1,9},{2,10},{3,11},{4,12},{5,13},{6,14},{7,15},{8,0},{9,1},... | collective-permute-start | bytes 1572872 | tf_op jit(solution)/shard_map/ppermute | solution.py:346
  51.2 8.2 %collective-permute-start.19 = (bf16[32,4096]{1,0:T(8,128)(2,1)S(1)}, bf16[32,4096]{1,0:T(8,128)(2,1)S(1)}, u32[]{:S(2)}, u32[]{:S(2)}) collective-permute-start(bf16[32,4096]{1,0:T(8,128)(2,1)S(1)} %get-tuple-element.52), channel_id=1, source_target_pairs={{0,4},{1,3},{2,6},{3,1},{4,0},{5,7},{6,2},{7,5},{8,12},{9,11},{10,... | collective-permute-start | bytes 786440 | tf_op jit(solution)/shard_map/ppermute | solution.py:346
  55.9 6.5 %collective-permute-start.21 = (bf16[32,4224]{1,0:T(8,128)(2,1)S(1)}, bf16[32,4224]{1,0:T(8,128)(2,1)S(1)}, u32[]{:S(2)}, u32[]{:S(2)}) collective-permute-start(bf16[32,4224]{1,0:T(8,128)(2,1)S(1)} %get-tuple-element.58), channel_id=1, source_target_pairs={{0,2},{1,5},{2,0},{3,7},{4,6},{5,1},{6,4},{7,3},{8,10},{9,13},{10,... | collective-permute-start | bytes 811016 | tf_op jit(solution)/shard_map/ppermute | solution.py:346
  62.5 5.1 %collective-permute-start.22 = (bf16[16,4224]{1,0:T(8,128)(2,1)S(1)}, bf16[16,4224]{1,0:T(8,128)(2,1)S(1)}, u32[]{:S(2)}, u32[]{:S(2)}) collective-permute-start(bf16[16,4224]{1,0:T(8,128)(2,1)S(1)} %get-tuple-element.60), channel_id=1, source_target_pairs={{0,8},{1,9},{2,10},{3,11},{4,12},{5,13},{6,14},{7,15},{8,0},{9,1},... | collective-permute-start | bytes 405512 | tf_op jit(solution)/shard_map/ppermute | solution.py:346
  64.4 6.7 %collective-permute-start.17 = (bf16[16,4096]{1,0:T(8,128)(2,1)S(1)}, bf16[16,4096]{1,0:T(8,128)(2,1)S(1)}, u32[]{:S(2)}, u32[]{:S(2)}) collective-permute-start(bf16[16,4096]{1,0:T(8,128)(2,1)S(1)} %get-tuple-element.65), channel_id=1, source_target_pairs={{0,4},{1,3},{2,6},{3,1},{4,0},{5,7},{6,2},{7,5},{8,12},{9,11},{10,... | collective-permute-start | bytes 393224 | tf_op jit(solution)/shard_map/ppermute | solution.py:346
  64.8 11.1 %collective-permute-start.16 = (bf16[16,4096]{1,0:T(8,128)(2,1)S(1)}, bf16[16,4096]{1,0:T(8,128)(2,1)S(1)}, u32[]{:S(2)}, u32[]{:S(2)}) collective-permute-start(bf16[16,4096]{1,0:T(8,128)(2,1)S(1)} %get-tuple-element.64), channel_id=1, source_target_pairs={{0,4},{1,3},{2,6},{3,1},{4,0},{5,7},{6,2},{7,5},{8,12},{9,11},{10,... | collective-permute-start | bytes 393224 | tf_op jit(solution)/shard_map/ppermute | solution.py:346
  67.6 8.2 %collective-permute-start.23 = (bf16[16,4224]{1,0:T(8,128)(2,1)S(1)}, bf16[16,4224]{1,0:T(8,128)(2,1)S(1)}, u32[]{:S(2)}, u32[]{:S(2)}) collective-permute-start(bf16[16,4224]{1,0:T(8,128)(2,1)S(1)} %get-tuple-element.62), channel_id=1, source_target_pairs={{0,16},{1,17},{2,18},{3,19},{4,20},{5,21},{6,22},{7,23},{8,24},{9,... | collective-permute-start | bytes 405512 | tf_op jit(solution)/shard_map/ppermute | solution.py:346
  71.1 5.0 %collective-permute-start.18 = (bf16[16,4096]{1,0:T(8,128)(2,1)S(1)}, bf16[16,4096]{1,0:T(8,128)(2,1)S(1)}, u32[]{:S(2)}, u32[]{:S(2)}) collective-permute-start(bf16[16,4096]{1,0:T(8,128)(2,1)S(1)} %add_convert_fusion.1), channel_id=1, source_target_pairs={{0,2},{1,5},{2,0},{3,7},{4,6},{5,1},{6,4},{7,3},{8,10},{9,13},{10,... | collective-permute-start | bytes 393224 | tf_op jit(solution)/shard_map/ppermute | solution.py:346
  75.8 1.2 %collective-permute-start.24 = (f32[128]{0:T(128)S(1)}, f32[128]{0:T(128)S(1)}, u32[]{:S(2)}, u32[]{:S(2)}) collective-permute-start(f32[128]{0:T(128)S(1)} %bitcast_add_fusion), channel_id=1, source_target_pairs={{0,1},{1,0},{2,3},{3,2},{4,5},{5,4},{6,7},{7,6},{8,9},{9,8},{10,11... | collective-permute-start | bytes 1544 | tf_op jit(solution)/shard_map/ppermute | solution.py:349

commit v7 on v6

--- a/solution.py
+++ b/solution.py
@@ -372,7 +372,7 @@
         pieces = [own, own_a, own_b, own_c, across, z2, z2_a, z2_b, z3, z3_a, z3_b]
         places = [(i * q,) for i in range(4)] + [tuple(i * q + rows for i in range(3))]
         places += [(half + i * q,) for i in range(3)] + [(half + i * q + rows,) for i in range(3)]
-        early = early_rows(pieces, places, gain, 2 * half, 10**9)
+        early = early_rows(pieces, places, gain, 2 * half, 2 * 10**8)
         early_places = [(0, half - rows), (half, half + 3 * q)]
         late_places = [(half - rows,), (half + 3 * q,), (half + 3 * q + rows,)]
         late = [across_c, z2_c, z3_c]

time: 77.7 us -> 77.7 us (level)
  no operation moved by 1% of the time
where the time goes in v7:
time: 77.7 us; the launch traced here: 77.5 us
  starting transfers between devices  30.7 us (40%)
  waiting for transfers between devices  27.6 us (36%)
  Pallas kernels  16.8 us (22%)
  other arithmetic  1.43 us (2%)
  between operations  0.92 us (1%)
    ppermute x22, starting transfers between devices, swap(): return lax.ppermute(v, BOTH, pairs)  30.1 us
    ppermute x22, waiting for transfers between devices, swap(): return lax.ppermute(v, BOTH, pairs)  24.7 us
    pallas_call x12, Pallas kernels, call(): pl.pallas_call(body, out_shape=out_shape, in_specs=[VMEM] * len(args), ou...  15.9 us
    ppermute x3, waiting for transfers between devices, tp_swap(): return lax.ppermute(v, 'tp', [(0, 1), (1, 0)])  2.87 us
  transfers between devices with their start and end apart: 25, of which 15 were waited for; matrix products, arithmetic and copies ran while one was open for 1% of the time, Pallas kernels for 3%

profile of v7, /device:TPU:0, one launch (start us, length us, event | category | flops | bytes accessed | tf_op | source)
XLA Modules:
  0.0 77.5 jit_solution(197606712306246070)
XLA Ops:
  0.6 0.9 %shard_map.86.refs_0_.own_ref = bf16[16,4224]{1,0:T(8,128)(2,1)S(1)} custom-call(bf16[16,4096]{1,0:T(8,128)(2,1)} %rows_ref.1, s32[16]{0:T(128)} %owner_ref.1), custom_call_target="tpu_custom_call" | custom-call | flops 10000000000 | bytes 262144 | tf_op jit(solution)/shard_map/pallas_call | solution.py:151
  1.6 4.1 %collective-permute-start = (bf16[16,4224]{1,0:T(8,128)(2,1)S(1)}, bf16[16,4224]{1,0:T(8,128)(2,1)S(1)}, u32[]{:S(2)}, u32[]{:S(2)}) collective-permute-start(bf16[16,4224]{1,0:T(8,128)(2,1)S(1)} %shard_map.86.refs_0_.own_ref), channel_id=1, source_target_pairs={{0,16},{1,17},{2,18},{3,19},{4,20},{5,21},{6,22},{7,23},{8,24},{9,... | collective-permute-start | bytes 405512 | tf_op jit(solution)/shard_map/ppermute | solution.py:346
  5.7 1.5 %collective-permute-start.2 = (bf16[16,4224]{1,0:T(8,128)(2,1)S(1)}, bf16[16,4224]{1,0:T(8,128)(2,1)S(1)}, u32[]{:S(2)}, u32[]{:S(2)}) collective-permute-start(bf16[16,4224]{1,0:T(8,128)(2,1)S(1)} %shard_map.86.refs_0_.own_ref), channel_id=1, source_target_pairs={{0,4},{1,3},{2,6},{3,1},{4,0},{5,7},{6,2},{7,5},{8,12},{9,11},{10,... | collective-permute-start | bytes 405512 | tf_op jit(solution)/shard_map/ppermute | solution.py:346
  7.2 1.5 %collective-permute-start.1 = (bf16[16,4224]{1,0:T(8,128)(2,1)S(1)}, bf16[16,4224]{1,0:T(8,128)(2,1)S(1)}, u32[]{:S(2)}, u32[]{:S(2)}) collective-permute-start(bf16[16,4224]{1,0:T(8,128)(2,1)S(1)} %shard_map.86.refs_0_.own_ref), channel_id=1, source_target_pairs={{0,2},{1,5},{2,0},{3,7},{4,6},{5,1},{6,4},{7,3},{8,10},{9,13},{10,... | collective-permute-start | bytes 405512 | tf_op jit(solution)/shard_map/ppermute | solution.py:346
  8.7 3.5 %collective-permute-done.refs_0_ = bf16[16,4224]{1,0:T(8,128)(2,1)S(1)} collective-permute-done((bf16[16,4224]{1,0:T(8,128)(2,1)S(1)}, bf16[16,4224]{1,0:T(8,128)(2,1)S(1)}, u32[]{:S(2)}, u32[]{:S(2)}) %collective-permute-start) | collective-permute-done | bytes 135200 | tf_op jit(solution)/shard_map/ppermute | solution.py:346
  12.2 0.7 collective-permute-start.7
  12.9 0.0 collective-permute-done.2.refs_2_
  12.9 0.0 collective-permute-done.1.refs_1_
  12.9 1.6 %collective-permute-start.6 = (bf16[16,4224]{1,0:T(8,128)(2,1)S(1)}, bf16[16,4224]{1,0:T(8,128)(2,1)S(1)}, u32[]{:S(2)}, u32[]{:S(2)}) collective-permute-start(bf16[16,4224]{1,0:T(8,128)(2,1)S(1)} %shard_map.87.refs_5_), channel_id=1, source_target_pairs={{0,4},{1,3},{2,6},{3,1},{4,0},{5,7},{6,2},{7,5},{8,12},{9,11},{10,... | collective-permute-start | bytes 405512 | tf_op jit(solution)/shard_map/ppermute | solution.py:346
  14.5 1.5 %collective-permute-start.3 = (bf16[16,4224]{1,0:T(8,128)(2,1)S(1)}, bf16[16,4224]{1,0:T(8,128)(2,1)S(1)}, u32[]{:S(2)}, u32[]{:S(2)}) collective-permute-start(bf16[16,4224]{1,0:T(8,128)(2,1)S(1)} %shard_map.87.refs_5_), channel_id=1, source_target_pairs={{0,2},{1,5},{2,0},{3,7},{4,6},{5,1},{6,4},{7,3},{8,10},{9,13},{10,... | collective-permute-start | bytes 405512 | tf_op jit(solution)/shard_map/ppermute | solution.py:346
  16.0 0.5 collective-permute-start.4
  16.5 1.4 %collective-permute-start.5 = (bf16[48,4224]{1,0:T(8,128)(2,1)S(1)}, bf16[48,4224]{1,0:T(8,128)(2,1)S(1)}, u32[]{:S(2)}, u32[]{:S(2)}) collective-permute-start(bf16[48,4224]{1,0:T(8,128)(2,1)S(1)} %shard_map.89), channel_id=1, source_target_pairs={{0,8},{1,9},{2,10},{3,11},{4,12},{5,13},{6,14},{7,15},{8,0},{9,1},... | collective-permute-start | bytes 1216520 | tf_op jit(solution)/shard_map/ppermute | solution.py:346
  17.9 0.0 collective-permute-done.7.refs_0_
  18.0 0.0 slice-start.5
  18.0 0.0 copy-start
  18.0 0.0 slice-start.2
  18.0 0.0 slice-start.6
  18.0 0.0 slice-start.7
  18.0 1.6 %collective-permute-start.9 = (bf16[16,4224]{1,0:T(8,128)(2,1)S(1)}, bf16[16,4224]{1,0:T(8,128)(2,1)S(1)}, u32[]{:S(2)}, u32[]{:S(2)}) collective-permute-start(bf16[16,4224]{1,0:T(8,128)(2,1)S(1)} %shard_map.90.refs_8_), channel_id=1, source_target_pairs={{0,4},{1,3},{2,6},{3,1},{4,0},{5,7},{6,2},{7,5},{8,12},{9,11},{10,... | collective-permute-start | bytes 405512 | tf_op jit(solution)/shard_map/ppermute | solution.py:346
  19.6 1.3 %collective-permute-done.3.refs_0_ = bf16[16,4224]{1,0:T(8,128)(2,1)S(1)} collective-permute-done((bf16[16,4224]{1,0:T(8,128)(2,1)S(1)}, bf16[16,4224]{1,0:T(8,128)(2,1)S(1)}, u32[]{:S(2)}, u32[]{:S(2)}) %collective-permute-start.3) | collective-permute-done | bytes 135200 | tf_op jit(solution)/shard_map/ppermute | solution.py:346
  20.9 1.5 %collective-permute-start.8 = (bf16[16,4224]{1,0:T(8,128)(2,1)S(1)}, bf16[16,4224]{1,0:T(8,128)(2,1)S(1)}, u32[]{:S(2)}, u32[]{:S(2)}) collective-permute-start(bf16[16,4224]{1,0:T(8,128)(2,1)S(1)} %shard_map.90.refs_8_), channel_id=1, source_target_pairs={{0,2},{1,5},{2,0},{3,7},{4,6},{5,1},{6,4},{7,3},{8,10},{9,13},{10,... | collective-permute-start | bytes 405512 | tf_op jit(solution)/shard_map/ppermute | solution.py:346
  22.5 0.0 collective-permute-done.4.refs_3_
  22.5 0.7 collective-permute-start.10
  23.2 3.2 %collective-permute-done.8.refs_9_ = bf16[16,4224]{1,0:T(8,128)(2,1)S(1)} collective-permute-done((bf16[16,4224]{1,0:T(8,128)(2,1)S(1)}, bf16[16,4224]{1,0:T(8,128)(2,1)S(1)}, u32[]{:S(2)}, u32[]{:S(2)}) %collective-permute-start.8) | collective-permute-done | bytes 135200 | tf_op jit(solution)/shard_map/ppermute | solution.py:346
  26.4 0.5 collective-permute-start.12
  26.9 1.3 %collective-permute-done.5.refs_4_ = bf16[48,4224]{1,0:T(8,128)(2,1)S(1)} collective-permute-done((bf16[48,4224]{1,0:T(8,128)(2,1)S(1)}, bf16[48,4224]{1,0:T(8,128)(2,1)S(1)}, u32[]{:S(2)}, u32[]{:S(2)}) %collective-permute-start.5) | collective-permute-done | bytes 405536 | tf_op jit(solution)/shard_map/ppermute | solution.py:346
  28.2 0.7 shard_map.91
  28.9 0.8 %collective-permute-done.10.refs_0_ = bf16[16,4224]{1,0:T(8,128)(2,1)S(1)} collective-permute-done((bf16[16,4224]{1,0:T(8,128)(2,1)S(1)}, bf16[16,4224]{1,0:T(8,128)(2,1)S(1)}, u32[]{:S(2)}, u32[]{:S(2)}) %collective-permute-start.10) | collective-permute-done | bytes 135200 | tf_op jit(solution)/shard_map/ppermute | solution.py:346
  29.7 1.7 %collective-permute-done.12.refs_2_ = bf16[16,4224]{1,0:T(8,128)(2,1)S(1)} collective-permute-done((bf16[16,4224]{1,0:T(8,128)(2,1)S(1)}, bf16[16,4224]{1,0:T(8,128)(2,1)S(1)}, u32[]{:S(2)}, u32[]{:S(2)}) %collective-permute-start.12) | collective-permute-done | bytes 135200 | tf_op jit(solution)/shard_map/ppermute | solution.py:346
  31.5 0.0 slice-start.11
  31.5 0.0 copy-start.1
  31.5 9.3 %shard_map.92 = (bf16[2,256,1408]{2,1,0:T(8,128)(2,1)S(1)}, bf16[2,256,512]{2,1,0:T(8,128)(2,1)S(1)}, f32[256,128]{1,0:T(8,128)S(1)}) custom-call(bf16[256,4096]{1,0:T(8,128)(2,1)S(1)} %get-tuple-element.38.x_in, f32[256,128]{1,0:T(8,128)S(1)} %get-tuple-element.39.squares_in, f32[256,128]{1,0:T(8,128)S(1)} %get-tuple-element.40.owner_in, ...), custom_call_target="tpu_custom_call" | custom-call | flops 7516192768 | bytes 32141312 | tf_op jit(solution)/shard_map/pallas_call | solution.py:129
  40.9 0.1 collective-permute-start.13
  40.9 0.5 collective-permute-start.14
  41.4 2.7 %collective-permute-done.13.other_ref = bf16[2,256,1408]{2,1,0:T(8,128)(2,1)S(1)} collective-permute-done((bf16[2,256,1408]{2,1,0:T(8,128)(2,1)S(1)}, bf16[2,256,1408]{2,1,0:T(8,128)(2,1)S(1)}, u32[]{:S(2)}, u32[]{:S(2)}) %collective-permute-start.13) | collective-permute-done | bytes 1441824 | tf_op jit(solution)/shard_map/ppermute | solution.py:349
  44.2 0.7 shard_map.93
  44.8 0.1 collective-permute-done.14.b
  44.9 4.4 %shard_map.94 = (bf16[16,4096]{1,0:T(8,128)(2,1)S(1)}, bf16[16,4096]{1,0:T(8,128)(2,1)S(1)}, bf16[16,4096]{1,0:T(8,128)(2,1)S(1)}, bf16[16,4096]{1,0:T(8,128)(2,...) custom-call(bf16[256,1280]{1,0:T(8,128)(2,1)S(1)} %get-tuple-element, ...), custom_call_target="tpu_custom_call" | custom-call | flops 3758096384 | bytes 16797696 | tf_op jit(solution)/shard_map/pallas_call | solution.py:129
  49.3 0.6 collective-permute-start.20
  49.9 1.3 %collective-permute-start.15 = (bf16[64,4096]{1,0:T(8,128)(2,1)S(1)}, bf16[64,4096]{1,0:T(8,128)(2,1)S(1)}, u32[]{:S(2)}, u32[]{:S(2)}) collective-permute-start(bf16[64,4096]{1,0:T(8,128)(2,1)S(1)} %get-tuple-element.47), channel_id=1, source_target_pairs={{0,8},{1,9},{2,10},{3,11},{4,12},{5,13},{6,14},{7,15},{8,0},{9,1},... | collective-permute-start | bytes 1572872 | tf_op jit(solution)/shard_map/ppermute | solution.py:346
  51.2 1.9 %collective-permute-start.19 = (bf16[32,4096]{1,0:T(8,128)(2,1)S(1)}, bf16[32,4096]{1,0:T(8,128)(2,1)S(1)}, u32[]{:S(2)}, u32[]{:S(2)}) collective-permute-start(bf16[32,4096]{1,0:T(8,128)(2,1)S(1)} %get-tuple-element.52), channel_id=1, source_target_pairs={{0,4},{1,3},{2,6},{3,1},{4,0},{5,7},{6,2},{7,5},{8,12},{9,11},{10,... | collective-permute-start | bytes 786440 | tf_op jit(solution)/shard_map/ppermute | solution.py:346
  53.1 2.7 %collective-permute-done.20.refs_1_.refs_3_ = bf16[32,4224]{1,0:T(8,128)(2,1)S(1)} collective-permute-done((bf16[32,4224]{1,0:T(8,128)(2,1)S(1)}, bf16[32,4224]{1,0:T(8,128)(2,1)S(1)}, u32[]{:S(2)}, u32[]{:S(2)}) %collective-permute-start.20) | collective-permute-done | bytes 270368 | tf_op jit(solution)/shard_map/ppermute | solution.py:346
  55.8 0.1 shard_map.95
  55.9 1.1 %collective-permute-start.21 = (bf16[32,4224]{1,0:T(8,128)(2,1)S(1)}, bf16[32,4224]{1,0:T(8,128)(2,1)S(1)}, u32[]{:S(2)}, u32[]{:S(2)}) collective-permute-start(bf16[32,4224]{1,0:T(8,128)(2,1)S(1)} %get-tuple-element.58), channel_id=1, source_target_pairs={{0,2},{1,5},{2,0},{3,7},{4,6},{5,1},{6,4},{7,3},{8,10},{9,13},{10,... | collective-permute-start | bytes 811016 | tf_op jit(solution)/shard_map/ppermute | solution.py:346
  57.0 2.3 %collective-permute-done.19.refs_1_ = bf16[32,4096]{1,0:T(8,128)(2,1)S(1)} collective-permute-done((bf16[32,4096]{1,0:T(8,128)(2,1)S(1)}, bf16[32,4096]{1,0:T(8,128)(2,1)S(1)}, u32[]{:S(2)}, u32[]{:S(2)}) %collective-permute-start.19) | collective-permute-done | bytes 262176 | tf_op jit(solution)/shard_map/ppermute | solution.py:346
  59.4 0.6 shard_map.96
  60.0 2.4 %collective-permute-done.21.refs_1_.refs_3_ = bf16[32,4224]{1,0:T(8,128)(2,1)S(1)} collective-permute-done((bf16[32,4224]{1,0:T(8,128)(2,1)S(1)}, bf16[32,4224]{1,0:T(8,128)(2,1)S(1)}, u32[]{:S(2)}, u32[]{:S(2)}) %collective-permute-start.21) | collective-permute-done | bytes 270368 | tf_op jit(solution)/shard_map/ppermute | solution.py:346
  62.4 0.1 shard_map.97
  62.5 1.8 %collective-permute-start.22 = (bf16[16,4224]{1,0:T(8,128)(2,1)S(1)}, bf16[16,4224]{1,0:T(8,128)(2,1)S(1)}, u32[]{:S(2)}, u32[]{:S(2)}) collective-permute-start(bf16[16,4224]{1,0:T(8,128)(2,1)S(1)} %get-tuple-element.60), channel_id=1, source_target_pairs={{0,8},{1,9},{2,10},{3,11},{4,12},{5,13},{6,14},{7,15},{8,0},{9,1},... | collective-permute-start | bytes 405512 | tf_op jit(solution)/shard_map/ppermute | solution.py:346
  64.3 0.0 collective-permute-done.15
  64.3 0.1 add_convert_fusion.4
  64.4 0.4 collective-permute-start.17
  64.8 1.7 %collective-permute-start.16 = (bf16[16,4096]{1,0:T(8,128)(2,1)S(1)}, bf16[16,4096]{1,0:T(8,128)(2,1)S(1)}, u32[]{:S(2)}, u32[]{:S(2)}) collective-permute-start(bf16[16,4096]{1,0:T(8,128)(2,1)S(1)} %get-tuple-element.64), channel_id=1, source_target_pairs={{0,4},{1,3},{2,6},{3,1},{4,0},{5,7},{6,2},{7,5},{8,12},{9,11},{10,... | collective-permute-start | bytes 393224 | tf_op jit(solution)/shard_map/ppermute | solution.py:346
  66.5 1.1 %collective-permute-done.22.refs_1_.refs_3_ = bf16[16,4224]{1,0:T(8,128)(2,1)S(1)} collective-permute-done((bf16[16,4224]{1,0:T(8,128)(2,1)S(1)}, bf16[16,4224]{1,0:T(8,128)(2,1)S(1)}, u32[]{:S(2)}, u32[]{:S(2)}) %collective-permute-start.22) | collective-permute-done | bytes 135200 | tf_op jit(solution)/shard_map/ppermute | solution.py:346
  67.6 3.4 %collective-permute-start.23 = (bf16[16,4224]{1,0:T(8,128)(2,1)S(1)}, bf16[16,4224]{1,0:T(8,128)(2,1)S(1)}, u32[]{:S(2)}, u32[]{:S(2)}) collective-permute-start(bf16[16,4224]{1,0:T(8,128)(2,1)S(1)} %get-tuple-element.62), channel_id=1, source_target_pairs={{0,16},{1,17},{2,18},{3,19},{4,20},{5,21},{6,22},{7,23},{8,24},{9,... | collective-permute-start | bytes 405512 | tf_op jit(solution)/shard_map/ppermute | solution.py:346
  71.1 0.0 collective-permute-done.17
  71.1 0.1 add_convert_fusion.1
  71.1 0.7 collective-permute-start.18
  71.8 4.0 %collective-permute-done.23 = bf16[16,4224]{1,0:T(8,128)(2,1)S(1)} collective-permute-done((bf16[16,4224]{1,0:T(8,128)(2,1)S(1)}, bf16[16,4224]{1,0:T(8,128)(2,1)S(1)}, u32[]{:S(2)}, u32[]{:S(2)}) %collective-permute-start.23) | collective-permute-done | bytes 135200 | tf_op jit(solution)/shard_map/ppermute | solution.py:346
  75.8 0.1 collective-permute-start.24
  75.9 0.3 collective-permute-done.18
  76.2 0.8 add_convert_fusion
  76.9 0.1 collective-permute-done.24
  77.0 0.5 bitcast_divide_fusion
  (37 shorter events, 0.2 us)
Async XLA Ops:
  1.6 10.6 %collective-permute-start = (bf16[16,4224]{1,0:T(8,128)(2,1)S(1)}, bf16[16,4224]{1,0:T(8,128)(2,1)S(1)}, u32[]{:S(2)}, u32[]{:S(2)}) collective-permute-start(bf16[16,4224]{1,0:T(8,128)(2,1)S(1)} %shard_map.86.refs_0_.own_ref), channel_id=1, source_target_pairs={{0,16},{1,17},{2,18},{3,19},{4,20},{5,21},{6,22},{7,23},{8,24},{9,... | collective-permute-start | bytes 405512 | tf_op jit(solution)/shard_map/ppermute | solution.py:346
  5.7 7.2 %collective-permute-start.2 = (bf16[16,4224]{1,0:T(8,128)(2,1)S(1)}, bf16[16,4224]{1,0:T(8,128)(2,1)S(1)}, u32[]{:S(2)}, u32[]{:S(2)}) collective-permute-start(bf16[16,4224]{1,0:T(8,128)(2,1)S(1)} %shard_map.86.refs_0_.own_ref), channel_id=1, source_target_pairs={{0,4},{1,3},{2,6},{3,1},{4,0},{5,7},{6,2},{7,5},{8,12},{9,11},{10,... | collective-permute-start | bytes 405512 | tf_op jit(solution)/shard_map/ppermute | solution.py:346
  7.2 5.7 %collective-permute-start.1 = (bf16[16,4224]{1,0:T(8,128)(2,1)S(1)}, bf16[16,4224]{1,0:T(8,128)(2,1)S(1)}, u32[]{:S(2)}, u32[]{:S(2)}) collective-permute-start(bf16[16,4224]{1,0:T(8,128)(2,1)S(1)} %shard_map.86.refs_0_.own_ref), channel_id=1, source_target_pairs={{0,2},{1,5},{2,0},{3,7},{4,6},{5,1},{6,4},{7,3},{8,10},{9,13},{10,... | collective-permute-start | bytes 405512 | tf_op jit(solution)/shard_map/ppermute | solution.py:346
  12.2 5.8 %collective-permute-start.7 = (bf16[16,4224]{1,0:T(8,128)(2,1)S(1)}, bf16[16,4224]{1,0:T(8,128)(2,1)S(1)}, u32[]{:S(2)}, u32[]{:S(2)}) collective-permute-start(bf16[16,4224]{1,0:T(8,128)(2,1)S(1)} %collective-permute-done.refs_0_), channel_id=1, source_target_pairs={{0,8},{1,9},{2,10},{3,11},{4,12},{5,13},{6,14},{7,15},{8,0},{9,1},... | collective-permute-start | bytes 405512 | tf_op jit(solution)/shard_map/ppermute | solution.py:346
  12.9 10.3 %collective-permute-start.6 = (bf16[16,4224]{1,0:T(8,128)(2,1)S(1)}, bf16[16,4224]{1,0:T(8,128)(2,1)S(1)}, u32[]{:S(2)}, u32[]{:S(2)}) collective-permute-start(bf16[16,4224]{1,0:T(8,128)(2,1)S(1)} %shard_map.87.refs_5_), channel_id=1, source_target_pairs={{0,4},{1,3},{2,6},{3,1},{4,0},{5,7},{6,2},{7,5},{8,12},{9,11},{10,... | collective-permute-start | bytes 405512 | tf_op jit(solution)/shard_map/ppermute | solution.py:346
  14.5 6.5 %collective-permute-start.3 = (bf16[16,4224]{1,0:T(8,128)(2,1)S(1)}, bf16[16,4224]{1,0:T(8,128)(2,1)S(1)}, u32[]{:S(2)}, u32[]{:S(2)}) collective-permute-start(bf16[16,4224]{1,0:T(8,128)(2,1)S(1)} %shard_map.87.refs_5_), channel_id=1, source_target_pairs={{0,2},{1,5},{2,0},{3,7},{4,6},{5,1},{6,4},{7,3},{8,10},{9,13},{10,... | collective-permute-start | bytes 405512 | tf_op jit(solution)/shard_map/ppermute | solution.py:346
  16.0 6.5 %collective-permute-start.4 = (bf16[16,4224]{1,0:T(8,128)(2,1)S(1)}, bf16[16,4224]{1,0:T(8,128)(2,1)S(1)}, u32[]{:S(2)}, u32[]{:S(2)}) collective-permute-start(bf16[16,4224]{1,0:T(8,128)(2,1)S(1)} %collective-permute-done.1.refs_1_), channel_id=1, source_target_pairs={{0,4},{1,3},{2,6},{3,1},{4,0},{5,7},{6,2},{7,5},{8,12},{9,11},{10,... | collective-permute-start | bytes 405512 | tf_op jit(solution)/shard_map/ppermute | solution.py:346
  16.5 11.7 %collective-permute-start.5 = (bf16[48,4224]{1,0:T(8,128)(2,1)S(1)}, bf16[48,4224]{1,0:T(8,128)(2,1)S(1)}, u32[]{:S(2)}, u32[]{:S(2)}) collective-permute-start(bf16[48,4224]{1,0:T(8,128)(2,1)S(1)} %shard_map.89), channel_id=1, source_target_pairs={{0,8},{1,9},{2,10},{3,11},{4,12},{5,13},{6,14},{7,15},{8,0},{9,1},... | collective-permute-start | bytes 1216520 | tf_op jit(solution)/shard_map/ppermute | solution.py:346
  17.9 13.5 %slice-start = ((s8[14680064]{0:T(1024)(128)(4,1)}), s8[4194304]{0:T(1024)(128)(4,1)S(1)}, s32[]{:S(2)}) async-start(s8[14680064]{0:T(1024)(128)(4,1)} %bitcast.6), calls=%async_computation | async-start | bytes 8388608
  17.9 13.5 %slice-start.1 = ((s8[14680064]{0:T(1024)(128)(4,1)}), s8[4194304]{0:T(1024)(128)(4,1)S(1)}, s32[]{:S(2)}) async-start(s8[14680064]{0:T(1024)(128)(4,1)} %bitcast.6), calls=%async_computation.1 | async-start | bytes 8388608
  17.9 13.5 %slice-start.4 = ((s8[14680064]{0:T(1024)(128)(4,1)}), s8[4194304]{0:T(1024)(128)(4,1)S(1)}, s32[]{:S(2)}) async-start(s8[14680064]{0:T(1024)(128)(4,1)} %bitcast.8), calls=%async_computation.4 | async-start | bytes 8388608
  18.0 13.5 %slice-start.5 = ((s8[14680064]{0:T(1024)(128)(4,1)}), s8[4194304]{0:T(1024)(128)(4,1)S(1)}, s32[]{:S(2)}) async-start(s8[14680064]{0:T(1024)(128)(4,1)} %bitcast.8), calls=%async_computation.5 | async-start | bytes 8388608
  18.0 10.3 %copy-start = (f32[4096]{0:T(1024)S(1)}, f32[4096]{0:T(1024)}, u32[]{:S(2)}) copy-start(f32[4096]{0:T(1024)} %param.9) | copy-start | bytes 49156
  18.0 13.5 %slice-start.2 = ((s8[14680064]{0:T(1024)(128)(4,1)}), s8[4194304]{0:T(1024)(128)(4,1)S(1)}, s32[]{:S(2)}) async-start(s8[14680064]{0:T(1024)(128)(4,1)} %bitcast.6), calls=%async_computation.2 | async-start | bytes 8388608
  18.0 13.5 %slice-start.3 = ((s8[14680064]{0:T(1024)(128)(4,1)}), s8[2097152]{0:T(1024)(128)(4,1)S(1)}, s32[]{:S(2)}) async-start(s8[14680064]{0:T(1024)(128)(4,1)} %bitcast.6), calls=%async_computation.3 | async-start | bytes 4194304
  18.0 13.5 %slice-start.6 = ((s8[14680064]{0:T(1024)(128)(4,1)}), s8[4194304]{0:T(1024)(128)(4,1)S(1)}, s32[]{:S(2)}) async-start(s8[14680064]{0:T(1024)(128)(4,1)} %bitcast.8), calls=%async_computation.6 | async-start | bytes 8388608
  18.0 13.4 %slice-start.7 = ((s8[14680064]{0:T(1024)(128)(4,1)}), s8[2097152]{0:T(1024)(128)(4,1)S(1)}, s32[]{:S(2)}) async-start(s8[14680064]{0:T(1024)(128)(4,1)} %bitcast.8), calls=%async_computation.7 | async-start | bytes 4194304
  18.0 8.9 %collective-permute-start.9 = (bf16[16,4224]{1,0:T(8,128)(2,1)S(1)}, bf16[16,4224]{1,0:T(8,128)(2,1)S(1)}, u32[]{:S(2)}, u32[]{:S(2)}) collective-permute-start(bf16[16,4224]{1,0:T(8,128)(2,1)S(1)} %shard_map.90.refs_8_), channel_id=1, source_target_pairs={{0,4},{1,3},{2,6},{3,1},{4,0},{5,7},{6,2},{7,5},{8,12},{9,11},{10,... | collective-permute-start | bytes 405512 | tf_op jit(solution)/shard_map/ppermute | solution.py:346
  20.9 5.5 %collective-permute-start.8 = (bf16[16,4224]{1,0:T(8,128)(2,1)S(1)}, bf16[16,4224]{1,0:T(8,128)(2,1)S(1)}, u32[]{:S(2)}, u32[]{:S(2)}) collective-permute-start(bf16[16,4224]{1,0:T(8,128)(2,1)S(1)} %shard_map.90.refs_8_), channel_id=1, source_target_pairs={{0,2},{1,5},{2,0},{3,7},{4,6},{5,1},{6,4},{7,3},{8,10},{9,13},{10,... | collective-permute-start | bytes 405512 | tf_op jit(solution)/shard_map/ppermute | solution.py:346
  22.5 22.4 %slice-start.8 = ((s8[14680064]{0:T(1024)(128)(4,1)}), s8[4194304]{0:T(1024)(128)(4,1)S(1)}, s32[]{:S(2)}) async-start(s8[14680064]{0:T(1024)(128)(4,1)} %bitcast.10), calls=%async_computation.8 | async-start | bytes 8388608
  22.5 22.4 %slice-start.9 = ((s8[14680064]{0:T(1024)(128)(4,1)}), s8[4194304]{0:T(1024)(128)(4,1)S(1)}, s32[]{:S(2)}) async-start(s8[14680064]{0:T(1024)(128)(4,1)} %bitcast.10), calls=%async_computation.9 | async-start | bytes 8388608
  22.5 22.4 %slice-start.10 = ((s8[14680064]{0:T(1024)(128)(4,1)}), s8[4194304]{0:T(1024)(128)(4,1)S(1)}, s32[]{:S(2)}) async-start(s8[14680064]{0:T(1024)(128)(4,1)} %bitcast.10), calls=%async_computation.10 | async-start | bytes 8388608
  22.5 7.2 %collective-permute-start.10 = (bf16[16,4224]{1,0:T(8,128)(2,1)S(1)}, bf16[16,4224]{1,0:T(8,128)(2,1)S(1)}, u32[]{:S(2)}, u32[]{:S(2)}) collective-permute-start(bf16[16,4224]{1,0:T(8,128)(2,1)S(1)} %collective-permute-done.4.refs_3_), channel_id=1, source_target_pairs={{0,8},{1,9},{2,10},{3,11},{4,12},{5,13},{6,14},{7,15},{8,0},{9,1},... | collective-permute-start | bytes 405512 | tf_op jit(solution)/shard_map/ppermute | solution.py:346
  23.2 6.5 %collective-permute-start.11 = (bf16[16,4224]{1,0:T(8,128)(2,1)S(1)}, bf16[16,4224]{1,0:T(8,128)(2,1)S(1)}, u32[]{:S(2)}, u32[]{:S(2)}) collective-permute-start(bf16[16,4224]{1,0:T(8,128)(2,1)S(1)} %shard_map.88.refs_6_), channel_id=1, source_target_pairs={{0,4},{1,3},{2,6},{3,1},{4,0},{5,7},{6,2},{7,5},{8,12},{9,11},{10,... | collective-permute-start | bytes 405512 | tf_op jit(solution)/shard_map/ppermute | solution.py:346
  26.4 5.0 %collective-permute-start.12 = (bf16[16,4224]{1,0:T(8,128)(2,1)S(1)}, bf16[16,4224]{1,0:T(8,128)(2,1)S(1)}, u32[]{:S(2)}, u32[]{:S(2)}) collective-permute-start(bf16[16,4224]{1,0:T(8,128)(2,1)S(1)} %collective-permute-done.8.refs_9_), channel_id=1, source_target_pairs={{0,4},{1,3},{2,6},{3,1},{4,0},{5,7},{6,2},{7,5},{8,12},{9,11},{10,... | collective-permute-start | bytes 405512 | tf_op jit(solution)/shard_map/ppermute | solution.py:346
  31.5 13.4 %slice-start.11 = ((s8[14680064]{0:T(1024)(128)(4,1)}), s8[2097152]{0:T(1024)(128)(4,1)S(1)}, s32[]{:S(2)}) async-start(s8[14680064]{0:T(1024)(128)(4,1)} %bitcast.10), calls=%async_computation.11 | async-start | bytes 4194304
  31.5 13.4 %copy-start.1 = (f32[4096]{0:T(1024)S(1)}, f32[4096]{0:T(1024)}, u32[]{:S(2)}) copy-start(f32[4096]{0:T(1024)} %param.13) | copy-start | bytes 49156
  40.9 3.3 %collective-permute-start.13 = (bf16[2,256,1408]{2,1,0:T(8,128)(2,1)S(1)}, bf16[2,256,1408]{2,1,0:T(8,128)(2,1)S(1)}, u32[]{:S(2)}, u32[]{:S(2)}) collective-permute-start(bf16[2,256,1408]{2,1,0:T(8,128)(2,1)S(1)} %get-tuple-element.41.part_ref), channel_id=1, source_target_pairs={{0,1},{1,0},{2,3},{3,2},{4,5},{5,4},{6,7},{7,6},{8,9},{9,8},{10,11... | collective-permute-start | bytes 4325384 | tf_op jit(solution)/shard_map/ppermute | solution.py:349
  40.9 4.0 %collective-permute-start.14 = (bf16[2,256,512]{2,1,0:T(8,128)(2,1)S(1)}, bf16[2,256,512]{2,1,0:T(8,128)(2,1)S(1)}, u32[]{:S(2)}, u32[]{:S(2)}) collective-permute-start(bf16[2,256,512]{2,1,0:T(8,128)(2,1)S(1)} %get-tuple-element.43.a), channel_id=1, source_target_pairs={{0,1},{1,0},{2,3},{3,2},{4,5},{5,4},{6,7},{7,6},{8,9},{9,8},{10,11... | collective-permute-start | bytes 1572872 | tf_op jit(solution)/shard_map/ppermute | solution.py:349
  49.3 6.5 %collective-permute-start.20 = (bf16[32,4224]{1,0:T(8,128)(2,1)S(1)}, bf16[32,4224]{1,0:T(8,128)(2,1)S(1)}, u32[]{:S(2)}, u32[]{:S(2)}) collective-permute-start(bf16[32,4224]{1,0:T(8,128)(2,1)S(1)} %get-tuple-element.54), channel_id=1, source_target_pairs={{0,4},{1,3},{2,6},{3,1},{4,0},{5,7},{6,2},{7,5},{8,12},{9,11},{10,... | collective-permute-start | bytes 811016 | tf_op jit(solution)/shard_map/ppermute | solution.py:346
  49.9 14.4 %collective-permute-start.15 = (bf16[64,4096]{1,0:T(8,128)(2,1)S(1)}, bf16[64,4096]{1,0:T(8,128)(2,1)S(1)}, u32[]{:S(2)}, u32[]{:S(2)}) collective-permute-start(bf16[64,4096]{1,0:T(8,128)(2,1)S(1)} %get-tuple-element.47), channel_id=1, source_target_pairs={{0,8},{1,9},{2,10},{3,11},{4,12},{5,13},{6,14},{7,15},{8,0},{9,1},... | collective-permute-start | bytes 1572872 | tf_op jit(solution)/shard_map/ppermute | solution.py:346
  51.2 8.2 %collective-permute-start.19 = (bf16[32,4096]{1,0:T(8,128)(2,1)S(1)}, bf16[32,4096]{1,0:T(8,128)(2,1)S(1)}, u32[]{:S(2)}, u32[]{:S(2)}) collective-permute-start(bf16[32,4096]{1,0:T(8,128)(2,1)S(1)} %get-tuple-element.52), channel_id=1, source_target_pairs={{0,4},{1,3},{2,6},{3,1},{4,0},{5,7},{6,2},{7,5},{8,12},{9,11},{10,... | collective-permute-start | bytes 786440 | tf_op jit(solution)/shard_map/ppermute | solution.py:346
  55.9 6.5 %collective-permute-start.21 = (bf16[32,4224]{1,0:T(8,128)(2,1)S(1)}, bf16[32,4224]{1,0:T(8,128)(2,1)S(1)}, u32[]{:S(2)}, u32[]{:S(2)}) collective-permute-start(bf16[32,4224]{1,0:T(8,128)(2,1)S(1)} %get-tuple-element.58), channel_id=1, source_target_pairs={{0,2},{1,5},{2,0},{3,7},{4,6},{5,1},{6,4},{7,3},{8,10},{9,13},{10,... | collective-permute-start | bytes 811016 | tf_op jit(solution)/shard_map/ppermute | solution.py:346
  62.5 5.1 %collective-permute-start.22 = (bf16[16,4224]{1,0:T(8,128)(2,1)S(1)}, bf16[16,4224]{1,0:T(8,128)(2,1)S(1)}, u32[]{:S(2)}, u32[]{:S(2)}) collective-permute-start(bf16[16,4224]{1,0:T(8,128)(2,1)S(1)} %get-tuple-element.60), channel_id=1, source_target_pairs={{0,8},{1,9},{2,10},{3,11},{4,12},{5,13},{6,14},{7,15},{8,0},{9,1},... | collective-permute-start | bytes 405512 | tf_op jit(solution)/shard_map/ppermute | solution.py:346
  64.4 6.7 %collective-permute-start.17 = (bf16[16,4096]{1,0:T(8,128)(2,1)S(1)}, bf16[16,4096]{1,0:T(8,128)(2,1)S(1)}, u32[]{:S(2)}, u32[]{:S(2)}) collective-permute-start(bf16[16,4096]{1,0:T(8,128)(2,1)S(1)} %get-tuple-element.65), channel_id=1, source_target_pairs={{0,4},{1,3},{2,6},{3,1},{4,0},{5,7},{6,2},{7,5},{8,12},{9,11},{10,... | collective-permute-start | bytes 393224 | tf_op jit(solution)/shard_map/ppermute | solution.py:346
  64.8 11.1 %collective-permute-start.16 = (bf16[16,4096]{1,0:T(8,128)(2,1)S(1)}, bf16[16,4096]{1,0:T(8,128)(2,1)S(1)}, u32[]{:S(2)}, u32[]{:S(2)}) collective-permute-start(bf16[16,4096]{1,0:T(8,128)(2,1)S(1)} %get-tuple-element.64), channel_id=1, source_target_pairs={{0,4},{1,3},{2,6},{3,1},{4,0},{5,7},{6,2},{7,5},{8,12},{9,11},{10,... | collective-permute-start | bytes 393224 | tf_op jit(solution)/shard_map/ppermute | solution.py:346
  67.6 8.2 %collective-permute-start.23 = (bf16[16,4224]{1,0:T(8,128)(2,1)S(1)}, bf16[16,4224]{1,0:T(8,128)(2,1)S(1)}, u32[]{:S(2)}, u32[]{:S(2)}) collective-permute-start(bf16[16,4224]{1,0:T(8,128)(2,1)S(1)} %get-tuple-element.62), channel_id=1, source_target_pairs={{0,16},{1,17},{2,18},{3,19},{4,20},{5,21},{6,22},{7,23},{8,24},{9,... | collective-permute-start | bytes 405512 | tf_op jit(solution)/shard_map/ppermute | solution.py:346
  71.1 5.0 %collective-permute-start.18 = (bf16[16,4096]{1,0:T(8,128)(2,1)S(1)}, bf16[16,4096]{1,0:T(8,128)(2,1)S(1)}, u32[]{:S(2)}, u32[]{:S(2)}) collective-permute-start(bf16[16,4096]{1,0:T(8,128)(2,1)S(1)} %add_convert_fusion.1), channel_id=1, source_target_pairs={{0,2},{1,5},{2,0},{3,7},{4,6},{5,1},{6,4},{7,3},{8,10},{9,13},{10,... | collective-permute-start | bytes 393224 | tf_op jit(solution)/shard_map/ppermute | solution.py:346
  75.8 1.2 %collective-permute-start.24 = (f32[128]{0:T(128)S(1)}, f32[128]{0:T(128)S(1)}, u32[]{:S(2)}, u32[]{:S(2)}) collective-permute-start(f32[128]{0:T(128)S(1)} %bitcast_add_fusion), channel_id=1, source_target_pairs={{0,1},{1,0},{2,3},{3,2},{4,5},{5,4},{6,7},{7,6},{8,9},{9,8},{10,11... | collective-permute-start | bytes 1544 | tf_op jit(solution)/shard_map/ppermute | solution.py:349
